TPU v7x, 32 devices: a whole 2x2x4 slice. The times are simulated.
32 devices in a mesh: grp: 4 (over y, x), dev: 8 (over z, core).
Axes of the slice: x: 2, y: 2, z: 4, core: 2. Of those that a mesh axis runs over, the one named last changes fastest.
Arguments:
- sketch: bfloat16 [65536, 256], P(('grp', 'dev')), may hold values from -4 to 4
- marginal_std: float32 [65536], P(('grp', 'dev')), may hold values from 0.1 to 10
- cov_tiles: bfloat16 [9, 256, 256], replicated, may hold values from 0 to 1
- tile_cols: int32 [256, 9], P(('grp', 'dev')), may hold values from -1 to 255, as said below
Outputs:
- basis: float32 [65536, 256], P(('grp', 'dev'))
- factor: float32 [256, 256], replicated
Inputs may be any that keep to these rules, and one draw needn't show every extreme that they name: `tile_cols`: tile t holds one line of 256 cells. The lines lie in depth order, except that the order within each aligned block of 4 tiles is permuted. Entry e of the list of tile t is the tile that holds the line e - 4 lines from the line of t (entry 4 is t itself), or -1 where that line lies beyond the ends of the field.
All inputs are finite; a program needn't handle non-finite values.
Results may differ from a plain program's by a relative error of at most 0.0035.
Values may be sent and summed in bfloat16 or wider, within the bound.
No kernel may reach another device: no remote copies, remote signals or barrier semaphores. Data moves between devices by JAX's collectives and lax.ppermute only.
A program may use at most 64 MiB of HBM per device.

v0:
```python
import jax
import jax.numpy as jnp
from jax import lax
from jax.sharding import PartitionSpec as P


def with_halo(block, sides, width):
    for axis, dim in sides:
        count = lax.axis_size(axis)
        forward = [(i, i + 1) for i in range(count - 1)]
        backward = [(target, source) for source, target in forward]
        low = lax.ppermute(
            lax.slice_in_dim(block, block.shape[dim] - width, None, axis=dim), axis, forward
        )
        high = lax.ppermute(lax.slice_in_dim(block, 0, width, axis=dim), axis, backward)
        block = jnp.concatenate([low, block, high], axis=dim)
    return block


def per_device(sketch, marginal_std, cov_tiles, tile_cols):
    row_count, column_count = sketch.shape
    tile_size = cov_tiles.shape[1]
    row_tiles = row_count // tile_size
    scaled = (sketch.astype(jnp.float32) * marginal_std[:, None]).astype(jnp.bfloat16)
    extended = with_halo(scaled, ((("grp", "dev"), 0),), row_tiles * tile_size)
    extended_tiles = extended.reshape(-1, tile_size, column_count)
    first_tile = lax.axis_index(("grp", "dev")) * row_tiles
    present = tile_cols >= 0
    local_cols = jnp.where(present, tile_cols - first_tile + row_tiles, 0)
    gathered = extended_tiles[local_cols.T]
    gathered = jnp.where(present.T[:, :, None, None], gathered, jnp.zeros((), jnp.bfloat16))
    products = jnp.einsum("eij,etjk->tik", cov_tiles, gathered, preferred_element_type=jnp.float32)
    latent_field = products.reshape(row_count, column_count) * marginal_std[:, None]
    total_rows = row_count * lax.axis_size("grp") * lax.axis_size("dev")
    gram_matrix = (
        jnp.dot(latent_field.T, latent_field, precision=lax.Precision.HIGHEST) / total_rows
    )
    gram_matrix = lax.psum(gram_matrix, "dev")
    gram_matrix = lax.psum(gram_matrix, "grp")
    lower_factor = jnp.linalg.cholesky(gram_matrix)
    basis = lax.linalg.triangular_solve(
        lower_factor, latent_field, left_side=False, lower=True, transpose_a=True
    )
    return (basis, lower_factor.T)


def solution(mesh):
    in_specs = (P(("grp", "dev"), None), P(("grp", "dev")), P(), P(("grp", "dev"), None))
    out_specs = (P(("grp", "dev"), None), P())
    return jax.shard_map(
        per_device, mesh=mesh, in_specs=in_specs, out_specs=out_specs, check_vma=False
    )
```

profile of v0, /device:TPU:0, one launch (start us, length us, event | category | flops | bytes accessed | tf_op | source)
XLA Modules:
  0.0 249.5 jit_solution(101902579957288969)
XLA Ops:
  7.2 0.0 copy-start
  7.2 0.0 copy-start.7
  7.2 0.0 copy-start.8
  7.2 0.0 all-reduce.4.cloned.1.call-start
  7.2 1.6 multiply_convert_fusion
  8.9 2.4 collective-permute-start
  11.3 1.3 collective-permute-start.1
  12.6 0.0 copy-done.7
  12.7 0.0 copy-done.8
  12.7 0.1 copy.13
  12.8 0.1 reshape.62
  12.9 0.1 copy.12
  13.0 0.6 collective-permute-done
  13.5 4.6 %collective-permute-done.1 = bf16[2048,256]{1,0:T(8,128)(2,1)} collective-permute-done((bf16[2048,256]{1,0:T(8,128)(2,1)S(1)}, bf16[2048,256]{1,0:T(8,128)(2,1)}, u32[]{:S(2)}, u32[]{:S(2)}) %collective-permute-start.1) | collective-permute-done | bytes 1048608 | tf_op jit(solution)/shard_map/ppermute | solution.py:15
  18.1 2.8 %pad_maximum_fusion = bf16[6144,256]{1,0:T(8,128)(2,1)} fusion(bf16[2048,256]{1,0:T(8,128)(2,1)} %collective-permute-done.1, bf16[2048,256]{1,0:T(8,128)(2,1)S(1)} %multiply_convert_fusion, bf16[2048,256]{1,0:T(8,128)(2,1)S(1)} %collective-permute-done), kind=kLoop, calls=%fused_computation.7 | loop fusion | flops 9437184 | bytes 6291456 | tf_op jit(solution)/shard_map/concatenate | solution.py:16
  21.0 7.8 %gather_fusion = bf16[72,256,256]{2,1,0:T(8,128)(2,1)} fusion(bf16[24,256,256]{2,1,0:T(8,128)(2,1)} %bitcast.60, s32[1024]{0:T(1024)S(1)} %pad_clamp_fusion), kind=kCustom, calls=%fused_computation | custom fusion | bytes 18874656 | tf_op jit(solution)/shard_map/gather | solution.py:30
  28.8 0.0 copy-done
  28.8 5.3 %fusion = f32[8,256,256,1]{1,2,0,3:T(8,128)S(1)} fusion(bf16[9,8,256,256]{3,2,1,0:T(8,128)(2,1)} %bitcast.61, pred[9,8]{1,0:T(8,128)(4,1)S(1)} %copy.12, bf16[9,256,256]{2,1,0:T(8,128)(2,1)S(1)} %copy-done), kind=kOutput, calls=%fused_computation.3 | convolution fusion | flops 2420637696 | bytes 12714056 | tf_op jit(solution)/shard_map/eij,etjk->tik/dot_general | solution.py:32
  34.1 0.0 copy-start.1
  34.1 1.3 copy-done.1
  35.4 4.8 %fusion.7 = f32[256,256]{0,1:T(8,128)} fusion(f32[8,256,256,1]{1,2,0,3:T(8,128)S(1)} %fusion, f32[8,256]{1,0:T(8,128)S(1)} %mul.33), kind=kOutput, calls=%fused_computation.16 | convolution fusion | flops 1611202560 | bytes 2367488 | tf_op jit(solution)/shard_map/dot_general | solution.py:36
  40.2 0.0 all-reduce.4.cloned.1.call-update
  40.3 0.2 all-reduce.6.cloned.1.call-start
  40.5 75.7 %all-reduce.4.cloned.1.call-done = f32[256,256]{0,1:T(8,128)} async-done(((f32[256,256]{0,1:T(8,128)}), f32[256,256]{0,1:T(8,128)}) %all-reduce.4.cloned.1.call-update) | async-done | bytes 262160 | tf_op jit(solution)/shard_map/psum | solution.py:38
  116.2 0.0 all-reduce.6.cloned.1.call-update
  116.3 1.9 bitcast_multiply_fusion
  118.2 43.2 %all-reduce.6.cloned.1.call-done = f32[256,256]{0,1:T(8,128)} async-done(((f32[256,256]{0,1:T(8,128)}), f32[256,256]{0,1:T(8,128)}) %all-reduce.6.cloned.1.call-update) | async-done | bytes 262160 | tf_op jit(solution)/shard_map/psum | solution.py:39
  161.3 1.1 copy.17
  162.4 1.0 fusion.11
  163.4 0.0 copy-start.4
  163.4 0.7 copy-done.4
  164.1 11.7 %cholesky.50 = f32[128,128]{1,0:T(8,128)S(1)} custom-call(f32[128,128]{1,0:T(8,128)S(1)} %cholesky.118), custom_call_target="Cholesky" | custom-call | tf_op jit(solution)/shard_map/jit(cholesky)/cholesky | solution.py:40
  175.8 0.0 copy-start.5
  175.9 0.6 copy-done.5
  176.5 10.4 %custom-call.14 = f32[1,128,128]{1,2,0:T(8,128)} custom-call(f32[1,128,128]{2,1,0:T(8,128)S(1)} %get-tuple-element.29), custom_call_target="InvertDiagBlocksLowerTriangular" | custom-call | tf_op jit(solution)/shard_map/jit(cholesky)/cholesky | solution.py:40
  186.9 0.9 cholesky.113
  187.8 1.1 constant_dynamic-update-slice_fusion.1
  188.9 1.7 convolution_subtract_fusion.1
  190.6 13.2 %cholesky.105 = f32[128,128]{1,0:T(8,128)} custom-call(f32[128,128]{1,0:T(8,128)} %convolution_subtract_fusion.1), custom_call_target="Cholesky" | custom-call | tf_op jit(solution)/shard_map/jit(cholesky)/cholesky | solution.py:40
  203.8 0.9 select_reduce_fusion
  204.7 0.0 copy-start.2
  204.7 0.7 compare_reduce_fusion
  206.7 0.0 copy-done.2
  206.7 1.7 fusion.13
  208.4 0.1 triangular_solve.58
  208.5 5.3 %while.1 = (s32[]{:T(128)}, f32[256,256]{1,0:T(8,128)S(1)}, s32[2,2]{1,0:T(2,128)S(1)}, f32[2,128,128]{2,1,0:T(8,128)}, s32[]{:T(128)}) while((s32[]{:T(128)}, f32[256,256]{1,0:T(8,128)S(1)}, s32[2,2]{1,0:T(2,128)S(1)}, f32[2,128,128]{2,1,0:T(8,128)}, s32[]{:T(128)}) %tuple.30), condition=%wide.while_cond, body=%wide.while_body.sunk | while | flops 2 | bytes 132705 | solution.py:41
  208.5 0.6 fusion.27
  209.1 2.1 bitcast_dynamic-update-slice_fusion.2
  211.2 0.6 fusion.27
  211.8 2.1 bitcast_dynamic-update-slice_fusion.2
  213.8 21.1 %custom-call.15 = f32[2,128,128]{1,2,0:T(8,128)} custom-call(f32[2,128,128]{2,1,0:T(8,128)} %get-tuple-element.9), custom_call_target="InvertDiagBlocksLowerTriangular" | custom-call | tf_op jit(solution)/shard_map/triangular_solve | solution.py:41
  234.9 1.9 fusion.8
  236.9 0.0 copy-start.6
  236.9 1.8 convolution_subtract_fusion
  238.7 0.0 copy-done.6
  238.7 1.1 fusion.14
  239.8 0.1 pad_maximum_fusion.1
  239.9 0.0 copy-start.3
  240.0 1.8 copy.18
  241.8 0.0 copy-done.3
  241.8 0.8 copy.19
  (10 shorter events, 0.1 us)
Async XLA Ops:
  7.2 21.6 %copy-start = (bf16[9,256,256]{2,1,0:T(8,128)(2,1)S(1)}, bf16[9,256,256]{2,1,0:T(8,128)(2,1)}, u32[]{:S(2)}) copy-start(bf16[9,256,256]{2,1,0:T(8,128)(2,1)} %param.6) | copy-start | bytes 3538948
  7.2 5.5 %copy-start.7 = (f32[2048]{0:T(1024)S(1)}, f32[2048]{0:T(1024)}, u32[]{:S(2)}) copy-start(f32[2048]{0:T(1024)} %param.5) | copy-start | bytes 24580
  7.2 5.5 %copy-start.8 = (s32[8,9]{1,0:T(8,128)S(1)}, s32[8,9]{1,0:T(8,128)}, u32[]{:S(2)}) copy-start(s32[8,9]{1,0:T(8,128)} %param.7) | copy-start | bytes 868
  7.2 109.0 %all-reduce.4.cloned.1.call-start = ((), (), s32[]{:S(2)}) async-start(), calls=%async_computation | async-start | bytes 524288 | tf_op jit(solution)/shard_map/psum | solution.py:38
  8.9 4.6 %collective-permute-start = (bf16[2048,256]{1,0:T(8,128)(2,1)S(1)}, bf16[2048,256]{1,0:T(8,128)(2,1)S(1)}, u32[]{:S(2)}, u32[]{:S(2)}) collective-permute-start(bf16[2048,256]{1,0:T(8,128)(2,1)S(1)} %multiply_convert_fusion), channel_id=1, source_target_pairs={{0,1},{1,2},{2,3},{3,4},{4,5},{5,6},{6,7},{7,8},{8,9},{9,10},{10,1... | collective-permute-start | bytes 3145736 | tf_op jit(solution)/shard_map/ppermute | solution.py:12
  11.3 6.8 %collective-permute-start.1 = (bf16[2048,256]{1,0:T(8,128)(2,1)S(1)}, bf16[2048,256]{1,0:T(8,128)(2,1)}, u32[]{:S(2)}, u32[]{:S(2)}) collective-permute-start(bf16[2048,256]{1,0:T(8,128)(2,1)S(1)} %multiply_convert_fusion), channel_id=1, source_target_pairs={{1,0},{2,1},{3,2},{4,3},{5,4},{6,5},{7,6},{8,7},{9,8},{10,9},{11,1... | collective-permute-start | bytes 3145736 | tf_op jit(solution)/shard_map/ppermute | solution.py:15
  34.1 1.3 copy-start.1
  40.3 121.1 %all-reduce.6.cloned.1.call-start = ((), (), s32[]{:S(2)}) async-start(), calls=%async_computation.1 | async-start | bytes 524288 | tf_op jit(solution)/shard_map/psum | solution.py:39
  163.4 0.7 copy-start.4
  175.8 0.6 copy-start.5
  204.7 2.1 copy-start.2
  236.9 1.8 copy-start.6
  239.9 1.8 copy-start.3
Sparse Core Ops, SparseCore 0:
  40.4 75.8 all-reduce.3
  119.4 41.8 all-reduce.5
where the time goes:
time: 250 us; the launch traced here: 249 us
  waiting for transfers between devices  124 us (50%)
  other arithmetic  67.3 us (27%)
  local copies, waits for them, and re-layouts  20.7 us (8%)
  matrix products  17.7 us (7%)
  between operations  15.6 us (6%)
  starting transfers between devices  3.97 us (2%)
    psum x1, waiting for transfers between devices, per_device(): gram_matrix = lax.psum(gram_matrix, 'dev')  75.7 us
    psum x1, waiting for transfers between devices, per_device(): gram_matrix = lax.psum(gram_matrix, 'grp')  43.2 us
    another operation x6, other arithmetic, per_device(): lower_factor = jnp.linalg.cholesky(gram_matrix)  37 us
    another operation x3, other arithmetic, per_device(): lax.linalg.triangular_solve(lower_factor, latent_field, left_side=False,...  21.2 us
    gather x1, local copies, waits for them, and re-layouts, per_device(): gathered = extended_tiles[local_cols.T]  7.83 us
    another operation x6, local copies, waits for them, and re-layouts  5.31 us
    unnamed x20, local copies, waits for them, and re-layouts  5.29 us
    dot_general x1, matrix products, per_device(): jnp.einsum('eij,etjk->tik', cov_tiles, gathered, preferred_element_type=j...  5.28 us
  transfers between devices with their start and end apart: 4, of which 4 were waited for; matrix products, arithmetic and copies ran while one was open for 1% of the time, Pallas kernels for 0%

commit v1 on v0

v1 whole, which is shorter than its diff:
```python
import functools

import jax
import jax.numpy as jnp
from jax import lax
from jax.experimental import pallas as pl
from jax.experimental.pallas import tpu as pltpu
from jax.sharding import PartitionSpec as P

AXES = ("grp", "dev")
F32 = jnp.float32
BF16 = jnp.bfloat16
LANES = 128
SUBLANES = 8
VMEM_LIMIT = 48 * 1024 * 1024


def rows_dot(left, right):
    return lax.dot_general(left, right, (((0,), (0,)), ((), ())), preferred_element_type=F32)


def split2(value):
    high = value.astype(BF16)
    return high, (value - high.astype(F32)).astype(BF16)


def split3(value):
    high = value.astype(BF16)
    rest = value - high.astype(F32)
    middle = rest.astype(BF16)
    return high, middle, (rest - middle.astype(F32)).astype(BF16)


def as_column(vector, width):
    count = vector.shape[1]
    parts = [
        jnp.broadcast_to(vector[:, i : i + LANES], (LANES, LANES)).T for i in range(0, count, LANES)
    ]
    column = jnp.concatenate(parts, axis=0)
    return jnp.concatenate([column] * (width // LANES), axis=1)


def own_tile(cols_ref, odd, line, reach):
    count = 2 * reach
    line = jnp.where(odd == 1, count - 1 - line, line)
    half = line // reach
    first = half * reach
    start = cols_ref[first, reach]
    place = jnp.int32(0)
    for e in range(reach):
        place = place + jnp.where(cols_ref[first, e] >= start, 1, 0)
    return cols_ref[first, reach - place + line % reach] - cols_ref[0, reach]


def halo_tile(cols_ref, odd, distance, reach, lags, outer):
    count = 2 * reach
    low_side = (odd == 0) if outer else (odd == 1)
    edge_line = 0 if outer else count - 1
    tile = own_tile(cols_ref, odd, edge_line, reach)
    lag = jnp.where(low_side, reach - 1 - distance, reach + 1 + distance)
    column = cols_ref[tile, lag]
    base = cols_ref[0, reach] + jnp.where(low_side, -reach, count)
    return jnp.clip(column - base, 0, reach - 1)


def near_kernel(
    odd_ref, cols_ref, cov_ref, std_ref, outer_ref, inner_ref, halo_ref,
    acc_ref, scale_ref, lag_ref, high_ref, low_ref, gram_ref, lags_ref, lines_ref,
    *, reach, lags, tile,
):
    odd = odd_ref[0]
    count = 2 * reach
    for e in range(lags):
        lags_ref[:, e * tile : (e + 1) * tile] = cov_ref[jnp.where(odd == 1, lags - 1 - e, e)]
    lag_ref[...] = lags_ref[:, : reach * tile]
    for line in range(3 * reach):
        if line < reach:
            index = own_tile(cols_ref, odd, line, reach) - jnp.where(odd == 1, reach, 0)
            source = outer_ref
        elif line < count:
            index = own_tile(cols_ref, odd, line, reach) - jnp.where(odd == 1, 0, reach)
            source = inner_ref
        else:
            index = halo_tile(cols_ref, odd, line - count, reach, lags, False)
            source = halo_ref
        place = pl.multiple_of(index * tile, tile)
        lines_ref[line * tile : (line + 1) * tile, :] = source[pl.ds(place, tile), :]
    for line in range(count):
        first = max(0, reach - line)
        start = max(0, line - reach) * tile
        product = jnp.dot(
            lags_ref[:, first * tile :],
            lines_ref[start : start + (lags - first) * tile, :],
            preferred_element_type=F32,
        )
        std = std_ref[pl.ds(own_tile(cols_ref, odd, line, reach), 1), :]
        if line < reach:
            rows = slice(line * tile, (line + 1) * tile)
            acc_ref[rows, :] = product
            scale_ref[rows, :] = as_column(std, LANES)
        else:
            rows = slice((line - reach) * tile, (line - reach + 1) * tile)
            high, low = split2(product * as_column(std, product.shape[1]))
            high_ref[rows, :] = high
            low_ref[rows, :] = low
    gram_ref[...] = rows_dot(
        high_ref[...], jnp.concatenate([high_ref[...], low_ref[...]], axis=1)
    )


def far_kernel(
    odd_ref, cols_ref, lag_ref, scale_ref, acc_ref, halo_ref, gram_ref,
    high_ref, low_ref, keep_ref, send_ref, lines_ref,
    *, reach, lags, tile, total,
):
    odd = odd_ref[0]
    width = acc_ref.shape[1]
    for line in range(reach):
        index = halo_tile(cols_ref, odd, reach - 1 - line, reach, lags, True)
        place = pl.multiple_of(index * tile, tile)
        lines_ref[line * tile : (line + 1) * tile, :] = halo_ref[pl.ds(place, tile), :]
    for line in range(reach):
        rows = slice(line * tile, (line + 1) * tile)
        product = acc_ref[rows, :] + jnp.dot(
            lag_ref[:, : (reach - line) * tile],
            lines_ref[line * tile :, :],
            preferred_element_type=F32,
        )
        scale = jnp.concatenate([scale_ref[rows, :]] * (width // LANES), axis=1)
        high, low = split2(product * scale)
        high_ref[rows, :] = high
        low_ref[rows, :] = low
    both = gram_ref[...] + rows_dot(
        high_ref[...], jnp.concatenate([high_ref[...], low_ref[...]], axis=1)
    )
    cross = both[:, width:]
    gram = (both[:, :width] + (cross + cross.T)) * (1.0 / total)
    half = width // 2
    packed = jnp.concatenate([gram[:half, :half], gram[:half, half:], gram[half:, half:]], axis=1)
    upper, lower = packed[: half // 2], packed[half // 2 :]
    keep_ref[...] = jnp.where(odd == 1, lower, upper)
    send_ref[...] = jnp.where(odd == 1, upper, lower)


def spread(value):
    return jnp.broadcast_to(value, (SUBLANES, LANES))


def eliminate(work_ref, factor_ref, inverse_ref, panel=32):
    size = work_ref.shape[0]
    groups = panel // SUBLANES
    sublane = lax.broadcasted_iota(jnp.int32, (SUBLANES, LANES), 0)
    lane = lax.broadcasted_iota(jnp.int32, (panel, size), 1)
    row = lax.broadcasted_iota(jnp.int32, (panel, size), 0)
    short_lane = lax.broadcasted_iota(jnp.int32, (panel, LANES), 1)
    short_row = lax.broadcasted_iota(jnp.int32, (panel, LANES), 0)
    chunks = range(0, size, LANES)
    for start in range(0, size, panel):
        stop = start + panel
        chunk = start // LANES * LANES
        offset = start - chunk
        block = work_ref[start:stop, :]
        identity = jnp.where(short_lane - offset == short_row, 1.0, 0.0).astype(F32)
        natural = [
            [block[i : i + SUBLANES, c : c + LANES] for c in chunks] + [identity[i : i + SUBLANES]]
            for i in range(0, panel, SUBLANES)
        ]
        corner = [natural[g][chunk // LANES] for g in range(groups)]
        columns = [
            {g: spread(corner[g][:, offset + k : offset + k + 1]) for g in range(k // SUBLANES, groups)}
            for k in range(panel)
        ]
        for k in range(panel):
            at, inside = divmod(k, SUBLANES)
            scale = lax.rsqrt(spread(columns[k][at][inside : inside + 1, :]))
            lower = {g: columns[k][g] * scale for g in range(at, groups)}
            for m in range(k + 1, panel):
                group, place = divmod(m, SUBLANES)
                factor = spread(lower[group][place : place + 1, :])
                for g in range(group, groups):
                    columns[m][g] = columns[m][g] - lower[g] * factor
            below = dict(lower)
            below[at] = jnp.where(sublane > inside, lower[at], 0.0)
            for c in range(len(natural[0])):
                pivot = spread(natural[at][c][inside : inside + 1, :]) * scale
                for g in range(at, groups):
                    natural[g][c] = natural[g][c] - below[g] * pivot
                natural[at][c] = jnp.where(sublane == inside, pivot, natural[at][c])
        done = jnp.concatenate([jnp.concatenate(v[:-1], axis=1) for v in natural], axis=0)
        inverse = jnp.concatenate([v[-1] for v in natural], axis=0)
        empty = jnp.zeros((panel, LANES), F32)
        inverse = jnp.concatenate([inverse if c == chunk else empty for c in chunks], axis=1)
        factor_ref[start:stop, :] = jnp.where(lane >= row + start, done, 0.0)
        inverse_ref[start:stop, :] = jnp.where(lane < start, done, inverse)
        if stop < size:
            own = (lane >= start) & (lane < stop)
            a, b, c = split3(done)
            x, y, z = split3(jnp.where(own, inverse, done))
            first = stop // LANES * LANES
            left = jnp.concatenate([a, a, b, a, c, b], axis=0)
            right = jnp.concatenate([x, y, x, z, x, y], axis=0)
            update = rows_dot(left[:, first:], right)
            rest = work_ref[stop:, :]
            rest_lane = lax.broadcasted_iota(jnp.int32, rest.shape, 1)
            rest = jnp.where((rest_lane >= start) & (rest_lane < stop), 0.0, rest)
            work_ref[stop:, :] = rest - update[stop - first :, :]


def basis_kernel(
    odd_ref, cols_ref, mine_ref, other_ref, far_high_ref, far_low_ref, near_high_ref, near_low_ref,
    basis_ref, factor_ref, work_ref, inverse_ref,
    *, reach, tile,
):
    odd = odd_ref[0]
    size = work_ref.shape[0]
    half = size // 2
    mine, other = mine_ref[...], other_ref[...]
    packed = jnp.concatenate(
        [jnp.where(odd == 1, other, mine), jnp.where(odd == 1, mine, other)], axis=0
    )
    corner = packed[:, half:size]
    work_ref[:half, :] = packed[:, :size]
    work_ref[half:, :half] = corner.T
    work_ref[half:, half:] = packed[:, size:]
    eliminate(work_ref, factor_ref, inverse_ref)
    high, low = split2(inverse_ref[...])
    right = jnp.concatenate([high, high, low], axis=1)
    for line in range(2 * reach):
        high_ref, low_ref = (far_high_ref, far_low_ref) if line < reach else (near_high_ref, near_low_ref)
        rows = slice(line % reach * tile, (line % reach + 1) * tile)
        left = jnp.concatenate([high_ref[rows, :], low_ref[rows, :], high_ref[rows, :]], axis=1)
        place = pl.multiple_of(own_tile(cols_ref, odd, line, reach) * tile, tile)
        basis_ref[pl.ds(place, tile), :] = lax.dot_general(
            left, right, (((1,), (1,)), ((), ())), preferred_element_type=F32
        )


def call(kernel, outs, scratch, smem_count, operands, flops, moved):
    in_specs = [
        pl.BlockSpec(memory_space=pltpu.SMEM if i < smem_count else pltpu.VMEM)
        for i in range(len(operands))
    ]
    return pl.pallas_call(
        kernel,
        out_shape=outs,
        in_specs=in_specs,
        out_specs=[pl.BlockSpec(memory_space=pltpu.VMEM) for _ in outs],
        scratch_shapes=scratch,
        cost_estimate=pl.CostEstimate(flops=flops, bytes_accessed=moved, transcendentals=0),
        compiler_params=pltpu.CompilerParams(vmem_limit_bytes=VMEM_LIMIT),
    )(*operands)


def per_device(device_count, sketch, marginal_std, cov_tiles, tile_cols):
    row_count, width = sketch.shape
    lags, tile, _ = cov_tiles.shape
    reach = (lags - 1) // 2
    halo = reach * tile
    assert row_count == 2 * halo and width % (2 * LANES) == 0
    assert device_count & (device_count - 1) == 0 and device_count > 1
    odd = lax.axis_index(AXES) % 2
    odd_arg = odd.astype(jnp.int32).reshape(1)

    def scaled(start):
        rows = lax.dynamic_slice_in_dim(sketch, start, halo, axis=0)
        std = lax.dynamic_slice_in_dim(marginal_std, start, halo, axis=0)
        return (rows.astype(F32) * std[:, None]).astype(BF16)

    def swap(value, mask):
        return lax.ppermute(value, AXES, [(i, i ^ mask) for i in range(device_count)])

    outer_pairs = []
    for i in range(1, device_count - 1, 2):
        outer_pairs += [(i, i + 1), (i + 1, i)]
    outer = scaled(jnp.where(odd == 1, halo, 0))
    inner = scaled(jnp.where(odd == 1, 0, halo))
    outer_halo = lax.ppermute(outer, AXES, outer_pairs)
    inner_halo = swap(inner, 1)

    def shape(rows, columns, dtype):
        return jax.ShapeDtypeStruct((rows, columns), dtype)

    acc, scale, lag_block, near_high, near_low, near_gram = call(
        functools.partial(near_kernel, reach=reach, lags=lags, tile=tile),
        [
            shape(halo, width, F32),
            shape(halo, LANES, F32),
            shape(tile, halo, BF16),
            shape(halo, width, BF16),
            shape(halo, width, BF16),
            shape(width, 2 * width, F32),
        ],
        [pltpu.VMEM((tile, lags * tile), BF16), pltpu.VMEM((3 * halo, width), BF16)],
        2,
        (odd_arg, tile_cols, cov_tiles, marginal_std.reshape(-1, tile), outer, inner, inner_halo),
        2 * 62 * tile * tile * width,
        8 << 20,
    )
    far_high, far_low, keep, send = call(
        functools.partial(
            far_kernel, reach=reach, lags=lags, tile=tile, total=row_count * device_count
        ),
        [
            shape(halo, width, BF16),
            shape(halo, width, BF16),
            shape(width // 4, width // 2 * 3, F32),
            shape(width // 4, width // 2 * 3, F32),
        ],
        [pltpu.VMEM((halo, width), BF16)],
        2,
        (odd_arg, tile_cols, lag_block, scale, acc, outer_halo, near_gram),
        2 * 18 * tile * tile * width,
        4 << 20,
    )
    gram = keep + swap(send, 1)
    mask = 2
    while mask < device_count:
        gram = gram + swap(gram, mask)
        mask *= 2
    other = swap(gram, 1)
    basis, factor = call(
        functools.partial(basis_kernel, reach=reach, tile=tile),
        [shape(row_count, width, F32), shape(width, width, F32)],
        [pltpu.VMEM((width, width), F32), pltpu.VMEM((width, width), F32)],
        2,
        (odd_arg, tile_cols, gram, other, far_high, far_low, near_high, near_low),
        2 * 24 * tile * tile * width,
        4 << 20,
    )
    return basis, factor


def solution(mesh):
    device_count = mesh.shape["grp"] * mesh.shape["dev"]
    in_specs = (P(AXES, None), P(AXES), P(), P(AXES, None))
    out_specs = (P(AXES, None), P())
    return jax.shard_map(
        functools.partial(per_device, device_count),
        mesh=mesh,
        in_specs=in_specs,
        out_specs=out_specs,
        check_vma=False,
    )
```

time: 250 us -> 59.2 us (0.24)
  waiting for transfers between devices: 124 us -> 16.4 us
  other arithmetic: 67.3 us -> 1.6 us
  starting transfers between devices: 3.97 us -> 24.4 us
  local copies, waits for them, and re-layouts: 20.7 us -> 0.74 us
  matrix products: 17.7 us -> 0 us
  Pallas kernels: 0 us -> 15.1 us
  between operations: 15.6 us -> 0.75 us
    psum x2 -> x0, waiting for transfers between devices: 119 us -> none  [the longest x1 75.7 us: per_device(): gram_matrix = lax.psum(gram_matrix, 'dev')]
    another operation x9 -> x0, other arithmetic: 58.2 us -> none  [the longest x6 37 us: per_device(): lower_factor = jnp.linalg.cholesky(gram_matrix)]
    ppermute x2 -> x8, starting transfers between devices: 3.72 us -> 24.4 us  [the longest x7 23.7 us: swap(): lax.ppermute(value, AXES, [(i, i ^ mask) for i in range(device_count)])]
    pallas_call x0 -> x3, Pallas kernels: none -> 15.1 us  [call(): pl.pallas_call(kernel, out_shape=outs, in_specs=in_specs, out_specs=[pl.B...]
    ppermute x2 -> x8, waiting for transfers between devices: 5.18 us -> 16.4 us  [the longest x7 16.4 us: swap(): lax.ppermute(value, AXES, [(i, i ^ mask) for i in range(device_count)])]
    dot_general x2 -> x0, matrix products: 10.1 us -> none  [the longest x1 5.28 us: per_device(): jnp.einsum('eij,etjk->tik', cov_tiles, gathered, preferred_element_type=j...]
    gather x1 -> x0, local copies, waits for them, and re-layouts: 7.83 us -> none  [per_device(): gathered = extended_tiles[local_cols.T]]
    another operation x5 -> x0, matrix products: 7.65 us -> none  [the longest x3 4.83 us: per_device(): lax.linalg.triangular_solve(lower_factor, latent_field, left_side=False,...]
  transfers between devices with their start and end apart: 4 -> 8, of which waited for: 4 -> 7; matrix products, arithmetic and copies ran while one was open for 1% -> 0% of each run, Pallas kernels for 0% -> 7%
where the time goes in v1:
time: 59.2 us; the launch traced here: 59 us
  starting transfers between devices  24.4 us (41%)
  waiting for transfers between devices  16.4 us (28%)
  Pallas kernels  15.1 us (26%)
  other arithmetic  1.6 us (3%)
  between operations  0.75 us (1%)
  local copies, waits for them, and re-layouts  0.74 us (1%)
    ppermute x7, starting transfers between devices, swap(): lax.ppermute(value, AXES, [(i, i ^ mask) for i in range(device_count)])  23.7 us
    ppermute x7, waiting for transfers between devices, swap(): lax.ppermute(value, AXES, [(i, i ^ mask) for i in range(device_count)])  16.4 us
    pallas_call x3, Pallas kernels, call(): pl.pallas_call(kernel, out_shape=outs, in_specs=in_specs, out_specs=[pl.B...  15.1 us
    convert_element_type x1, other arithmetic, scaled(): return (rows.astype(F32) * std[:, None]).astype(BF16)  1.53 us
  transfers between devices with their start and end apart: 8, of which 7 were waited for; matrix products, arithmetic and copies ran while one was open for 0% of the time, Pallas kernels for 7%

profile of v1, /device:TPU:0, one launch (start us, length us, event | category | flops | bytes accessed | tf_op | source)
XLA Modules:
  0.0 59.0 jit_solution(8096105560881544659)
XLA Ops:
  0.6 0.0 copy-start.1
  0.6 0.0 copy-start
  0.7 0.7 %fusion = (f32[1024]{0:T(1024)S(1)}, f32[1024]{0:T(1024)S(1)}) fusion(f32[2048]{0:T(1024)} %param.5, s32[]{:T(128)S(6)} %select_n.20, s32[]{:T(128)S(6)} %select_n.19), kind=kLoop, calls=%fused_computation.2 | loop fusion | bytes 16392 | tf_op jit(solution)/shard_map/dynamic_slice | solution.py:266
  1.4 1.5 %multiply_convert_fusion = (bf16[1024,256]{1,0:T(8,128)(2,1)S(1)}, bf16[1024,256]{1,0:T(8,128)(2,1)S(1)}) fusion(f32[1024]{0:T(1024)S(1)} %get-tuple-element.24, bf16[2048,256]{1,0:T(8,128)(2,1)} %param.4, s32[]{:T(128)S(6)} %select_n.20, f32[1024]{0:T(1024)S(1)} %get-tuple-element.25, s32[]{:T(128)S(6)} %select_n.19), kind=kLoop, calls=%fused_computation | loop fusion | flops 1572864 | bytes 2105352 | tf_op jit(solution)/shard_map/convert_element_type | solution.py:267
  2.9 0.5 collective-permute-start
  3.5 0.7 %collective-permute-start.1 = (bf16[1024,256]{1,0:T(8,128)(2,1)S(1)}, bf16[1024,256]{1,0:T(8,128)(2,1)S(1)}, u32[]{:S(2)}, u32[]{:S(2)}) collective-permute-start(bf16[1024,256]{1,0:T(8,128)(2,1)S(1)} %get-tuple-element.23.outer_ref), channel_id=1, source_target_pairs={{1,2},{2,1},{3,4},{4,3},{5,6},{6,5},{7,8},{8,7},{9,10},{10,9},{11,... | collective-permute-start | bytes 1572872 | tf_op jit(solution)/shard_map/ppermute | solution.py:277
  4.1 0.0 copy-done.1
  4.2 0.8 %collective-permute-done.halo_ref = bf16[1024,256]{1,0:T(8,128)(2,1)S(1)} collective-permute-done((bf16[1024,256]{1,0:T(8,128)(2,1)S(1)}, bf16[1024,256]{1,0:T(8,128)(2,1)S(1)}, u32[]{:S(2)}, u32[]{:S(2)}) %collective-permute-start) | collective-permute-done | bytes 524320 | tf_op jit(solution)/shard_map/ppermute | solution.py:270
  5.0 0.0 copy-done
  5.0 3.9 %shard_map.59 = (f32[1024,256]{1,0:T(8,128)S(1)}, f32[1024,128]{1,0:T(8,128)S(1)}, bf16[256,1024]{1,0:T(8,128)(2,1)S(1)}, bf16[1024,256]{1,0:T(8,128)(2,1)S(1)},...) custom-call(s32[1]{0:T(128)} %bitcast.odd_ref, s32[8,9]{1,0:T(8,128)S(1)} %copy-done, ...), custom_call_target="tpu_custom_call" | custom-call | flops 2080374784 | bytes 8388608 | tf_op jit(solution)/shard_map/pallas_call | solution.py:243
  8.9 0.0 collective-permute-done.1.halo_ref
  8.9 1.6 %shard_map.60 = (bf16[1024,256]{1,0:T(8,128)(2,1)S(1)}, bf16[1024,256]{1,0:T(8,128)(2,1)S(1)}, f32[64,384]{1,0:T(8,128)S(1)}, f32[64,384]{1,0:T(8,128)S(1)}) custom-call(s32[1]{0:T(128)} %bitcast.odd_ref, s32[8,9]{1,0:T(8,128)S(1)} %copy-done, bf16[256,1024]{1,0:T(8,128)(2,1)S(1)} %get-tuple-element.12.lag_ref, f32[1024,128]{1,0:T(8,128)S(1)} %get-tuple-element.13.scale_ref, ...), custom_call_target="tpu_custom_call" | custom-call | flops 603979776 | bytes 4194304 | tf_op jit(solution)/shard_map/pallas_call | solution.py:243
  10.6 9.1 %collective-permute-start.2 = (f32[64,384]{1,0:T(8,128)S(1)}, f32[64,384]{1,0:T(8,128)S(1)}, u32[]{:S(2)}, u32[]{:S(2)}) collective-permute-start(f32[64,384]{1,0:T(8,128)S(1)} %get-tuple-element.17), channel_id=1, source_target_pairs={{0,1},{1,0},{2,3},{3,2},{4,5},{5,4},{6,7},{7,6},{8,9},{9,8},{10,11... | collective-permute-start | bytes 294920 | tf_op jit(solution)/shard_map/ppermute | solution.py:270
  19.6 0.9 %collective-permute-done.2 = f32[64,384]{1,0:T(8,128)S(1)} collective-permute-done((f32[64,384]{1,0:T(8,128)S(1)}, f32[64,384]{1,0:T(8,128)S(1)}, u32[]{:S(2)}, u32[]{:S(2)}) %collective-permute-start.2) | collective-permute-done | bytes 98336 | tf_op jit(solution)/shard_map/ppermute | solution.py:270
  20.6 3.7 %collective-permute-start.3 = (f32[64,384]{1,0:T(8,128)S(1)}, f32[64,384]{1,0:T(8,128)S(1)}, u32[]{:S(2)}, u32[]{:S(2)}) collective-permute-start(f32[64,384]{1,0:T(8,128)S(1)} %add.28), channel_id=1, source_target_pairs={{0,2},{1,3},{2,0},{3,1},{4,6},{5,7},{6,4},{7,5},{8,10},{9,11},{10,... | collective-permute-start | bytes 294920 | tf_op jit(solution)/shard_map/ppermute | solution.py:270
  24.3 3.3 %collective-permute-done.3 = f32[64,384]{1,0:T(8,128)S(1)} collective-permute-done((f32[64,384]{1,0:T(8,128)S(1)}, f32[64,384]{1,0:T(8,128)S(1)}, u32[]{:S(2)}, u32[]{:S(2)}) %collective-permute-start.3) | collective-permute-done | bytes 98336 | tf_op jit(solution)/shard_map/ppermute | solution.py:270
  27.6 3.9 %collective-permute-start.4 = (f32[64,384]{1,0:T(8,128)S(1)}, f32[64,384]{1,0:T(8,128)S(1)}, u32[]{:S(2)}, u32[]{:S(2)}) collective-permute-start(f32[64,384]{1,0:T(8,128)S(1)} %add.29), channel_id=1, source_target_pairs={{0,4},{1,5},{2,6},{3,7},{4,0},{5,1},{6,2},{7,3},{8,12},{9,13},{10,... | collective-permute-start | bytes 294920 | tf_op jit(solution)/shard_map/ppermute | solution.py:270
  31.5 4.7 %collective-permute-done.4 = f32[64,384]{1,0:T(8,128)S(1)} collective-permute-done((f32[64,384]{1,0:T(8,128)S(1)}, f32[64,384]{1,0:T(8,128)S(1)}, u32[]{:S(2)}, u32[]{:S(2)}) %collective-permute-start.4) | collective-permute-done | bytes 98336 | tf_op jit(solution)/shard_map/ppermute | solution.py:270
  36.3 3.6 %collective-permute-start.5 = (f32[64,384]{1,0:T(8,128)S(1)}, f32[64,384]{1,0:T(8,128)S(1)}, u32[]{:S(2)}, u32[]{:S(2)}) collective-permute-start(f32[64,384]{1,0:T(8,128)S(1)} %add.30), channel_id=1, source_target_pairs={{0,8},{1,9},{2,10},{3,11},{4,12},{5,13},{6,14},{7,15},{8,0},{9,1},... | collective-permute-start | bytes 294920 | tf_op jit(solution)/shard_map/ppermute | solution.py:270
  39.8 2.8 %collective-permute-done.5 = f32[64,384]{1,0:T(8,128)S(1)} collective-permute-done((f32[64,384]{1,0:T(8,128)S(1)}, f32[64,384]{1,0:T(8,128)S(1)}, u32[]{:S(2)}, u32[]{:S(2)}) %collective-permute-start.5) | collective-permute-done | bytes 98336 | tf_op jit(solution)/shard_map/ppermute | solution.py:270
  42.6 2.9 %collective-permute-start.6 = (f32[64,384]{1,0:T(8,128)S(1)}, f32[64,384]{1,0:T(8,128)S(1)}, u32[]{:S(2)}, u32[]{:S(2)}) collective-permute-start(f32[64,384]{1,0:T(8,128)S(1)} %add.31), channel_id=1, source_target_pairs={{0,16},{1,17},{2,18},{3,19},{4,20},{5,21},{6,22},{7,23},{8,24},{9,... | collective-permute-start | bytes 294920 | tf_op jit(solution)/shard_map/ppermute | solution.py:270
  45.5 2.6 %collective-permute-done.6 = f32[64,384]{1,0:T(8,128)S(1)} collective-permute-done((f32[64,384]{1,0:T(8,128)S(1)}, f32[64,384]{1,0:T(8,128)S(1)}, u32[]{:S(2)}, u32[]{:S(2)}) %collective-permute-start.6) | collective-permute-done | bytes 98336 | tf_op jit(solution)/shard_map/ppermute | solution.py:270
  48.1 0.1 collective-permute-start.7
  48.2 1.3 %collective-permute-done.7.other_ref = f32[64,384]{1,0:T(8,128)S(1)} collective-permute-done((f32[64,384]{1,0:T(8,128)S(1)}, f32[64,384]{1,0:T(8,128)S(1)}, u32[]{:S(2)}, u32[]{:S(2)}) %collective-permute-start.7) | collective-permute-done | bytes 98336 | tf_op jit(solution)/shard_map/ppermute | solution.py:270
  49.5 9.5 %shard_map.61 = (f32[2048,256]{1,0:T(8,128)}, f32[256,256]{1,0:T(8,128)}) custom-call(s32[1]{0:T(128)} %bitcast.odd_ref, s32[8,9]{1,0:T(8,128)S(1)} %copy-done, f32[64,384]{1,0:T(8,128)S(1)} %add.32.mine_ref, f32[64,384]{1,0:T(8,128)S(1)} %collective-permute-done.7.other_ref, bf16[1024,256]{1,0:T(8,128)(2,1)S(1)} %get-tuple-element.18.far_high_ref, ...), custom_call_target="tpu_custom_call" | custom-call | flops 805306368 | bytes 4194304 | tf_op jit(solution)/shard_map/pallas_call | solution.py:243
  (6 shorter events, 0.1 us)
Async XLA Ops:
  0.6 3.5 %copy-start.1 = (f32[2048]{0:T(1024)S(1)}, f32[2048]{0:T(1024)}, u32[]{:S(2)}) copy-start(f32[2048]{0:T(1024)} %param.5) | copy-start | bytes 24580
  0.6 4.4 %copy-start = (s32[8,9]{1,0:T(8,128)S(1)}, s32[8,9]{1,0:T(8,128)}, u32[]{:S(2)}) copy-start(s32[8,9]{1,0:T(8,128)} %cols_ref.5) | copy-start | bytes 868
  2.9 2.1 %collective-permute-start = (bf16[1024,256]{1,0:T(8,128)(2,1)S(1)}, bf16[1024,256]{1,0:T(8,128)(2,1)S(1)}, u32[]{:S(2)}, u32[]{:S(2)}) collective-permute-start(bf16[1024,256]{1,0:T(8,128)(2,1)S(1)} %get-tuple-element.22.inner_ref), channel_id=1, source_target_pairs={{0,1},{1,0},{2,3},{3,2},{4,5},{5,4},{6,7},{7,6},{8,9},{9,8},{10,11... | collective-permute-start | bytes 1572872 | tf_op jit(solution)/shard_map/ppermute | solution.py:270
  3.5 5.5 %collective-permute-start.1 = (bf16[1024,256]{1,0:T(8,128)(2,1)S(1)}, bf16[1024,256]{1,0:T(8,128)(2,1)S(1)}, u32[]{:S(2)}, u32[]{:S(2)}) collective-permute-start(bf16[1024,256]{1,0:T(8,128)(2,1)S(1)} %get-tuple-element.23.outer_ref), channel_id=1, source_target_pairs={{1,2},{2,1},{3,4},{4,3},{5,6},{6,5},{7,8},{8,7},{9,10},{10,9},{11,... | collective-permute-start | bytes 1572872 | tf_op jit(solution)/shard_map/ppermute | solution.py:277
  10.6 10.0 %collective-permute-start.2 = (f32[64,384]{1,0:T(8,128)S(1)}, f32[64,384]{1,0:T(8,128)S(1)}, u32[]{:S(2)}, u32[]{:S(2)}) collective-permute-start(f32[64,384]{1,0:T(8,128)S(1)} %get-tuple-element.17), channel_id=1, source_target_pairs={{0,1},{1,0},{2,3},{3,2},{4,5},{5,4},{6,7},{7,6},{8,9},{9,8},{10,11... | collective-permute-start | bytes 294920 | tf_op jit(solution)/shard_map/ppermute | solution.py:270
  20.6 7.0 %collective-permute-start.3 = (f32[64,384]{1,0:T(8,128)S(1)}, f32[64,384]{1,0:T(8,128)S(1)}, u32[]{:S(2)}, u32[]{:S(2)}) collective-permute-start(f32[64,384]{1,0:T(8,128)S(1)} %add.28), channel_id=1, source_target_pairs={{0,2},{1,3},{2,0},{3,1},{4,6},{5,7},{6,4},{7,5},{8,10},{9,11},{10,... | collective-permute-start | bytes 294920 | tf_op jit(solution)/shard_map/ppermute | solution.py:270
  27.6 8.6 %collective-permute-start.4 = (f32[64,384]{1,0:T(8,128)S(1)}, f32[64,384]{1,0:T(8,128)S(1)}, u32[]{:S(2)}, u32[]{:S(2)}) collective-permute-start(f32[64,384]{1,0:T(8,128)S(1)} %add.29), channel_id=1, source_target_pairs={{0,4},{1,5},{2,6},{3,7},{4,0},{5,1},{6,2},{7,3},{8,12},{9,13},{10,... | collective-permute-start | bytes 294920 | tf_op jit(solution)/shard_map/ppermute | solution.py:270
  36.3 6.3 %collective-permute-start.5 = (f32[64,384]{1,0:T(8,128)S(1)}, f32[64,384]{1,0:T(8,128)S(1)}, u32[]{:S(2)}, u32[]{:S(2)}) collective-permute-start(f32[64,384]{1,0:T(8,128)S(1)} %add.30), channel_id=1, source_target_pairs={{0,8},{1,9},{2,10},{3,11},{4,12},{5,13},{6,14},{7,15},{8,0},{9,1},... | collective-permute-start | bytes 294920 | tf_op jit(solution)/shard_map/ppermute | solution.py:270
  42.6 5.5 %collective-permute-start.6 = (f32[64,384]{1,0:T(8,128)S(1)}, f32[64,384]{1,0:T(8,128)S(1)}, u32[]{:S(2)}, u32[]{:S(2)}) collective-permute-start(f32[64,384]{1,0:T(8,128)S(1)} %add.31), channel_id=1, source_target_pairs={{0,16},{1,17},{2,18},{3,19},{4,20},{5,21},{6,22},{7,23},{8,24},{9,... | collective-permute-start | bytes 294920 | tf_op jit(solution)/shard_map/ppermute | solution.py:270
  48.1 1.4 %collective-permute-start.7 = (f32[64,384]{1,0:T(8,128)S(1)}, f32[64,384]{1,0:T(8,128)S(1)}, u32[]{:S(2)}, u32[]{:S(2)}) collective-permute-start(f32[64,384]{1,0:T(8,128)S(1)} %add.32.mine_ref), channel_id=1, source_target_pairs={{0,1},{1,0},{2,3},{3,2},{4,5},{5,4},{6,7},{7,6},{8,9},{9,8},{10,11... | collective-permute-start | bytes 294920 | tf_op jit(solution)/shard_map/ppermute | solution.py:270

commit v2 on v1

--- a/solution.py
+++ b/solution.py
@@ -13,6 +13,7 @@
 LANES = 128
 SUBLANES = 8
 VMEM_LIMIT = 48 * 1024 * 1024
+SMALL_COST = pl.CostEstimate(flops=1, bytes_accessed=1, transcendentals=0)
 
 
 def rows_dot(left, right):
@@ -31,10 +32,10 @@
     return high, middle, (rest - middle.astype(F32)).astype(BF16)
 
 
-def as_column(vector, width):
-    count = vector.shape[1]
+def std_column(std_ref, index, tile, width):
+    rows = tile // LANES
     parts = [
-        jnp.broadcast_to(vector[:, i : i + LANES], (LANES, LANES)).T for i in range(0, count, LANES)
+        jnp.broadcast_to(std_ref[pl.ds(index * rows + i, 1), :], (LANES, LANES)).T for i in range(rows)
     ]
     column = jnp.concatenate(parts, axis=0)
     return jnp.concatenate([column] * (width // LANES), axis=1)
@@ -61,6 +62,27 @@
     column = cols_ref[tile, lag]
     base = cols_ref[0, reach] + jnp.where(low_side, -reach, count)
     return jnp.clip(column - base, 0, reach - 1)
+
+
+def scale_kernel(odd_ref, std_hbm_ref, sketch_ref, outer_ref, inner_ref, std_ref, rows_ref, sems, *, reach, tile):
+    width = outer_ref.shape[1]
+    count = 2 * reach
+    first = jnp.where(odd_ref[0] == 1, reach, 0)
+    order = [(first + i) % count for i in range(count)]
+    copies = [pltpu.make_async_copy(std_hbm_ref, std_ref, sems.at[count])]
+    for i, index in enumerate(order):
+        place = pl.multiple_of(index * tile, tile)
+        target = rows_ref.at[pl.ds(i * tile, tile), :]
+        copies.append(pltpu.make_async_copy(sketch_ref.at[pl.ds(place, tile), :], target, sems.at[i]))
+    for copy in copies:
+        copy.start()
+    copies[0].wait()
+    for i, index in enumerate(order):
+        std = std_column(std_ref, index, tile, width)
+        copies[i + 1].wait()
+        scaled = (rows_ref[i * tile : (i + 1) * tile, :].astype(F32) * std).astype(BF16)
+        place = i % reach * tile
+        (outer_ref if i < reach else inner_ref)[place : place + tile, :] = scaled
 
 
 def near_kernel(
@@ -93,14 +115,14 @@
             lines_ref[start : start + (lags - first) * tile, :],
             preferred_element_type=F32,
         )
-        std = std_ref[pl.ds(own_tile(cols_ref, odd, line, reach), 1), :]
+        own = own_tile(cols_ref, odd, line, reach)
         if line < reach:
             rows = slice(line * tile, (line + 1) * tile)
             acc_ref[rows, :] = product
-            scale_ref[rows, :] = as_column(std, LANES)
+            scale_ref[rows, :] = std_column(std_ref, own, tile, LANES)
         else:
             rows = slice((line - reach) * tile, (line - reach + 1) * tile)
-            high, low = split2(product * as_column(std, product.shape[1]))
+            high, low = split2(product * std_column(std_ref, own, tile, product.shape[1]))
             high_ref[rows, :] = high
             low_ref[rows, :] = low
     gram_ref[...] = rows_dot(
@@ -135,11 +157,40 @@
     )
     cross = both[:, width:]
     gram = (both[:, :width] + (cross + cross.T)) * (1.0 / total)
-    half = width // 2
-    packed = jnp.concatenate([gram[:half, :half], gram[:half, half:], gram[half:, half:]], axis=1)
-    upper, lower = packed[: half // 2], packed[half // 2 :]
+    packed = pack(gram)
+    count = packed.shape[0] // 2
+    upper, lower = packed[:count], packed[count:]
     keep_ref[...] = jnp.where(odd == 1, lower, upper)
     send_ref[...] = jnp.where(odd == 1, upper, lower)
+
+
+def pack(gram):
+    half = gram.shape[0] // 2
+    row = lax.broadcasted_iota(jnp.int32, (half, half), 0)
+    column = lax.broadcasted_iota(jnp.int32, (half, half), 1)
+    last = gram[half:, half:]
+    diagonal = jnp.sum(jnp.where(row == column, last, 0.0), axis=0, keepdims=True)
+    extra = jnp.broadcast_to(diagonal, (SUBLANES, half))
+    extra = jnp.concatenate([extra, extra], axis=1)
+    body = jnp.concatenate([gram[:half, half:], jnp.where(column >= row, gram[:half, :half], last)], axis=1)
+    return jnp.concatenate([body[: half // 2], extra, body[half // 2 :], extra], axis=0)
+
+
+def unpack(upper, lower, work_ref):
+    size = work_ref.shape[0]
+    half = size // 2
+    body = jnp.concatenate([upper[: half // 2], lower[: half // 2]], axis=0)
+    corner, mixed = body[:, :half], body[:, half:]
+    row = lax.broadcasted_iota(jnp.int32, (half, half), 0)
+    column = lax.broadcasted_iota(jnp.int32, (half, half), 1)
+    turned = mixed.T
+    diagonal = jnp.broadcast_to(upper[half // 2 : half // 2 + 1, :half], (half, half))
+    work_ref[:half, :half] = jnp.where(column >= row, mixed, turned)
+    work_ref[:half, half:] = corner
+    work_ref[half:, :half] = corner.T
+    work_ref[half:, half:] = jnp.where(
+        row == column, diagonal, jnp.where(column > row, turned, mixed)
+    )
 
 
 def spread(value):
@@ -212,16 +263,8 @@
     *, reach, tile,
 ):
     odd = odd_ref[0]
-    size = work_ref.shape[0]
-    half = size // 2
     mine, other = mine_ref[...], other_ref[...]
-    packed = jnp.concatenate(
-        [jnp.where(odd == 1, other, mine), jnp.where(odd == 1, mine, other)], axis=0
-    )
-    corner = packed[:, half:size]
-    work_ref[:half, :] = packed[:, :size]
-    work_ref[half:, :half] = corner.T
-    work_ref[half:, half:] = packed[:, size:]
+    unpack(jnp.where(odd == 1, other, mine), jnp.where(odd == 1, mine, other), work_ref)
     eliminate(work_ref, factor_ref, inverse_ref)
     high, low = split2(inverse_ref[...])
     right = jnp.concatenate([high, high, low], axis=1)
@@ -235,7 +278,7 @@
         )
 
 
-def call(kernel, outs, scratch, smem_count, operands, flops, moved):
+def call(kernel, outs, scratch, smem_count, operands):
     in_specs = [
         pl.BlockSpec(memory_space=pltpu.SMEM if i < smem_count else pltpu.VMEM)
         for i in range(len(operands))
@@ -246,7 +289,7 @@
         in_specs=in_specs,
         out_specs=[pl.BlockSpec(memory_space=pltpu.VMEM) for _ in outs],
         scratch_shapes=scratch,
-        cost_estimate=pl.CostEstimate(flops=flops, bytes_accessed=moved, transcendentals=0),
+        cost_estimate=SMALL_COST,
         compiler_params=pltpu.CompilerParams(vmem_limit_bytes=VMEM_LIMIT),
     )(*operands)
 
@@ -261,10 +304,29 @@
     odd = lax.axis_index(AXES) % 2
     odd_arg = odd.astype(jnp.int32).reshape(1)
 
-    def scaled(start):
-        rows = lax.dynamic_slice_in_dim(sketch, start, halo, axis=0)
-        std = lax.dynamic_slice_in_dim(marginal_std, start, halo, axis=0)
-        return (rows.astype(F32) * std[:, None]).astype(BF16)
+    std_rows = marginal_std.reshape(-1, LANES)
+
+    outer, inner = pl.pallas_call(
+        functools.partial(scale_kernel, reach=reach, tile=tile),
+        out_shape=[jax.ShapeDtypeStruct((halo, width), BF16)] * 2,
+        in_specs=[
+            pl.BlockSpec(memory_space=pltpu.SMEM),
+            pl.BlockSpec(memory_space=pltpu.HBM),
+            pl.BlockSpec(memory_space=pltpu.HBM),
+        ],
+        out_specs=[pl.BlockSpec(memory_space=pltpu.VMEM)] * 2,
+        scratch_shapes=[
+            pltpu.VMEM(std_rows.shape, F32),
+            pltpu.VMEM((row_count, width), BF16),
+            pltpu.SemaphoreType.DMA((2 * reach + 1,)),
+        ],
+        cost_estimate=SMALL_COST,
+        compiler_params=pltpu.CompilerParams(vmem_limit_bytes=VMEM_LIMIT),
+    )(
+        odd_arg,
+        pltpu.with_memory_space_constraint(std_rows, pltpu.HBM),
+        pltpu.with_memory_space_constraint(sketch, pltpu.HBM),
+    )
 
     def swap(value, mask):
         return lax.ppermute(value, AXES, [(i, i ^ mask) for i in range(device_count)])
@@ -272,8 +334,6 @@
     outer_pairs = []
     for i in range(1, device_count - 1, 2):
         outer_pairs += [(i, i + 1), (i + 1, i)]
-    outer = scaled(jnp.where(odd == 1, halo, 0))
-    inner = scaled(jnp.where(odd == 1, 0, halo))
     outer_halo = lax.ppermute(outer, AXES, outer_pairs)
     inner_halo = swap(inner, 1)
 
@@ -292,9 +352,7 @@
         ],
         [pltpu.VMEM((tile, lags * tile), BF16), pltpu.VMEM((3 * halo, width), BF16)],
         2,
-        (odd_arg, tile_cols, cov_tiles, marginal_std.reshape(-1, tile), outer, inner, inner_halo),
-        2 * 62 * tile * tile * width,
-        8 << 20,
+        (odd_arg, tile_cols, cov_tiles, std_rows, outer, inner, inner_halo),
     )
     far_high, far_low, keep, send = call(
         functools.partial(
@@ -303,20 +361,19 @@
         [
             shape(halo, width, BF16),
             shape(halo, width, BF16),
-            shape(width // 4, width // 2 * 3, F32),
-            shape(width // 4, width // 2 * 3, F32),
+            shape(width // 4 + SUBLANES, width, F32),
+            shape(width // 4 + SUBLANES, width, F32),
         ],
         [pltpu.VMEM((halo, width), BF16)],
         2,
         (odd_arg, tile_cols, lag_block, scale, acc, outer_halo, near_gram),
-        2 * 18 * tile * tile * width,
-        4 << 20,
     )
     gram = keep + swap(send, 1)
-    mask = 2
-    while mask < device_count:
-        gram = gram + swap(gram, mask)
-        mask *= 2
+    masks = [1 << i for i in range(1, device_count.bit_length() - 1)]
+    middle = len(masks) // 2
+    for even_mask, odd_mask in zip(masks[middle:] + masks[:middle], masks):
+        pairs = [(i, i ^ (odd_mask if i % 2 else even_mask)) for i in range(device_count)]
+        gram = gram + lax.ppermute(gram, AXES, pairs)
     other = swap(gram, 1)
     basis, factor = call(
         functools.partial(basis_kernel, reach=reach, tile=tile),
@@ -324,8 +381,6 @@
         [pltpu.VMEM((width, width), F32), pltpu.VMEM((width, width), F32)],
         2,
         (odd_arg, tile_cols, gram, other, far_high, far_low, near_high, near_low),
-        2 * 24 * tile * tile * width,
-        4 << 20,
     )
     return basis, factor
 

time: 59.2 us -> 56.2 us (0.949)
  starting transfers between devices: 24.4 us -> 19.3 us
  Pallas kernels: 15.1 us -> 17 us
  other arithmetic: 1.6 us -> 0.06 us
  waiting for transfers between devices: 16.4 us -> 17.5 us
  local copies, waits for them, and re-layouts: 0.74 us -> 1.38 us
    ppermute x7 -> x3, starting transfers between devices: 23.7 us -> 8.27 us  [swap(): lax.ppermute(value, AXES, [(i, i ^ mask) for i in range(device_count)])]
    ppermute x0 -> x4, waiting for transfers between devices: none -> 14.5 us  [per_device(): gram = gram + lax.ppermute(gram, AXES, pairs)]
    ppermute x7 -> x3, waiting for transfers between devices: 16.4 us -> 3.01 us  [swap(): lax.ppermute(value, AXES, [(i, i ^ mask) for i in range(device_count)])]
    ppermute x0 -> x4, starting transfers between devices: none -> 10.4 us  [per_device(): gram = gram + lax.ppermute(gram, AXES, pairs)]
    pallas_call x0 -> x1, Pallas kernels: none -> 1.81 us  [per_device(): pl.pallas_call(functools.partial(scale_kernel, reach=reach, tile=tile), o...]
    convert_element_type x1 -> x0, other arithmetic: 1.53 us -> none  [scaled(): return (rows.astype(F32) * std[:, None]).astype(BF16)]
    unnamed x4, local copies, waits for them, and re-layouts: 0.01 us -> 1.38 us
    dynamic_slice x1 -> x0, local copies, waits for them, and re-layouts: 0.72 us -> none  [scaled(): std = lax.dynamic_slice_in_dim(marginal_std, start, halo, axis=0)]
where the time goes in v2:
time: 56.2 us; the launch traced here: 55.9 us
  starting transfers between devices  19.3 us (34%)
  waiting for transfers between devices  17.5 us (31%)
  Pallas kernels  17 us (30%)
  local copies, waits for them, and re-layouts  1.38 us (2%)
  between operations  0.72 us (1%)
    pallas_call x3, Pallas kernels, call(): pl.pallas_call(kernel, out_shape=outs, in_specs=in_specs, out_specs=[pl.B...  15.2 us
    ppermute x4, waiting for transfers between devices, per_device(): gram = gram + lax.ppermute(gram, AXES, pairs)  14.5 us
    ppermute x4, starting transfers between devices, per_device(): gram = gram + lax.ppermute(gram, AXES, pairs)  10.4 us
    ppermute x3, starting transfers between devices, swap(): lax.ppermute(value, AXES, [(i, i ^ mask) for i in range(device_count)])  8.27 us
    ppermute x3, waiting for transfers between devices, swap(): lax.ppermute(value, AXES, [(i, i ^ mask) for i in range(device_count)])  3.01 us
    pallas_call x1, Pallas kernels, per_device(): pl.pallas_call(functools.partial(scale_kernel, reach=reach, tile=tile), o...  1.81 us
    unnamed x4, local copies, waits for them, and re-layouts  1.38 us
  transfers between devices with their start and end apart: 8, of which 7 were waited for; matrix products, arithmetic and copies ran while one was open for 0% of the time, Pallas kernels for 7%

profile of v2, /device:TPU:0, one launch (start us, length us, event | category | flops | bytes accessed | tf_op | source)
XLA Modules:
  0.0 55.9 jit_solution(515623385032308847)
XLA Ops:
  0.6 1.8 %shard_map.59 = (bf16[1024,256]{1,0:T(8,128)(2,1)S(1)}, bf16[1024,256]{1,0:T(8,128)(2,1)S(1)}) custom-call(s32[1]{0:T(128)} %bitcast.odd_ref, f32[16,128]{1,0:T(8,128)} %bitcast.2, bf16[2048,256]{1,0:T(8,128)(2,1)} %sketch_ref.1), custom_call_target="tpu_custom_call" | custom-call | flops 1 | bytes 1 | tf_op jit(solution)/shard_map/pallas_call | solution.py:309
  2.5 0.5 collective-permute-start
  3.0 0.7 %collective-permute-start.1 = (bf16[1024,256]{1,0:T(8,128)(2,1)S(1)}, bf16[1024,256]{1,0:T(8,128)(2,1)S(1)}, u32[]{:S(2)}, u32[]{:S(2)}) collective-permute-start(bf16[1024,256]{1,0:T(8,128)(2,1)S(1)} %get-tuple-element.14.outer_ref), channel_id=1, source_target_pairs={{1,2},{2,1},{3,4},{4,3},{5,6},{6,5},{7,8},{8,7},{9,10},{10,9},{11,... | collective-permute-start | bytes 1572872 | tf_op jit(solution)/shard_map/ppermute | solution.py:337
  3.7 0.8 %collective-permute-done.halo_ref = bf16[1024,256]{1,0:T(8,128)(2,1)S(1)} collective-permute-done((bf16[1024,256]{1,0:T(8,128)(2,1)S(1)}, bf16[1024,256]{1,0:T(8,128)(2,1)S(1)}, u32[]{:S(2)}, u32[]{:S(2)}) %collective-permute-start) | collective-permute-done | bytes 524320 | tf_op jit(solution)/shard_map/ppermute | solution.py:332
  4.5 0.0 copy-start
  4.5 0.7 %copy-done = s32[8,9]{1,0:T(8,128)S(1)} copy-done((s32[8,9]{1,0:T(8,128)S(1)}, s32[8,9]{1,0:T(8,128)}, u32[]{:S(2)}) %copy-start) | copy-done | bytes 312
  5.2 0.0 copy-start.1
  5.2 0.7 %copy-done.1 = f32[2048]{0:T(1024)S(1)} copy-done((f32[2048]{0:T(1024)S(1)}, f32[2048]{0:T(1024)}, u32[]{:S(2)}) %copy-start.1) | copy-done | bytes 8216
  5.9 3.9 %shard_map.60 = (f32[1024,256]{1,0:T(8,128)S(1)}, f32[1024,128]{1,0:T(8,128)S(1)}, bf16[256,1024]{1,0:T(8,128)(2,1)S(1)}, bf16[1024,256]{1,0:T(8,128)(2,1)S(1)},...) custom-call(s32[1]{0:T(128)} %bitcast.odd_ref, s32[8,9]{1,0:T(8,128)S(1)} %copy-done, ...), custom_call_target="tpu_custom_call" | custom-call | flops 1 | bytes 1 | tf_op jit(solution)/shard_map/pallas_call | solution.py:286
  9.8 0.0 collective-permute-done.1.halo_ref
  9.8 1.6 %shard_map.61 = (bf16[1024,256]{1,0:T(8,128)(2,1)S(1)}, bf16[1024,256]{1,0:T(8,128)(2,1)S(1)}, f32[72,256]{1,0:T(8,128)S(1)}, f32[72,256]{1,0:T(8,128)S(1)}) custom-call(s32[1]{0:T(128)} %bitcast.odd_ref, s32[8,9]{1,0:T(8,128)S(1)} %copy-done, bf16[256,1024]{1,0:T(8,128)(2,1)S(1)} %get-tuple-element.16.lag_ref, f32[1024,128]{1,0:T(8,128)S(1)} %get-tuple-element.17.scale_ref, ...), custom_call_target="tpu_custom_call" | custom-call | flops 1 | bytes 1 | tf_op jit(solution)/shard_map/pallas_call | solution.py:286
  11.5 7.7 %collective-permute-start.2 = (f32[72,256]{1,0:T(8,128)S(1)}, f32[72,256]{1,0:T(8,128)S(1)}, u32[]{:S(2)}, u32[]{:S(2)}) collective-permute-start(f32[72,256]{1,0:T(8,128)S(1)} %get-tuple-element.21), channel_id=1, source_target_pairs={{0,1},{1,0},{2,3},{3,2},{4,5},{5,4},{6,7},{7,6},{8,9},{9,8},{10,11... | collective-permute-start | bytes 221192 | tf_op jit(solution)/shard_map/ppermute | solution.py:332
  19.2 0.9 %collective-permute-done.2 = f32[72,256]{1,0:T(8,128)S(1)} collective-permute-done((f32[72,256]{1,0:T(8,128)S(1)}, f32[72,256]{1,0:T(8,128)S(1)}, u32[]{:S(2)}, u32[]{:S(2)}) %collective-permute-start.2) | collective-permute-done | bytes 73760 | tf_op jit(solution)/shard_map/ppermute | solution.py:332
  20.1 7.2 %collective-permute-start.3 = (f32[72,256]{1,0:T(8,128)S(1)}, f32[72,256]{1,0:T(8,128)S(1)}, u32[]{:S(2)}, u32[]{:S(2)}) collective-permute-start(f32[72,256]{1,0:T(8,128)S(1)} %add.24), channel_id=1, source_target_pairs={{0,8},{1,3},{2,10},{3,1},{4,12},{5,7},{6,14},{7,5},{8,0},{9,11},{1... | collective-permute-start | bytes 221192 | tf_op jit(solution)/shard_map/ppermute | solution.py:376
  27.3 2.3 %collective-permute-done.3 = f32[72,256]{1,0:T(8,128)S(1)} collective-permute-done((f32[72,256]{1,0:T(8,128)S(1)}, f32[72,256]{1,0:T(8,128)S(1)}, u32[]{:S(2)}, u32[]{:S(2)}) %collective-permute-start.3) | collective-permute-done | bytes 73760 | tf_op jit(solution)/shard_map/ppermute | solution.py:376
  29.6 3.0 %collective-permute-start.4 = (f32[72,256]{1,0:T(8,128)S(1)}, f32[72,256]{1,0:T(8,128)S(1)}, u32[]{:S(2)}, u32[]{:S(2)}) collective-permute-start(f32[72,256]{1,0:T(8,128)S(1)} %add.25), channel_id=1, source_target_pairs={{0,16},{1,5},{2,18},{3,7},{4,20},{5,1},{6,22},{7,3},{8,24},{9,13},... | collective-permute-start | bytes 221192 | tf_op jit(solution)/shard_map/ppermute | solution.py:376
  32.6 2.3 %collective-permute-done.4 = f32[72,256]{1,0:T(8,128)S(1)} collective-permute-done((f32[72,256]{1,0:T(8,128)S(1)}, f32[72,256]{1,0:T(8,128)S(1)}, u32[]{:S(2)}, u32[]{:S(2)}) %collective-permute-start.4) | collective-permute-done | bytes 73760 | tf_op jit(solution)/shard_map/ppermute | solution.py:376
  35.0 0.1 collective-permute-start.5
  35.1 4.3 %collective-permute-done.5 = f32[72,256]{1,0:T(8,128)S(1)} collective-permute-done((f32[72,256]{1,0:T(8,128)S(1)}, f32[72,256]{1,0:T(8,128)S(1)}, u32[]{:S(2)}, u32[]{:S(2)}) %collective-permute-start.5) | collective-permute-done | bytes 73760 | tf_op jit(solution)/shard_map/ppermute | solution.py:376
  39.4 0.1 collective-permute-start.6
  39.5 5.5 %collective-permute-done.6 = f32[72,256]{1,0:T(8,128)S(1)} collective-permute-done((f32[72,256]{1,0:T(8,128)S(1)}, f32[72,256]{1,0:T(8,128)S(1)}, u32[]{:S(2)}, u32[]{:S(2)}) %collective-permute-start.6) | collective-permute-done | bytes 73760 | tf_op jit(solution)/shard_map/ppermute | solution.py:376
  45.0 0.1 collective-permute-start.7
  45.1 1.3 %collective-permute-done.7.other_ref = f32[72,256]{1,0:T(8,128)S(1)} collective-permute-done((f32[72,256]{1,0:T(8,128)S(1)}, f32[72,256]{1,0:T(8,128)S(1)}, u32[]{:S(2)}, u32[]{:S(2)}) %collective-permute-start.7) | collective-permute-done | bytes 73760 | tf_op jit(solution)/shard_map/ppermute | solution.py:332
  46.3 9.6 %shard_map.62 = (f32[2048,256]{1,0:T(8,128)}, f32[256,256]{1,0:T(8,128)}) custom-call(s32[1]{0:T(128)} %bitcast.odd_ref, s32[8,9]{1,0:T(8,128)S(1)} %copy-done, f32[72,256]{1,0:T(8,128)S(1)} %add.28.mine_ref, f32[72,256]{1,0:T(8,128)S(1)} %collective-permute-done.7.other_ref, bf16[1024,256]{1,0:T(8,128)(2,1)S(1)} %get-tuple-element.22.far_high_ref, ...), custom_call_target="tpu_custom_call" | custom-call | flops 1 | bytes 1 | tf_op jit(solution)/shard_map/pallas_call | solution.py:286
  (5 shorter events, 0.1 us)
Async XLA Ops:
  2.5 2.1 %collective-permute-start = (bf16[1024,256]{1,0:T(8,128)(2,1)S(1)}, bf16[1024,256]{1,0:T(8,128)(2,1)S(1)}, u32[]{:S(2)}, u32[]{:S(2)}) collective-permute-start(bf16[1024,256]{1,0:T(8,128)(2,1)S(1)} %get-tuple-element.15.inner_ref), channel_id=1, source_target_pairs={{0,1},{1,0},{2,3},{3,2},{4,5},{5,4},{6,7},{7,6},{8,9},{9,8},{10,11... | collective-permute-start | bytes 1572872 | tf_op jit(solution)/shard_map/ppermute | solution.py:332
  3.0 6.9 %collective-permute-start.1 = (bf16[1024,256]{1,0:T(8,128)(2,1)S(1)}, bf16[1024,256]{1,0:T(8,128)(2,1)S(1)}, u32[]{:S(2)}, u32[]{:S(2)}) collective-permute-start(bf16[1024,256]{1,0:T(8,128)(2,1)S(1)} %get-tuple-element.14.outer_ref), channel_id=1, source_target_pairs={{1,2},{2,1},{3,4},{4,3},{5,6},{6,5},{7,8},{8,7},{9,10},{10,9},{11,... | collective-permute-start | bytes 1572872 | tf_op jit(solution)/shard_map/ppermute | solution.py:337
  4.5 0.7 %copy-start = (s32[8,9]{1,0:T(8,128)S(1)}, s32[8,9]{1,0:T(8,128)}, u32[]{:S(2)}) copy-start(s32[8,9]{1,0:T(8,128)} %cols_ref.5) | copy-start | bytes 868
  5.2 0.7 %copy-start.1 = (f32[2048]{0:T(1024)S(1)}, f32[2048]{0:T(1024)}, u32[]{:S(2)}) copy-start(f32[2048]{0:T(1024)} %param.5) | copy-start | bytes 24580
  11.5 8.6 %collective-permute-start.2 = (f32[72,256]{1,0:T(8,128)S(1)}, f32[72,256]{1,0:T(8,128)S(1)}, u32[]{:S(2)}, u32[]{:S(2)}) collective-permute-start(f32[72,256]{1,0:T(8,128)S(1)} %get-tuple-element.21), channel_id=1, source_target_pairs={{0,1},{1,0},{2,3},{3,2},{4,5},{5,4},{6,7},{7,6},{8,9},{9,8},{10,11... | collective-permute-start | bytes 221192 | tf_op jit(solution)/shard_map/ppermute | solution.py:332
  20.1 9.5 %collective-permute-start.3 = (f32[72,256]{1,0:T(8,128)S(1)}, f32[72,256]{1,0:T(8,128)S(1)}, u32[]{:S(2)}, u32[]{:S(2)}) collective-permute-start(f32[72,256]{1,0:T(8,128)S(1)} %add.24), channel_id=1, source_target_pairs={{0,8},{1,3},{2,10},{3,1},{4,12},{5,7},{6,14},{7,5},{8,0},{9,11},{1... | collective-permute-start | bytes 221192 | tf_op jit(solution)/shard_map/ppermute | solution.py:376
  29.6 5.3 %collective-permute-start.4 = (f32[72,256]{1,0:T(8,128)S(1)}, f32[72,256]{1,0:T(8,128)S(1)}, u32[]{:S(2)}, u32[]{:S(2)}) collective-permute-start(f32[72,256]{1,0:T(8,128)S(1)} %add.25), channel_id=1, source_target_pairs={{0,16},{1,5},{2,18},{3,7},{4,20},{5,1},{6,22},{7,3},{8,24},{9,13},... | collective-permute-start | bytes 221192 | tf_op jit(solution)/shard_map/ppermute | solution.py:376
  35.0 4.4 %collective-permute-start.5 = (f32[72,256]{1,0:T(8,128)S(1)}, f32[72,256]{1,0:T(8,128)S(1)}, u32[]{:S(2)}, u32[]{:S(2)}) collective-permute-start(f32[72,256]{1,0:T(8,128)S(1)} %add.26), channel_id=1, source_target_pairs={{0,2},{1,9},{2,0},{3,11},{4,6},{5,13},{6,4},{7,15},{8,10},{9,1},{1... | collective-permute-start | bytes 221192 | tf_op jit(solution)/shard_map/ppermute | solution.py:376
  39.4 5.5 %collective-permute-start.6 = (f32[72,256]{1,0:T(8,128)S(1)}, f32[72,256]{1,0:T(8,128)S(1)}, u32[]{:S(2)}, u32[]{:S(2)}) collective-permute-start(f32[72,256]{1,0:T(8,128)S(1)} %add.27), channel_id=1, source_target_pairs={{0,4},{1,17},{2,6},{3,19},{4,0},{5,21},{6,2},{7,23},{8,12},{9,25},... | collective-permute-start | bytes 221192 | tf_op jit(solution)/shard_map/ppermute | solution.py:376
  45.0 1.3 %collective-permute-start.7 = (f32[72,256]{1,0:T(8,128)S(1)}, f32[72,256]{1,0:T(8,128)S(1)}, u32[]{:S(2)}, u32[]{:S(2)}) collective-permute-start(f32[72,256]{1,0:T(8,128)S(1)} %add.28.mine_ref), channel_id=1, source_target_pairs={{0,1},{1,0},{2,3},{3,2},{4,5},{5,4},{6,7},{7,6},{8,9},{9,8},{10,11... | collective-permute-start | bytes 221192 | tf_op jit(solution)/shard_map/ppermute | solution.py:332

commit v3 on v2

--- a/solution.py
+++ b/solution.py
@@ -197,7 +197,7 @@
     return jnp.broadcast_to(value, (SUBLANES, LANES))
 
 
-def eliminate(work_ref, factor_ref, inverse_ref, panel=32):
+def eliminate(work_ref, factor_ref, inverse_ref, panel=32, held=16):
     size = work_ref.shape[0]
     groups = panel // SUBLANES
     sublane = lax.broadcasted_iota(jnp.int32, (SUBLANES, LANES), 0)
@@ -216,27 +216,39 @@
             [block[i : i + SUBLANES, c : c + LANES] for c in chunks] + [identity[i : i + SUBLANES]]
             for i in range(0, panel, SUBLANES)
         ]
-        corner = [natural[g][chunk // LANES] for g in range(groups)]
-        columns = [
-            {g: spread(corner[g][:, offset + k : offset + k + 1]) for g in range(k // SUBLANES, groups)}
-            for k in range(panel)
-        ]
-        for k in range(panel):
-            at, inside = divmod(k, SUBLANES)
-            scale = lax.rsqrt(spread(columns[k][at][inside : inside + 1, :]))
-            lower = {g: columns[k][g] * scale for g in range(at, groups)}
-            for m in range(k + 1, panel):
-                group, place = divmod(m, SUBLANES)
-                factor = spread(lower[group][place : place + 1, :])
-                for g in range(group, groups):
-                    columns[m][g] = columns[m][g] - lower[g] * factor
-            below = dict(lower)
-            below[at] = jnp.where(sublane > inside, lower[at], 0.0)
-            for c in range(len(natural[0])):
-                pivot = spread(natural[at][c][inside : inside + 1, :]) * scale
-                for g in range(at, groups):
-                    natural[g][c] = natural[g][c] - below[g] * pivot
-                natural[at][c] = jnp.where(sublane == inside, pivot, natural[at][c])
+        for begin in range(0, panel, held):
+            end = begin + held
+            columns = {
+                k: {
+                    g: spread(natural[g][chunk // LANES][:, offset + k : offset + k + 1])
+                    for g in range(k // SUBLANES, groups)
+                }
+                for k in range(begin, end)
+            }
+            pivot = None
+            for k in range(begin, end):
+                at, inside = divmod(k, SUBLANES)
+                if pivot is None:
+                    pivot = spread(columns[k][at][inside : inside + 1, :])
+                inverse = 1.0 / pivot
+                scale = lax.rsqrt(pivot)
+                ratio = {g: columns[k][g] * inverse for g in range(at, groups)}
+                if k + 1 < end:
+                    group, place = divmod(k + 1, SUBLANES)
+                    element = spread(columns[k][group][place : place + 1, :])
+                    pivot = spread(columns[k + 1][group][place : place + 1, :]) - element * element * inverse
+                for m in range(k + 1, end):
+                    group, place = divmod(m, SUBLANES)
+                    factor = spread(ratio[group][place : place + 1, :])
+                    for g in range(group, groups):
+                        columns[m][g] = columns[m][g] - columns[k][g] * factor
+                below = dict(ratio)
+                below[at] = jnp.where(sublane > inside, ratio[at], 0.0)
+                for c in range(len(natural[0])):
+                    raw = spread(natural[at][c][inside : inside + 1, :])
+                    for g in range(at, groups):
+                        natural[g][c] = natural[g][c] - below[g] * raw
+                    natural[at][c] = jnp.where(sublane == inside, raw * scale, natural[at][c])
         done = jnp.concatenate([jnp.concatenate(v[:-1], axis=1) for v in natural], axis=0)
         inverse = jnp.concatenate([v[-1] for v in natural], axis=0)
         empty = jnp.zeros((panel, LANES), F32)
@@ -259,7 +271,7 @@
 
 def basis_kernel(
     odd_ref, cols_ref, mine_ref, other_ref, far_high_ref, far_low_ref, near_high_ref, near_low_ref,
-    basis_ref, factor_ref, work_ref, inverse_ref,
+    basis_ref, factor_ref, work_ref, inverse_ref, tiles_ref, sems,
     *, reach, tile,
 ):
     odd = odd_ref[0]
@@ -268,17 +280,24 @@
     eliminate(work_ref, factor_ref, inverse_ref)
     high, low = split2(inverse_ref[...])
     right = jnp.concatenate([high, high, low], axis=1)
+    copies = []
     for line in range(2 * reach):
         high_ref, low_ref = (far_high_ref, far_low_ref) if line < reach else (near_high_ref, near_low_ref)
         rows = slice(line % reach * tile, (line % reach + 1) * tile)
         left = jnp.concatenate([high_ref[rows, :], low_ref[rows, :], high_ref[rows, :]], axis=1)
-        place = pl.multiple_of(own_tile(cols_ref, odd, line, reach) * tile, tile)
-        basis_ref[pl.ds(place, tile), :] = lax.dot_general(
+        tiles_ref[line] = lax.dot_general(
             left, right, (((1,), (1,)), ((), ())), preferred_element_type=F32
         )
-
-
-def call(kernel, outs, scratch, smem_count, operands):
+        place = pl.multiple_of(own_tile(cols_ref, odd, line, reach) * tile, tile)
+        copies.append(
+            pltpu.make_async_copy(tiles_ref.at[line], basis_ref.at[pl.ds(place, tile), :], sems.at[line])
+        )
+        copies[-1].start()
+    for copy in copies:
+        copy.wait()
+
+
+def call(kernel, outs, scratch, smem_count, operands, hbm_outs=0):
     in_specs = [
         pl.BlockSpec(memory_space=pltpu.SMEM if i < smem_count else pltpu.VMEM)
         for i in range(len(operands))
@@ -287,7 +306,9 @@
         kernel,
         out_shape=outs,
         in_specs=in_specs,
-        out_specs=[pl.BlockSpec(memory_space=pltpu.VMEM) for _ in outs],
+        out_specs=[
+            pl.BlockSpec(memory_space=pl.ANY if i < hbm_outs else pltpu.VMEM) for i in range(len(outs))
+        ],
         scratch_shapes=scratch,
         cost_estimate=SMALL_COST,
         compiler_params=pltpu.CompilerParams(vmem_limit_bytes=VMEM_LIMIT),
@@ -369,18 +390,34 @@
         (odd_arg, tile_cols, lag_block, scale, acc, outer_halo, near_gram),
     )
     gram = keep + swap(send, 1)
-    masks = [1 << i for i in range(1, device_count.bit_length() - 1)]
-    middle = len(masks) // 2
-    for even_mask, odd_mask in zip(masks[middle:] + masks[:middle], masks):
-        pairs = [(i, i ^ (odd_mask if i % 2 else even_mask)) for i in range(device_count)]
-        gram = gram + lax.ppermute(gram, AXES, pairs)
+    bits = [1 << i for i in range(1, device_count.bit_length() - 1)]
+    if len(bits) % 2:
+        gram = gram + swap(gram, bits.pop())
+    rounds = [(bits[i], bits[i + 1]) for i in range(0, len(bits), 2)]
+    middle = len(rounds) // 2
+    for even, odd_one in zip(rounds[middle:] + rounds[:middle], rounds):
+        near, across, both = (
+            lax.ppermute(
+                gram, AXES, [(i, i ^ (odd_mask if i % 2 else even_mask)) for i in range(device_count)]
+            )
+            for even_mask, odd_mask in zip(
+                (even[0], even[1], even[0] | even[1]), (odd_one[0], odd_one[1], odd_one[0] | odd_one[1])
+            )
+        )
+        gram = (gram + near) + (across + both)
     other = swap(gram, 1)
     basis, factor = call(
         functools.partial(basis_kernel, reach=reach, tile=tile),
         [shape(row_count, width, F32), shape(width, width, F32)],
-        [pltpu.VMEM((width, width), F32), pltpu.VMEM((width, width), F32)],
+        [
+            pltpu.VMEM((width, width), F32),
+            pltpu.VMEM((width, width), F32),
+            pltpu.VMEM((2 * reach, tile, width), F32),
+            pltpu.SemaphoreType.DMA((2 * reach,)),
+        ],
         2,
         (odd_arg, tile_cols, gram, other, far_high, far_low, near_high, near_low),
+        1,
     )
     return basis, factor
 

time: 56.2 us -> 52.6 us (0.936)
  waiting for transfers between devices: 17.5 us -> 10.7 us
  starting transfers between devices: 19.3 us -> 23 us
    ppermute x4 -> x6, waiting for transfers between devices: 14.5 us -> 7.69 us  [per_device(): lax.ppermute(gram, AXES, [(i, i ^ (odd_mask if i % 2 else even_mask)) for...]
    ppermute x4 -> x6, starting transfers between devices: 10.4 us -> 14 us  [per_device(): lax.ppermute(gram, AXES, [(i, i ^ (odd_mask if i % 2 else even_mask)) for...]
  transfers between devices with their start and end apart: 8 -> 10, of which waited for: 7 -> 7; matrix products, arithmetic and copies ran while one was open for 0% -> 0% of each run, Pallas kernels for 7% -> 7%
where the time goes in v3:
time: 52.6 us; the launch traced here: 52.3 us
  starting transfers between devices  23 us (44%)
  Pallas kernels  16.5 us (31%)
  waiting for transfers between devices  10.7 us (20%)
  local copies, waits for them, and re-layouts  1.38 us (3%)
  between operations  0.71 us (1%)
    pallas_call x3, Pallas kernels, call(): pl.pallas_call(kernel, out_shape=outs, in_specs=in_specs, out_specs=[pl.B...  14.6 us
    ppermute x6, starting transfers between devices, per_device(): lax.ppermute(gram, AXES, [(i, i ^ (odd_mask if i % 2 else even_mask)) for...  14 us
    ppermute x3, starting transfers between devices, swap(): lax.ppermute(value, AXES, [(i, i ^ mask) for i in range(device_count)])  8.27 us
    ppermute x6, waiting for transfers between devices, per_device(): lax.ppermute(gram, AXES, [(i, i ^ (odd_mask if i % 2 else even_mask)) for...  7.69 us
    ppermute x3, waiting for transfers between devices, swap(): lax.ppermute(value, AXES, [(i, i ^ mask) for i in range(device_count)])  3.01 us
    pallas_call x1, Pallas kernels, per_device(): pl.pallas_call(functools.partial(scale_kernel, reach=reach, tile=tile), o...  1.81 us
    unnamed x4, local copies, waits for them, and re-layouts  1.38 us
  transfers between devices with their start and end apart: 10, of which 7 were waited for; matrix products, arithmetic and copies ran while one was open for 0% of the time, Pallas kernels for 7%

profile of v3, /device:TPU:0, one launch (start us, length us, event | category | flops | bytes accessed | tf_op | source)
XLA Modules:
  0.0 52.3 jit_solution(275510101367024774)
XLA Ops:
  0.6 1.8 %shard_map.59 = (bf16[1024,256]{1,0:T(8,128)(2,1)S(1)}, bf16[1024,256]{1,0:T(8,128)(2,1)S(1)}) custom-call(s32[1]{0:T(128)} %bitcast.odd_ref, f32[16,128]{1,0:T(8,128)} %bitcast.2, bf16[2048,256]{1,0:T(8,128)(2,1)} %sketch_ref.1), custom_call_target="tpu_custom_call" | custom-call | flops 1 | bytes 1 | tf_op jit(solution)/shard_map/pallas_call | solution.py:330
  2.5 0.5 collective-permute-start
  3.0 0.7 %collective-permute-start.1 = (bf16[1024,256]{1,0:T(8,128)(2,1)S(1)}, bf16[1024,256]{1,0:T(8,128)(2,1)S(1)}, u32[]{:S(2)}, u32[]{:S(2)}) collective-permute-start(bf16[1024,256]{1,0:T(8,128)(2,1)S(1)} %get-tuple-element.14.outer_ref), channel_id=1, source_target_pairs={{1,2},{2,1},{3,4},{4,3},{5,6},{6,5},{7,8},{8,7},{9,10},{10,9},{11,... | collective-permute-start | bytes 1572872 | tf_op jit(solution)/shard_map/ppermute | solution.py:358
  3.7 0.8 %collective-permute-done.halo_ref = bf16[1024,256]{1,0:T(8,128)(2,1)S(1)} collective-permute-done((bf16[1024,256]{1,0:T(8,128)(2,1)S(1)}, bf16[1024,256]{1,0:T(8,128)(2,1)S(1)}, u32[]{:S(2)}, u32[]{:S(2)}) %collective-permute-start) | collective-permute-done | bytes 524320 | tf_op jit(solution)/shard_map/ppermute | solution.py:353
  4.5 0.0 copy-start
  4.5 0.7 %copy-done = s32[8,9]{1,0:T(8,128)S(1)} copy-done((s32[8,9]{1,0:T(8,128)S(1)}, s32[8,9]{1,0:T(8,128)}, u32[]{:S(2)}) %copy-start) | copy-done | bytes 312
  5.2 0.0 copy-start.1
  5.2 0.7 %copy-done.1 = f32[2048]{0:T(1024)S(1)} copy-done((f32[2048]{0:T(1024)S(1)}, f32[2048]{0:T(1024)}, u32[]{:S(2)}) %copy-start.1) | copy-done | bytes 8216
  5.9 3.9 %shard_map.60 = (f32[1024,256]{1,0:T(8,128)S(1)}, f32[1024,128]{1,0:T(8,128)S(1)}, bf16[256,1024]{1,0:T(8,128)(2,1)S(1)}, bf16[1024,256]{1,0:T(8,128)(2,1)S(1)},...) custom-call(s32[1]{0:T(128)} %bitcast.odd_ref, s32[8,9]{1,0:T(8,128)S(1)} %copy-done, ...), custom_call_target="tpu_custom_call" | custom-call | flops 1 | bytes 1 | tf_op jit(solution)/shard_map/pallas_call | solution.py:305
  9.8 0.0 collective-permute-done.1.halo_ref
  9.8 1.6 %shard_map.61 = (bf16[1024,256]{1,0:T(8,128)(2,1)S(1)}, bf16[1024,256]{1,0:T(8,128)(2,1)S(1)}, f32[72,256]{1,0:T(8,128)S(1)}, f32[72,256]{1,0:T(8,128)S(1)}) custom-call(s32[1]{0:T(128)} %bitcast.odd_ref, s32[8,9]{1,0:T(8,128)S(1)} %copy-done, bf16[256,1024]{1,0:T(8,128)(2,1)S(1)} %get-tuple-element.16.lag_ref, f32[1024,128]{1,0:T(8,128)S(1)} %get-tuple-element.17.scale_ref, ...), custom_call_target="tpu_custom_call" | custom-call | flops 1 | bytes 1 | tf_op jit(solution)/shard_map/pallas_call | solution.py:305
  11.5 7.7 %collective-permute-start.2 = (f32[72,256]{1,0:T(8,128)S(1)}, f32[72,256]{1,0:T(8,128)S(1)}, u32[]{:S(2)}, u32[]{:S(2)}) collective-permute-start(f32[72,256]{1,0:T(8,128)S(1)} %get-tuple-element.21), channel_id=1, source_target_pairs={{0,1},{1,0},{2,3},{3,2},{4,5},{5,4},{6,7},{7,6},{8,9},{9,8},{10,11... | collective-permute-start | bytes 221192 | tf_op jit(solution)/shard_map/ppermute | solution.py:353
  19.2 0.9 %collective-permute-done.2 = f32[72,256]{1,0:T(8,128)S(1)} collective-permute-done((f32[72,256]{1,0:T(8,128)S(1)}, f32[72,256]{1,0:T(8,128)S(1)}, u32[]{:S(2)}, u32[]{:S(2)}) %collective-permute-start.2) | collective-permute-done | bytes 73760 | tf_op jit(solution)/shard_map/ppermute | solution.py:353
  20.1 7.2 %collective-permute-start.3 = (f32[72,256]{1,0:T(8,128)S(1)}, f32[72,256]{1,0:T(8,128)S(1)}, u32[]{:S(2)}, u32[]{:S(2)}) collective-permute-start(f32[72,256]{1,0:T(8,128)S(1)} %add.30), channel_id=1, source_target_pairs={{0,8},{1,3},{2,10},{3,1},{4,12},{5,7},{6,14},{7,5},{8,0},{9,11},{1... | collective-permute-start | bytes 221192 | tf_op jit(solution)/shard_map/ppermute | solution.py:400
  27.3 1.5 %collective-permute-start.4 = (f32[72,256]{1,0:T(8,128)S(1)}, f32[72,256]{1,0:T(8,128)S(1)}, u32[]{:S(2)}, u32[]{:S(2)}) collective-permute-start(f32[72,256]{1,0:T(8,128)S(1)} %add.30), channel_id=1, source_target_pairs={{0,16},{1,5},{2,18},{3,7},{4,20},{5,1},{6,22},{7,3},{8,24},{9,13},... | collective-permute-start | bytes 221192 | tf_op jit(solution)/shard_map/ppermute | solution.py:400
  28.8 0.9 %collective-permute-start.5 = (f32[72,256]{1,0:T(8,128)S(1)}, f32[72,256]{1,0:T(8,128)S(1)}, u32[]{:S(2)}, u32[]{:S(2)}) collective-permute-start(f32[72,256]{1,0:T(8,128)S(1)} %add.30), channel_id=1, source_target_pairs={{0,24},{1,7},{2,26},{3,5},{4,28},{5,3},{6,30},{7,1},{8,16},{9,15},... | collective-permute-start | bytes 221192 | tf_op jit(solution)/shard_map/ppermute | solution.py:400
  29.7 0.0 collective-permute-done.3
  29.7 2.0 %collective-permute-done.4 = f32[72,256]{1,0:T(8,128)S(1)} collective-permute-done((f32[72,256]{1,0:T(8,128)S(1)}, f32[72,256]{1,0:T(8,128)S(1)}, u32[]{:S(2)}, u32[]{:S(2)}) %collective-permute-start.4) | collective-permute-done | bytes 73760 | tf_op jit(solution)/shard_map/ppermute | solution.py:400
  31.6 2.4 %collective-permute-done.5 = f32[72,256]{1,0:T(8,128)S(1)} collective-permute-done((f32[72,256]{1,0:T(8,128)S(1)}, f32[72,256]{1,0:T(8,128)S(1)}, u32[]{:S(2)}, u32[]{:S(2)}) %collective-permute-start.5) | collective-permute-done | bytes 73760 | tf_op jit(solution)/shard_map/ppermute | solution.py:400
  34.1 0.1 collective-permute-start.6
  34.2 1.5 %collective-permute-start.7 = (f32[72,256]{1,0:T(8,128)S(1)}, f32[72,256]{1,0:T(8,128)S(1)}, u32[]{:S(2)}, u32[]{:S(2)}) collective-permute-start(f32[72,256]{1,0:T(8,128)S(1)} %add_add_fusion.1), channel_id=1, source_target_pairs={{0,4},{1,17},{2,6},{3,19},{4,0},{5,21},{6,2},{7,23},{8,12},{9,25},... | collective-permute-start | bytes 221192 | tf_op jit(solution)/shard_map/ppermute | solution.py:400
  35.7 2.9 %collective-permute-start.8 = (f32[72,256]{1,0:T(8,128)S(1)}, f32[72,256]{1,0:T(8,128)S(1)}, u32[]{:S(2)}, u32[]{:S(2)}) collective-permute-start(f32[72,256]{1,0:T(8,128)S(1)} %add_add_fusion.1), channel_id=1, source_target_pairs={{0,6},{1,25},{2,4},{3,27},{4,2},{5,29},{6,0},{7,31},{8,14},{9,17},... | collective-permute-start | bytes 221192 | tf_op jit(solution)/shard_map/ppermute | solution.py:400
  38.5 0.0 collective-permute-done.6
  38.5 0.9 %collective-permute-done.7 = f32[72,256]{1,0:T(8,128)S(1)} collective-permute-done((f32[72,256]{1,0:T(8,128)S(1)}, f32[72,256]{1,0:T(8,128)S(1)}, u32[]{:S(2)}, u32[]{:S(2)}) %collective-permute-start.7) | collective-permute-done | bytes 73760 | tf_op jit(solution)/shard_map/ppermute | solution.py:400
  39.5 2.4 %collective-permute-done.8 = f32[72,256]{1,0:T(8,128)S(1)} collective-permute-done((f32[72,256]{1,0:T(8,128)S(1)}, f32[72,256]{1,0:T(8,128)S(1)}, u32[]{:S(2)}, u32[]{:S(2)}) %collective-permute-start.8) | collective-permute-done | bytes 73760 | tf_op jit(solution)/shard_map/ppermute | solution.py:400
  41.9 0.1 collective-permute-start.9
  41.9 1.3 %collective-permute-done.9.other_ref = f32[72,256]{1,0:T(8,128)S(1)} collective-permute-done((f32[72,256]{1,0:T(8,128)S(1)}, f32[72,256]{1,0:T(8,128)S(1)}, u32[]{:S(2)}, u32[]{:S(2)}) %collective-permute-start.9) | collective-permute-done | bytes 73760 | tf_op jit(solution)/shard_map/ppermute | solution.py:353
  43.2 9.1 %shard_map.62 = (f32[2048,256]{1,0:T(8,128)}, f32[256,256]{1,0:T(8,128)}) custom-call(s32[1]{0:T(128)} %bitcast.odd_ref, s32[8,9]{1,0:T(8,128)S(1)} %copy-done, f32[72,256]{1,0:T(8,128)S(1)} %add_add_fusion.mine_ref, f32[72,256]{1,0:T(8,128)S(1)} %collective-permute-done.9.other_ref, bf16[1024,256]{1,0:T(8,128)(2,1)S(1)} %get-tuple-element.22.far_high_ref, ...), custom_call_target="tpu_custom_call" | custom-call | flops 1 | bytes 1 | tf_op jit(solution)/shard_map/pallas_call | solution.py:305
  (3 shorter events, 0.1 us)
Async XLA Ops:
  2.5 2.1 %collective-permute-start = (bf16[1024,256]{1,0:T(8,128)(2,1)S(1)}, bf16[1024,256]{1,0:T(8,128)(2,1)S(1)}, u32[]{:S(2)}, u32[]{:S(2)}) collective-permute-start(bf16[1024,256]{1,0:T(8,128)(2,1)S(1)} %get-tuple-element.15.inner_ref), channel_id=1, source_target_pairs={{0,1},{1,0},{2,3},{3,2},{4,5},{5,4},{6,7},{7,6},{8,9},{9,8},{10,11... | collective-permute-start | bytes 1572872 | tf_op jit(solution)/shard_map/ppermute | solution.py:353
  3.0 6.9 %collective-permute-start.1 = (bf16[1024,256]{1,0:T(8,128)(2,1)S(1)}, bf16[1024,256]{1,0:T(8,128)(2,1)S(1)}, u32[]{:S(2)}, u32[]{:S(2)}) collective-permute-start(bf16[1024,256]{1,0:T(8,128)(2,1)S(1)} %get-tuple-element.14.outer_ref), channel_id=1, source_target_pairs={{1,2},{2,1},{3,4},{4,3},{5,6},{6,5},{7,8},{8,7},{9,10},{10,9},{11,... | collective-permute-start | bytes 1572872 | tf_op jit(solution)/shard_map/ppermute | solution.py:358
  4.5 0.7 %copy-start = (s32[8,9]{1,0:T(8,128)S(1)}, s32[8,9]{1,0:T(8,128)}, u32[]{:S(2)}) copy-start(s32[8,9]{1,0:T(8,128)} %cols_ref.5) | copy-start | bytes 868
  5.2 0.7 %copy-start.1 = (f32[2048]{0:T(1024)S(1)}, f32[2048]{0:T(1024)}, u32[]{:S(2)}) copy-start(f32[2048]{0:T(1024)} %param.5) | copy-start | bytes 24580
  11.5 8.6 %collective-permute-start.2 = (f32[72,256]{1,0:T(8,128)S(1)}, f32[72,256]{1,0:T(8,128)S(1)}, u32[]{:S(2)}, u32[]{:S(2)}) collective-permute-start(f32[72,256]{1,0:T(8,128)S(1)} %get-tuple-element.21), channel_id=1, source_target_pairs={{0,1},{1,0},{2,3},{3,2},{4,5},{5,4},{6,7},{7,6},{8,9},{9,8},{10,11... | collective-permute-start | bytes 221192 | tf_op jit(solution)/shard_map/ppermute | solution.py:353
  20.1 9.6 %collective-permute-start.3 = (f32[72,256]{1,0:T(8,128)S(1)}, f32[72,256]{1,0:T(8,128)S(1)}, u32[]{:S(2)}, u32[]{:S(2)}) collective-permute-start(f32[72,256]{1,0:T(8,128)S(1)} %add.30), channel_id=1, source_target_pairs={{0,8},{1,3},{2,10},{3,1},{4,12},{5,7},{6,14},{7,5},{8,0},{9,11},{1... | collective-permute-start | bytes 221192 | tf_op jit(solution)/shard_map/ppermute | solution.py:400
  27.3 4.4 %collective-permute-start.4 = (f32[72,256]{1,0:T(8,128)S(1)}, f32[72,256]{1,0:T(8,128)S(1)}, u32[]{:S(2)}, u32[]{:S(2)}) collective-permute-start(f32[72,256]{1,0:T(8,128)S(1)} %add.30), channel_id=1, source_target_pairs={{0,16},{1,5},{2,18},{3,7},{4,20},{5,1},{6,22},{7,3},{8,24},{9,13},... | collective-permute-start | bytes 221192 | tf_op jit(solution)/shard_map/ppermute | solution.py:400
  28.8 5.3 %collective-permute-start.5 = (f32[72,256]{1,0:T(8,128)S(1)}, f32[72,256]{1,0:T(8,128)S(1)}, u32[]{:S(2)}, u32[]{:S(2)}) collective-permute-start(f32[72,256]{1,0:T(8,128)S(1)} %add.30), channel_id=1, source_target_pairs={{0,24},{1,7},{2,26},{3,5},{4,28},{5,3},{6,30},{7,1},{8,16},{9,15},... | collective-permute-start | bytes 221192 | tf_op jit(solution)/shard_map/ppermute | solution.py:400
  34.1 4.5 %collective-permute-start.6 = (f32[72,256]{1,0:T(8,128)S(1)}, f32[72,256]{1,0:T(8,128)S(1)}, u32[]{:S(2)}, u32[]{:S(2)}) collective-permute-start(f32[72,256]{1,0:T(8,128)S(1)} %add_add_fusion.1), channel_id=1, source_target_pairs={{0,2},{1,9},{2,0},{3,11},{4,6},{5,13},{6,4},{7,15},{8,10},{9,1},{1... | collective-permute-start | bytes 221192 | tf_op jit(solution)/shard_map/ppermute | solution.py:400
  34.2 5.3 %collective-permute-start.7 = (f32[72,256]{1,0:T(8,128)S(1)}, f32[72,256]{1,0:T(8,128)S(1)}, u32[]{:S(2)}, u32[]{:S(2)}) collective-permute-start(f32[72,256]{1,0:T(8,128)S(1)} %add_add_fusion.1), channel_id=1, source_target_pairs={{0,4},{1,17},{2,6},{3,19},{4,0},{5,21},{6,2},{7,23},{8,12},{9,25},... | collective-permute-start | bytes 221192 | tf_op jit(solution)/shard_map/ppermute | solution.py:400
  35.7 6.2 %collective-permute-start.8 = (f32[72,256]{1,0:T(8,128)S(1)}, f32[72,256]{1,0:T(8,128)S(1)}, u32[]{:S(2)}, u32[]{:S(2)}) collective-permute-start(f32[72,256]{1,0:T(8,128)S(1)} %add_add_fusion.1), channel_id=1, source_target_pairs={{0,6},{1,25},{2,4},{3,27},{4,2},{5,29},{6,0},{7,31},{8,14},{9,17},... | collective-permute-start | bytes 221192 | tf_op jit(solution)/shard_map/ppermute | solution.py:400
  41.9 1.3 %collective-permute-start.9 = (f32[72,256]{1,0:T(8,128)S(1)}, f32[72,256]{1,0:T(8,128)S(1)}, u32[]{:S(2)}, u32[]{:S(2)}) collective-permute-start(f32[72,256]{1,0:T(8,128)S(1)} %add_add_fusion.mine_ref), channel_id=1, source_target_pairs={{0,1},{1,0},{2,3},{3,2},{4,5},{5,4},{6,7},{7,6},{8,9},{9,8},{10,11... | collective-permute-start | bytes 221192 | tf_op jit(solution)/shard_map/ppermute | solution.py:353

commit v4 on v3

--- a/solution.py
+++ b/solution.py
@@ -64,25 +64,23 @@
     return jnp.clip(column - base, 0, reach - 1)
 
 
-def scale_kernel(odd_ref, std_hbm_ref, sketch_ref, outer_ref, inner_ref, std_ref, rows_ref, sems, *, reach, tile):
-    width = outer_ref.shape[1]
-    count = 2 * reach
-    first = jnp.where(odd_ref[0] == 1, reach, 0)
-    order = [(first + i) % count for i in range(count)]
+def scale_kernel(first_ref, std_hbm_ref, sketch_ref, *refs, tile):
+    out_ref, std_ref, rows_ref, sems = refs[-4:]
+    count = out_ref.shape[0] // tile
+    first = first_ref[0]
     copies = [pltpu.make_async_copy(std_hbm_ref, std_ref, sems.at[count])]
-    for i, index in enumerate(order):
-        place = pl.multiple_of(index * tile, tile)
+    for i in range(count):
+        place = pl.multiple_of((first + i) * tile, tile)
         target = rows_ref.at[pl.ds(i * tile, tile), :]
         copies.append(pltpu.make_async_copy(sketch_ref.at[pl.ds(place, tile), :], target, sems.at[i]))
     for copy in copies:
         copy.start()
     copies[0].wait()
-    for i, index in enumerate(order):
-        std = std_column(std_ref, index, tile, width)
+    for i in range(count):
+        std = std_column(std_ref, first + i, tile, out_ref.shape[1])
         copies[i + 1].wait()
-        scaled = (rows_ref[i * tile : (i + 1) * tile, :].astype(F32) * std).astype(BF16)
-        place = i % reach * tile
-        (outer_ref if i < reach else inner_ref)[place : place + tile, :] = scaled
+        rows = slice(i * tile, (i + 1) * tile)
+        out_ref[rows, :] = (rows_ref[rows, :].astype(F32) * std).astype(BF16)
 
 
 def near_kernel(
@@ -271,13 +269,15 @@
 
 def basis_kernel(
     odd_ref, cols_ref, mine_ref, other_ref, far_high_ref, far_low_ref, near_high_ref, near_low_ref,
-    basis_ref, factor_ref, work_ref, inverse_ref, tiles_ref, sems,
+    basis_ref, factor_ref, work_ref, inverse_ref, tiles_ref, held_ref, sems,
     *, reach, tile,
 ):
     odd = odd_ref[0]
     mine, other = mine_ref[...], other_ref[...]
     unpack(jnp.where(odd == 1, other, mine), jnp.where(odd == 1, mine, other), work_ref)
-    eliminate(work_ref, factor_ref, inverse_ref)
+    eliminate(work_ref, held_ref, inverse_ref)
+    factor_copy = pltpu.make_async_copy(held_ref, factor_ref, sems.at[2 * reach])
+    factor_copy.start()
     high, low = split2(inverse_ref[...])
     right = jnp.concatenate([high, high, low], axis=1)
     copies = []
@@ -295,6 +295,7 @@
         copies[-1].start()
     for copy in copies:
         copy.wait()
+    factor_copy.wait()
 
 
 def call(kernel, outs, scratch, smem_count, operands, hbm_outs=0):
@@ -327,27 +328,33 @@
 
     std_rows = marginal_std.reshape(-1, LANES)
 
-    outer, inner = pl.pallas_call(
-        functools.partial(scale_kernel, reach=reach, tile=tile),
-        out_shape=[jax.ShapeDtypeStruct((halo, width), BF16)] * 2,
-        in_specs=[
-            pl.BlockSpec(memory_space=pltpu.SMEM),
-            pl.BlockSpec(memory_space=pltpu.HBM),
-            pl.BlockSpec(memory_space=pltpu.HBM),
-        ],
-        out_specs=[pl.BlockSpec(memory_space=pltpu.VMEM)] * 2,
-        scratch_shapes=[
-            pltpu.VMEM(std_rows.shape, F32),
-            pltpu.VMEM((row_count, width), BF16),
-            pltpu.SemaphoreType.DMA((2 * reach + 1,)),
-        ],
-        cost_estimate=SMALL_COST,
-        compiler_params=pltpu.CompilerParams(vmem_limit_bytes=VMEM_LIMIT),
-    )(
-        odd_arg,
-        pltpu.with_memory_space_constraint(std_rows, pltpu.HBM),
-        pltpu.with_memory_space_constraint(sketch, pltpu.HBM),
-    )
+    def scaled(first, *after):
+        return pl.pallas_call(
+            functools.partial(scale_kernel, tile=tile),
+            out_shape=jax.ShapeDtypeStruct((halo, width), BF16),
+            in_specs=[
+                pl.BlockSpec(memory_space=pltpu.SMEM),
+                pl.BlockSpec(memory_space=pltpu.HBM),
+                pl.BlockSpec(memory_space=pltpu.HBM),
+            ]
+            + [pl.BlockSpec(memory_space=pl.ANY)] * len(after),
+            out_specs=pl.BlockSpec(memory_space=pltpu.VMEM),
+            scratch_shapes=[
+                pltpu.VMEM(std_rows.shape, F32),
+                pltpu.VMEM((halo, width), BF16),
+                pltpu.SemaphoreType.DMA((reach + 1,)),
+            ],
+            cost_estimate=SMALL_COST,
+            compiler_params=pltpu.CompilerParams(vmem_limit_bytes=VMEM_LIMIT),
+        )(
+            first.astype(jnp.int32).reshape(1),
+            pltpu.with_memory_space_constraint(std_rows, pltpu.HBM),
+            pltpu.with_memory_space_constraint(sketch, pltpu.HBM),
+            *after,
+        )
+
+    outer = scaled(jnp.where(odd == 1, reach, 0))
+    inner = scaled(jnp.where(odd == 1, 0, reach), outer)
 
     def swap(value, mask):
         return lax.ppermute(value, AXES, [(i, i ^ mask) for i in range(device_count)])
@@ -356,7 +363,7 @@
     for i in range(1, device_count - 1, 2):
         outer_pairs += [(i, i + 1), (i + 1, i)]
     outer_halo = lax.ppermute(outer, AXES, outer_pairs)
-    inner_halo = swap(inner, 1)
+    inner_halo = jnp.concatenate([swap(inner[: halo // 2], 1), swap(inner[halo // 2 :], 1)], axis=0)
 
     def shape(rows, columns, dtype):
         return jax.ShapeDtypeStruct((rows, columns), dtype)
@@ -413,11 +420,12 @@
             pltpu.VMEM((width, width), F32),
             pltpu.VMEM((width, width), F32),
             pltpu.VMEM((2 * reach, tile, width), F32),
-            pltpu.SemaphoreType.DMA((2 * reach,)),
+            pltpu.VMEM((width, width), F32),
+            pltpu.SemaphoreType.DMA((2 * reach + 1,)),
         ],
         2,
         (odd_arg, tile_cols, gram, other, far_high, far_low, near_high, near_low),
-        1,
+        2,
     )
     return basis, factor
 

time: 52.6 us -> 51.2 us (0.973)
  local copies, waits for them, and re-layouts: 1.38 us -> 0.05 us
  starting transfers between devices: 23 us -> 21.7 us
  waiting for transfers between devices: 10.7 us -> 11.8 us
    unnamed x4, local copies, waits for them, and re-layouts: 1.38 us -> 0.01 us
    pallas_call x1 -> x2, Pallas kernels: 1.81 us -> 2.65 us  [scaled(): pl.pallas_call(functools.partial(scale_kernel, tile=tile), out_shape=jax....]
    ppermute x3 -> x4, starting transfers between devices: 8.27 us -> 7.54 us  [swap(): lax.ppermute(value, AXES, [(i, i ^ mask) for i in range(device_count)])]
    pallas_call x3, Pallas kernels: 14.6 us -> 14 us  [call(): pl.pallas_call(kernel, out_shape=outs, in_specs=in_specs, out_specs=[pl.B...]
    ppermute x3 -> x4, waiting for transfers between devices: 3.01 us -> 3.62 us  [swap(): lax.ppermute(value, AXES, [(i, i ^ mask) for i in range(device_count)])]
    ppermute x6, starting transfers between devices: 14 us -> 13.5 us  [per_device(): lax.ppermute(gram, AXES, [(i, i ^ (odd_mask if i % 2 else even_mask)) for...]
  transfers between devices with their start and end apart: 10 -> 11, of which waited for: 7 -> 8; matrix products, arithmetic and copies ran while one was open for 0% -> 0% of each run, Pallas kernels for 7% -> 10%
where the time goes in v4:
time: 51.2 us; the launch traced here: 51 us
  starting transfers between devices  21.7 us (42%)
  Pallas kernels  16.6 us (32%)
  waiting for transfers between devices  11.8 us (23%)
  between operations  0.77 us (2%)
    pallas_call x3, Pallas kernels, call(): pl.pallas_call(kernel, out_shape=outs, in_specs=in_specs, out_specs=[pl.B...  14 us
    ppermute x6, starting transfers between devices, per_device(): lax.ppermute(gram, AXES, [(i, i ^ (odd_mask if i % 2 else even_mask)) for...  13.5 us
    ppermute x6, waiting for transfers between devices, per_device(): lax.ppermute(gram, AXES, [(i, i ^ (odd_mask if i % 2 else even_mask)) for...  8.17 us
    ppermute x4, starting transfers between devices, swap(): lax.ppermute(value, AXES, [(i, i ^ mask) for i in range(device_count)])  7.54 us
    ppermute x4, waiting for transfers between devices, swap(): lax.ppermute(value, AXES, [(i, i ^ mask) for i in range(device_count)])  3.62 us
    pallas_call x2, Pallas kernels, scaled(): pl.pallas_call(functools.partial(scale_kernel, tile=tile), out_shape=jax....  2.65 us
  transfers between devices with their start and end apart: 11, of which 8 were waited for; matrix products, arithmetic and copies ran while one was open for 0% of the time, Pallas kernels for 10%

profile of v4, /device:TPU:0, one launch (start us, length us, event | category | flops | bytes accessed | tf_op | source)
XLA Modules:
  0.0 51.0 jit_solution(9156892400625874163)
XLA Ops:
  0.6 1.3 %shard_map.59.refs_0_.outer_ref = bf16[1024,256]{1,0:T(8,128)(2,1)S(1)} custom-call(s32[1]{0:T(128)} %bitcast.2.first_ref, f32[16,128]{1,0:T(8,128)} %bitcast.4, bf16[2048,256]{1,0:T(8,128)(2,1)} %sketch_ref.3), custom_call_target="tpu_custom_call" | custom-call | flops 1 | bytes 1 | tf_op jit(solution)/shard_map/pallas_call | solution.py:332
  2.0 0.7 %collective-permute-start.2 = (bf16[1024,256]{1,0:T(8,128)(2,1)S(1)}, bf16[1024,256]{1,0:T(8,128)(2,1)S(1)}, u32[]{:S(2)}, u32[]{:S(2)}) collective-permute-start(bf16[1024,256]{1,0:T(8,128)(2,1)S(1)} %shard_map.59.refs_0_.outer_ref), channel_id=1, source_target_pairs={{1,2},{2,1},{3,4},{4,3},{5,6},{6,5},{7,8},{8,7},{9,10},{10,9},{11,... | collective-permute-start | bytes 1572872 | tf_op jit(solution)/shard_map/ppermute | solution.py:365
  2.7 0.0 copy-start
  2.7 0.0 copy-start.1
  2.7 1.3 %shard_map.60.inner_ref = bf16[1024,256]{1,0:T(8,128)(2,1)S(1)} custom-call(s32[1]{0:T(128)} %bitcast.3.first_ref, f32[16,128]{1,0:T(8,128)} %bitcast.5, bf16[2048,256]{1,0:T(8,128)(2,1)} %sketch_ref.3, bf16[1024,256]{1,0:T(8,128)(2,1)S(1)} %shard_map.59.refs_0_.outer_ref), custom_call_target="tpu_custom_call" | custom-call | flops 1 | bytes 1 | tf_op jit(solution)/shard_map/pallas_call | solution.py:332
  4.1 4.4 %collective-permute-start = (bf16[512,256]{1,0:T(8,128)(2,1)S(1)}, bf16[512,256]{1,0:T(8,128)(2,1)S(1)}, u32[]{:S(2)}, u32[]{:S(2)}) collective-permute-start(bf16[512,256]{1,0:T(8,128)(2,1)S(1)} %get-tuple-element.22), channel_id=1, source_target_pairs={{0,1},{1,0},{2,3},{3,2},{4,5},{5,4},{6,7},{7,6},{8,9},{9,8},{10,11... | collective-permute-start | bytes 786440 | tf_op jit(solution)/shard_map/ppermute | solution.py:360
  8.5 0.1 collective-permute-start.1
  8.6 1.1 %collective-permute-done = bf16[512,256]{1,0:T(8,128)(2,1)S(1)} collective-permute-done((bf16[512,256]{1,0:T(8,128)(2,1)S(1)}, bf16[512,256]{1,0:T(8,128)(2,1)S(1)}, u32[]{:S(2)}, u32[]{:S(2)}) %collective-permute-start) | collective-permute-done | bytes 262176 | tf_op jit(solution)/shard_map/ppermute | solution.py:360
  9.7 0.4 collective-permute-done.1
  10.1 0.0 copy-done
  10.1 0.0 copy-done.1
  10.1 3.9 %shard_map.61 = (f32[1024,256]{1,0:T(8,128)S(1)}, f32[1024,128]{1,0:T(8,128)S(1)}, bf16[256,1024]{1,0:T(8,128)(2,1)S(1)}, bf16[1024,256]{1,0:T(8,128)(2,1)S(1)},...) custom-call(s32[1]{0:T(128)} %bitcast.odd_ref, s32[8,9]{1,0:T(8,128)S(1)} %copy-done.1, ...), custom_call_target="tpu_custom_call" | custom-call | flops 1 | bytes 1 | tf_op jit(solution)/shard_map/pallas_call | solution.py:306
  14.0 0.0 collective-permute-done.2.halo_ref
  14.1 1.6 %shard_map.62 = (bf16[1024,256]{1,0:T(8,128)(2,1)S(1)}, bf16[1024,256]{1,0:T(8,128)(2,1)S(1)}, f32[72,256]{1,0:T(8,128)S(1)}, f32[72,256]{1,0:T(8,128)S(1)}) custom-call(s32[1]{0:T(128)} %bitcast.odd_ref, s32[8,9]{1,0:T(8,128)S(1)} %copy-done.1, bf16[256,1024]{1,0:T(8,128)(2,1)S(1)} %get-tuple-element.12.lag_ref, ...), custom_call_target="tpu_custom_call" | custom-call | flops 1 | bytes 1 | tf_op jit(solution)/shard_map/pallas_call | solution.py:306
  15.7 3.0 %collective-permute-start.3 = (f32[72,256]{1,0:T(8,128)S(1)}, f32[72,256]{1,0:T(8,128)S(1)}, u32[]{:S(2)}, u32[]{:S(2)}) collective-permute-start(f32[72,256]{1,0:T(8,128)S(1)} %get-tuple-element.17), channel_id=1, source_target_pairs={{0,1},{1,0},{2,3},{3,2},{4,5},{5,4},{6,7},{7,6},{8,9},{9,8},{10,11... | collective-permute-start | bytes 221192 | tf_op jit(solution)/shard_map/ppermute | solution.py:360
  18.6 0.9 %collective-permute-done.3 = f32[72,256]{1,0:T(8,128)S(1)} collective-permute-done((f32[72,256]{1,0:T(8,128)S(1)}, f32[72,256]{1,0:T(8,128)S(1)}, u32[]{:S(2)}, u32[]{:S(2)}) %collective-permute-start.3) | collective-permute-done | bytes 73760 | tf_op jit(solution)/shard_map/ppermute | solution.py:360
  19.6 6.6 %collective-permute-start.4 = (f32[72,256]{1,0:T(8,128)S(1)}, f32[72,256]{1,0:T(8,128)S(1)}, u32[]{:S(2)}, u32[]{:S(2)}) collective-permute-start(f32[72,256]{1,0:T(8,128)S(1)} %add.30), channel_id=1, source_target_pairs={{0,8},{1,3},{2,10},{3,1},{4,12},{5,7},{6,14},{7,5},{8,0},{9,11},{1... | collective-permute-start | bytes 221192 | tf_op jit(solution)/shard_map/ppermute | solution.py:407
  26.2 1.5 %collective-permute-start.5 = (f32[72,256]{1,0:T(8,128)S(1)}, f32[72,256]{1,0:T(8,128)S(1)}, u32[]{:S(2)}, u32[]{:S(2)}) collective-permute-start(f32[72,256]{1,0:T(8,128)S(1)} %add.30), channel_id=1, source_target_pairs={{0,16},{1,5},{2,18},{3,7},{4,20},{5,1},{6,22},{7,3},{8,24},{9,13},... | collective-permute-start | bytes 221192 | tf_op jit(solution)/shard_map/ppermute | solution.py:407
  27.7 0.9 %collective-permute-start.6 = (f32[72,256]{1,0:T(8,128)S(1)}, f32[72,256]{1,0:T(8,128)S(1)}, u32[]{:S(2)}, u32[]{:S(2)}) collective-permute-start(f32[72,256]{1,0:T(8,128)S(1)} %add.30), channel_id=1, source_target_pairs={{0,24},{1,7},{2,26},{3,5},{4,28},{5,3},{6,30},{7,1},{8,16},{9,15},... | collective-permute-start | bytes 221192 | tf_op jit(solution)/shard_map/ppermute | solution.py:407
  28.6 0.0 collective-permute-done.4
  28.6 2.0 %collective-permute-done.5 = f32[72,256]{1,0:T(8,128)S(1)} collective-permute-done((f32[72,256]{1,0:T(8,128)S(1)}, f32[72,256]{1,0:T(8,128)S(1)}, u32[]{:S(2)}, u32[]{:S(2)}) %collective-permute-start.5) | collective-permute-done | bytes 73760 | tf_op jit(solution)/shard_map/ppermute | solution.py:407
  30.5 2.4 %collective-permute-done.6 = f32[72,256]{1,0:T(8,128)S(1)} collective-permute-done((f32[72,256]{1,0:T(8,128)S(1)}, f32[72,256]{1,0:T(8,128)S(1)}, u32[]{:S(2)}, u32[]{:S(2)}) %collective-permute-start.6) | collective-permute-done | bytes 73760 | tf_op jit(solution)/shard_map/ppermute | solution.py:407
  33.0 0.1 collective-permute-start.7
  33.1 2.0 %collective-permute-start.8 = (f32[72,256]{1,0:T(8,128)S(1)}, f32[72,256]{1,0:T(8,128)S(1)}, u32[]{:S(2)}, u32[]{:S(2)}) collective-permute-start(f32[72,256]{1,0:T(8,128)S(1)} %add_add_fusion.1), channel_id=1, source_target_pairs={{0,4},{1,17},{2,6},{3,19},{4,0},{5,21},{6,2},{7,23},{8,12},{9,25},... | collective-permute-start | bytes 221192 | tf_op jit(solution)/shard_map/ppermute | solution.py:407
  35.1 2.3 %collective-permute-start.9 = (f32[72,256]{1,0:T(8,128)S(1)}, f32[72,256]{1,0:T(8,128)S(1)}, u32[]{:S(2)}, u32[]{:S(2)}) collective-permute-start(f32[72,256]{1,0:T(8,128)S(1)} %add_add_fusion.1), channel_id=1, source_target_pairs={{0,6},{1,25},{2,4},{3,27},{4,2},{5,29},{6,0},{7,31},{8,14},{9,17},... | collective-permute-start | bytes 221192 | tf_op jit(solution)/shard_map/ppermute | solution.py:407
  37.4 0.0 collective-permute-done.7
  37.4 0.9 %collective-permute-done.8 = f32[72,256]{1,0:T(8,128)S(1)} collective-permute-done((f32[72,256]{1,0:T(8,128)S(1)}, f32[72,256]{1,0:T(8,128)S(1)}, u32[]{:S(2)}, u32[]{:S(2)}) %collective-permute-start.8) | collective-permute-done | bytes 73760 | tf_op jit(solution)/shard_map/ppermute | solution.py:407
  38.4 2.9 %collective-permute-done.9 = f32[72,256]{1,0:T(8,128)S(1)} collective-permute-done((f32[72,256]{1,0:T(8,128)S(1)}, f32[72,256]{1,0:T(8,128)S(1)}, u32[]{:S(2)}, u32[]{:S(2)}) %collective-permute-start.9) | collective-permute-done | bytes 73760 | tf_op jit(solution)/shard_map/ppermute | solution.py:407
  41.3 0.1 collective-permute-start.10
  41.3 1.3 %collective-permute-done.10.other_ref = f32[72,256]{1,0:T(8,128)S(1)} collective-permute-done((f32[72,256]{1,0:T(8,128)S(1)}, f32[72,256]{1,0:T(8,128)S(1)}, u32[]{:S(2)}, u32[]{:S(2)}) %collective-permute-start.10) | collective-permute-done | bytes 73760 | tf_op jit(solution)/shard_map/ppermute | solution.py:360
  42.6 8.4 %shard_map.63 = (f32[2048,256]{1,0:T(8,128)}, f32[256,256]{1,0:T(8,128)}) custom-call(s32[1]{0:T(128)} %bitcast.odd_ref, s32[8,9]{1,0:T(8,128)S(1)} %copy-done.1, f32[72,256]{1,0:T(8,128)S(1)} %add_add_fusion.mine_ref, f32[72,256]{1,0:T(8,128)S(1)} %collective-permute-done.10.other_ref, bf16[1024,256]{1,0:T(8,128)(2,1)S(1)} %get-tuple-element.18.far_high_ref, ...), custom_call_target="tpu_custom_call" | custom-call | flops 1 | bytes 1 | tf_op jit(solution)/shard_map/pallas_call | solution.py:306
  (5 shorter events, 0.1 us)
Async XLA Ops:
  2.0 12.1 %collective-permute-start.2 = (bf16[1024,256]{1,0:T(8,128)(2,1)S(1)}, bf16[1024,256]{1,0:T(8,128)(2,1)S(1)}, u32[]{:S(2)}, u32[]{:S(2)}) collective-permute-start(bf16[1024,256]{1,0:T(8,128)(2,1)S(1)} %shard_map.59.refs_0_.outer_ref), channel_id=1, source_target_pairs={{1,2},{2,1},{3,4},{4,3},{5,6},{6,5},{7,8},{8,7},{9,10},{10,9},{11,... | collective-permute-start | bytes 1572872 | tf_op jit(solution)/shard_map/ppermute | solution.py:365
  2.7 7.4 %copy-start = (f32[2048]{0:T(1024)S(1)}, f32[2048]{0:T(1024)}, u32[]{:S(2)}) copy-start(f32[2048]{0:T(1024)} %param.5) | copy-start | bytes 24580
  2.7 7.4 %copy-start.1 = (s32[8,9]{1,0:T(8,128)S(1)}, s32[8,9]{1,0:T(8,128)}, u32[]{:S(2)}) copy-start(s32[8,9]{1,0:T(8,128)} %cols_ref.5) | copy-start | bytes 868
  4.1 5.6 %collective-permute-start = (bf16[512,256]{1,0:T(8,128)(2,1)S(1)}, bf16[512,256]{1,0:T(8,128)(2,1)S(1)}, u32[]{:S(2)}, u32[]{:S(2)}) collective-permute-start(bf16[512,256]{1,0:T(8,128)(2,1)S(1)} %get-tuple-element.22), channel_id=1, source_target_pairs={{0,1},{1,0},{2,3},{3,2},{4,5},{5,4},{6,7},{7,6},{8,9},{9,8},{10,11... | collective-permute-start | bytes 786440 | tf_op jit(solution)/shard_map/ppermute | solution.py:360
  8.5 1.5 %collective-permute-start.1 = (bf16[512,256]{1,0:T(8,128)(2,1)S(1)}, bf16[512,256]{1,0:T(8,128)(2,1)S(1)}, u32[]{:S(2)}, u32[]{:S(2)}) collective-permute-start(bf16[512,256]{1,0:T(8,128)(2,1)S(1)} %get-tuple-element.23), channel_id=1, source_target_pairs={{0,1},{1,0},{2,3},{3,2},{4,5},{5,4},{6,7},{7,6},{8,9},{9,8},{10,11... | collective-permute-start | bytes 786440 | tf_op jit(solution)/shard_map/ppermute | solution.py:360
  15.7 3.9 %collective-permute-start.3 = (f32[72,256]{1,0:T(8,128)S(1)}, f32[72,256]{1,0:T(8,128)S(1)}, u32[]{:S(2)}, u32[]{:S(2)}) collective-permute-start(f32[72,256]{1,0:T(8,128)S(1)} %get-tuple-element.17), channel_id=1, source_target_pairs={{0,1},{1,0},{2,3},{3,2},{4,5},{5,4},{6,7},{7,6},{8,9},{9,8},{10,11... | collective-permute-start | bytes 221192 | tf_op jit(solution)/shard_map/ppermute | solution.py:360
  19.6 9.0 %collective-permute-start.4 = (f32[72,256]{1,0:T(8,128)S(1)}, f32[72,256]{1,0:T(8,128)S(1)}, u32[]{:S(2)}, u32[]{:S(2)}) collective-permute-start(f32[72,256]{1,0:T(8,128)S(1)} %add.30), channel_id=1, source_target_pairs={{0,8},{1,3},{2,10},{3,1},{4,12},{5,7},{6,14},{7,5},{8,0},{9,11},{1... | collective-permute-start | bytes 221192 | tf_op jit(solution)/shard_map/ppermute | solution.py:407
  26.2 4.4 %collective-permute-start.5 = (f32[72,256]{1,0:T(8,128)S(1)}, f32[72,256]{1,0:T(8,128)S(1)}, u32[]{:S(2)}, u32[]{:S(2)}) collective-permute-start(f32[72,256]{1,0:T(8,128)S(1)} %add.30), channel_id=1, source_target_pairs={{0,16},{1,5},{2,18},{3,7},{4,20},{5,1},{6,22},{7,3},{8,24},{9,13},... | collective-permute-start | bytes 221192 | tf_op jit(solution)/shard_map/ppermute | solution.py:407
  27.7 5.3 %collective-permute-start.6 = (f32[72,256]{1,0:T(8,128)S(1)}, f32[72,256]{1,0:T(8,128)S(1)}, u32[]{:S(2)}, u32[]{:S(2)}) collective-permute-start(f32[72,256]{1,0:T(8,128)S(1)} %add.30), channel_id=1, source_target_pairs={{0,24},{1,7},{2,26},{3,5},{4,28},{5,3},{6,30},{7,1},{8,16},{9,15},... | collective-permute-start | bytes 221192 | tf_op jit(solution)/shard_map/ppermute | solution.py:407
  33.0 4.5 %collective-permute-start.7 = (f32[72,256]{1,0:T(8,128)S(1)}, f32[72,256]{1,0:T(8,128)S(1)}, u32[]{:S(2)}, u32[]{:S(2)}) collective-permute-start(f32[72,256]{1,0:T(8,128)S(1)} %add_add_fusion.1), channel_id=1, source_target_pairs={{0,2},{1,9},{2,0},{3,11},{4,6},{5,13},{6,4},{7,15},{8,10},{9,1},{1... | collective-permute-start | bytes 221192 | tf_op jit(solution)/shard_map/ppermute | solution.py:407
  33.1 5.3 %collective-permute-start.8 = (f32[72,256]{1,0:T(8,128)S(1)}, f32[72,256]{1,0:T(8,128)S(1)}, u32[]{:S(2)}, u32[]{:S(2)}) collective-permute-start(f32[72,256]{1,0:T(8,128)S(1)} %add_add_fusion.1), channel_id=1, source_target_pairs={{0,4},{1,17},{2,6},{3,19},{4,0},{5,21},{6,2},{7,23},{8,12},{9,25},... | collective-permute-start | bytes 221192 | tf_op jit(solution)/shard_map/ppermute | solution.py:407
  35.1 6.2 %collective-permute-start.9 = (f32[72,256]{1,0:T(8,128)S(1)}, f32[72,256]{1,0:T(8,128)S(1)}, u32[]{:S(2)}, u32[]{:S(2)}) collective-permute-start(f32[72,256]{1,0:T(8,128)S(1)} %add_add_fusion.1), channel_id=1, source_target_pairs={{0,6},{1,25},{2,4},{3,27},{4,2},{5,29},{6,0},{7,31},{8,14},{9,17},... | collective-permute-start | bytes 221192 | tf_op jit(solution)/shard_map/ppermute | solution.py:407
  41.3 1.3 %collective-permute-start.10 = (f32[72,256]{1,0:T(8,128)S(1)}, f32[72,256]{1,0:T(8,128)S(1)}, u32[]{:S(2)}, u32[]{:S(2)}) collective-permute-start(f32[72,256]{1,0:T(8,128)S(1)} %add_add_fusion.mine_ref), channel_id=1, source_target_pairs={{0,1},{1,0},{2,3},{3,2},{4,5},{5,4},{6,7},{7,6},{8,9},{9,8},{10,11... | collective-permute-start | bytes 221192 | tf_op jit(solution)/shard_map/ppermute | solution.py:360

commit v5 on v4

--- a/solution.py
+++ b/solution.py
@@ -13,6 +13,7 @@
 LANES = 128
 SUBLANES = 8
 VMEM_LIMIT = 48 * 1024 * 1024
+HALO_PARTS = 2
 SMALL_COST = pl.CostEstimate(flops=1, bytes_accessed=1, transcendentals=0)
 
 
@@ -53,58 +54,54 @@
     return cols_ref[first, reach - place + line % reach] - cols_ref[0, reach]
 
 
-def halo_tile(cols_ref, odd, distance, reach, lags, outer):
-    count = 2 * reach
-    low_side = (odd == 0) if outer else (odd == 1)
-    edge_line = 0 if outer else count - 1
-    tile = own_tile(cols_ref, odd, edge_line, reach)
-    lag = jnp.where(low_side, reach - 1 - distance, reach + 1 + distance)
-    column = cols_ref[tile, lag]
-    base = cols_ref[0, reach] + jnp.where(low_side, -reach, count)
-    return jnp.clip(column - base, 0, reach - 1)
-
-
-def scale_kernel(first_ref, std_hbm_ref, sketch_ref, *refs, tile):
-    out_ref, std_ref, rows_ref, sems = refs[-4:]
-    count = out_ref.shape[0] // tile
-    first = first_ref[0]
-    copies = [pltpu.make_async_copy(std_hbm_ref, std_ref, sems.at[count])]
-    for i in range(count):
-        place = pl.multiple_of((first + i) * tile, tile)
-        target = rows_ref.at[pl.ds(i * tile, tile), :]
-        copies.append(pltpu.make_async_copy(sketch_ref.at[pl.ds(place, tile), :], target, sems.at[i]))
+def odd_device():
+    return lax.rem(lax.axis_index(AXES), 2)
+
+
+def scale_kernel(cols_hbm_ref, std_hbm_ref, sketch_ref, *refs, reach, tile, inner):
+    out_ref, cols_ref, std_ref, rows_ref, sems = refs[-5:]
+    odd = odd_device()
+    first = jnp.where(odd == (0 if inner else 1), reach, 0)
+    place = pl.multiple_of(first * tile, tile)
+    copies = [
+        pltpu.make_async_copy(sketch_ref.at[pl.ds(place, reach * tile), :], rows_ref, sems.at[0]),
+        pltpu.make_async_copy(cols_hbm_ref, cols_ref, sems.at[1]),
+        pltpu.make_async_copy(std_hbm_ref, std_ref, sems.at[2]),
+    ]
     for copy in copies:
         copy.start()
+    copies[1].wait()
+    copies[2].wait()
+    tiles = [own_tile(cols_ref, odd, line + (reach if inner else 0), reach) for line in range(reach)]
+    columns = [std_column(std_ref, index, tile, out_ref.shape[1]) for index in tiles]
     copies[0].wait()
-    for i in range(count):
-        std = std_column(std_ref, first + i, tile, out_ref.shape[1])
-        copies[i + 1].wait()
-        rows = slice(i * tile, (i + 1) * tile)
-        out_ref[rows, :] = (rows_ref[rows, :].astype(F32) * std).astype(BF16)
+    for line in range(reach):
+        place = pl.multiple_of((tiles[line] - first) * tile, tile)
+        rows = rows_ref[pl.ds(place, tile), :].astype(F32)
+        out_ref[line * tile : (line + 1) * tile, :] = (rows * columns[line]).astype(BF16)
 
 
 def near_kernel(
-    odd_ref, cols_ref, cov_ref, std_ref, outer_ref, inner_ref, halo_ref,
-    acc_ref, scale_ref, lag_ref, high_ref, low_ref, gram_ref, lags_ref, lines_ref,
-    *, reach, lags, tile,
+    cols_ref, cov_ref, std_ref, outer_ref, inner_ref, *refs, reach, lags, tile
 ):
-    odd = odd_ref[0]
+    halo_refs = refs[:HALO_PARTS]
+    acc_ref, scale_ref, lag_ref, high_ref, low_ref, gram_ref, lags_ref, lines_ref = refs[HALO_PARTS:]
+    odd = odd_device()
     count = 2 * reach
     for e in range(lags):
         lags_ref[:, e * tile : (e + 1) * tile] = cov_ref[jnp.where(odd == 1, lags - 1 - e, e)]
-    lag_ref[...] = lags_ref[:, : reach * tile]
-    for line in range(3 * reach):
-        if line < reach:
-            index = own_tile(cols_ref, odd, line, reach) - jnp.where(odd == 1, reach, 0)
-            source = outer_ref
-        elif line < count:
-            index = own_tile(cols_ref, odd, line, reach) - jnp.where(odd == 1, 0, reach)
-            source = inner_ref
-        else:
-            index = halo_tile(cols_ref, odd, line - count, reach, lags, False)
-            source = halo_ref
-        place = pl.multiple_of(index * tile, tile)
-        lines_ref[line * tile : (line + 1) * tile, :] = source[pl.ds(place, tile), :]
+    for e in range(reach):
+        lag_ref[:, e * tile : (e + 1) * tile] = lags_ref[:, (reach - 1 - e) * tile : (reach - e) * tile]
+    half = reach * tile
+    lines_ref[:half, :] = outer_ref[...]
+    lines_ref[half : 2 * half, :] = inner_ref[...]
+    part = half // HALO_PARTS
+    for line in range(reach):
+        place = (reach - 1 - line) * tile
+        source = halo_refs[place // part]
+        lines_ref[2 * half + line * tile : 2 * half + (line + 1) * tile, :] = source[
+            place % part : place % part + tile, :
+        ]
     for line in range(count):
         first = max(0, reach - line)
         start = max(0, line - reach) * tile
@@ -129,21 +126,16 @@
 
 
 def far_kernel(
-    odd_ref, cols_ref, lag_ref, scale_ref, acc_ref, halo_ref, gram_ref,
-    high_ref, low_ref, keep_ref, send_ref, lines_ref,
-    *, reach, lags, tile, total,
+    lag_ref, scale_ref, acc_ref, halo_ref, gram_ref, high_ref, low_ref, keep_ref, send_ref,
+    *, reach, tile, total,
 ):
-    odd = odd_ref[0]
+    odd = odd_device()
     width = acc_ref.shape[1]
-    for line in range(reach):
-        index = halo_tile(cols_ref, odd, reach - 1 - line, reach, lags, True)
-        place = pl.multiple_of(index * tile, tile)
-        lines_ref[line * tile : (line + 1) * tile, :] = halo_ref[pl.ds(place, tile), :]
     for line in range(reach):
         rows = slice(line * tile, (line + 1) * tile)
         product = acc_ref[rows, :] + jnp.dot(
-            lag_ref[:, : (reach - line) * tile],
-            lines_ref[line * tile :, :],
+            lag_ref[:, line * tile :],
+            halo_ref[: (reach - line) * tile, :],
             preferred_element_type=F32,
         )
         scale = jnp.concatenate([scale_ref[rows, :]] * (width // LANES), axis=1)
@@ -268,16 +260,19 @@
 
 
 def basis_kernel(
-    odd_ref, cols_ref, mine_ref, other_ref, far_high_ref, far_low_ref, near_high_ref, near_low_ref,
-    basis_ref, factor_ref, work_ref, inverse_ref, tiles_ref, held_ref, sems,
+    cols_hbm_ref, mine_ref, other_ref, far_high_ref, far_low_ref, near_high_ref, near_low_ref,
+    basis_ref, factor_ref, work_ref, inverse_ref, tiles_ref, held_ref, cols_ref, sems,
     *, reach, tile,
 ):
-    odd = odd_ref[0]
+    odd = odd_device()
+    cols_copy = pltpu.make_async_copy(cols_hbm_ref, cols_ref, sems.at[2 * reach + 1])
+    cols_copy.start()
     mine, other = mine_ref[...], other_ref[...]
     unpack(jnp.where(odd == 1, other, mine), jnp.where(odd == 1, mine, other), work_ref)
     eliminate(work_ref, held_ref, inverse_ref)
     factor_copy = pltpu.make_async_copy(held_ref, factor_ref, sems.at[2 * reach])
     factor_copy.start()
+    cols_copy.wait()
     high, low = split2(inverse_ref[...])
     right = jnp.concatenate([high, high, low], axis=1)
     copies = []
@@ -298,18 +293,16 @@
     factor_copy.wait()
 
 
-def call(kernel, outs, scratch, smem_count, operands, hbm_outs=0):
-    in_specs = [
-        pl.BlockSpec(memory_space=pltpu.SMEM if i < smem_count else pltpu.VMEM)
-        for i in range(len(operands))
+def call(kernel, outs, scratch, spaces, operands, out_spaces=None):
+    operands = [
+        pltpu.with_memory_space_constraint(operand, space) if space is pltpu.HBM else operand
+        for operand, space in zip(operands, spaces)
     ]
     return pl.pallas_call(
         kernel,
         out_shape=outs,
-        in_specs=in_specs,
-        out_specs=[
-            pl.BlockSpec(memory_space=pl.ANY if i < hbm_outs else pltpu.VMEM) for i in range(len(outs))
-        ],
+        in_specs=[pl.BlockSpec(memory_space=space) for space in spaces],
+        out_specs=[pl.BlockSpec(memory_space=space) for space in out_spaces or [pltpu.VMEM] * len(outs)],
         scratch_shapes=scratch,
         cost_estimate=SMALL_COST,
         compiler_params=pltpu.CompilerParams(vmem_limit_bytes=VMEM_LIMIT),
@@ -323,51 +316,36 @@
     halo = reach * tile
     assert row_count == 2 * halo and width % (2 * LANES) == 0
     assert device_count & (device_count - 1) == 0 and device_count > 1
-    odd = lax.axis_index(AXES) % 2
-    odd_arg = odd.astype(jnp.int32).reshape(1)
-
-    std_rows = marginal_std.reshape(-1, LANES)
-
-    def scaled(first, *after):
-        return pl.pallas_call(
-            functools.partial(scale_kernel, tile=tile),
-            out_shape=jax.ShapeDtypeStruct((halo, width), BF16),
-            in_specs=[
-                pl.BlockSpec(memory_space=pltpu.SMEM),
-                pl.BlockSpec(memory_space=pltpu.HBM),
-                pl.BlockSpec(memory_space=pltpu.HBM),
-            ]
-            + [pl.BlockSpec(memory_space=pl.ANY)] * len(after),
-            out_specs=pl.BlockSpec(memory_space=pltpu.VMEM),
-            scratch_shapes=[
-                pltpu.VMEM(std_rows.shape, F32),
-                pltpu.VMEM((halo, width), BF16),
-                pltpu.SemaphoreType.DMA((reach + 1,)),
-            ],
-            cost_estimate=SMALL_COST,
-            compiler_params=pltpu.CompilerParams(vmem_limit_bytes=VMEM_LIMIT),
-        )(
-            first.astype(jnp.int32).reshape(1),
-            pltpu.with_memory_space_constraint(std_rows, pltpu.HBM),
-            pltpu.with_memory_space_constraint(sketch, pltpu.HBM),
-            *after,
-        )
-
-    outer = scaled(jnp.where(odd == 1, reach, 0))
-    inner = scaled(jnp.where(odd == 1, 0, reach), outer)
-
     def swap(value, mask):
         return lax.ppermute(value, AXES, [(i, i ^ mask) for i in range(device_count)])
 
     outer_pairs = []
     for i in range(1, device_count - 1, 2):
         outer_pairs += [(i, i + 1), (i + 1, i)]
-    outer_halo = lax.ppermute(outer, AXES, outer_pairs)
-    inner_halo = jnp.concatenate([swap(inner[: halo // 2], 1), swap(inner[halo // 2 :], 1)], axis=0)
+    std_rows = marginal_std.reshape(-1, LANES)
 
     def shape(rows, columns, dtype):
         return jax.ShapeDtypeStruct((rows, columns), dtype)
 
+    def scaled(inner, *after):
+        return call(
+            functools.partial(scale_kernel, reach=reach, tile=tile, inner=inner),
+            [shape(halo, width, BF16)],
+            [
+                pltpu.SMEM(tile_cols.shape, jnp.int32),
+                pltpu.VMEM(std_rows.shape, F32),
+                pltpu.VMEM((halo, width), BF16),
+                pltpu.SemaphoreType.DMA((3,)),
+            ],
+            [pltpu.HBM] * 3 + [pl.ANY] * len(after),
+            (tile_cols, std_rows, sketch, *after),
+        )[0]
+
+    outer = scaled(False)
+    inner = scaled(True, outer)
+    outer_halo = lax.ppermute(outer, AXES, outer_pairs)
+    part = halo // HALO_PARTS
+    inner_halo = [swap(inner[i : i + part], 1) for i in range(0, halo, part)]
     acc, scale, lag_block, near_high, near_low, near_gram = call(
         functools.partial(near_kernel, reach=reach, lags=lags, tile=tile),
         [
@@ -379,22 +357,20 @@
             shape(width, 2 * width, F32),
         ],
         [pltpu.VMEM((tile, lags * tile), BF16), pltpu.VMEM((3 * halo, width), BF16)],
-        2,
-        (odd_arg, tile_cols, cov_tiles, std_rows, outer, inner, inner_halo),
+        [pltpu.SMEM] + [pltpu.VMEM] * (4 + HALO_PARTS),
+        (tile_cols, cov_tiles, std_rows, outer, inner, *inner_halo),
     )
     far_high, far_low, keep, send = call(
-        functools.partial(
-            far_kernel, reach=reach, lags=lags, tile=tile, total=row_count * device_count
-        ),
+        functools.partial(far_kernel, reach=reach, tile=tile, total=row_count * device_count),
         [
             shape(halo, width, BF16),
             shape(halo, width, BF16),
             shape(width // 4 + SUBLANES, width, F32),
             shape(width // 4 + SUBLANES, width, F32),
         ],
-        [pltpu.VMEM((halo, width), BF16)],
-        2,
-        (odd_arg, tile_cols, lag_block, scale, acc, outer_halo, near_gram),
+        [],
+        [pltpu.VMEM] * 5,
+        (lag_block, scale, acc, outer_halo, near_gram),
     )
     gram = keep + swap(send, 1)
     bits = [1 << i for i in range(1, device_count.bit_length() - 1)]
@@ -421,11 +397,12 @@
             pltpu.VMEM((width, width), F32),
             pltpu.VMEM((2 * reach, tile, width), F32),
             pltpu.VMEM((width, width), F32),
-            pltpu.SemaphoreType.DMA((2 * reach + 1,)),
+            pltpu.SMEM(tile_cols.shape, jnp.int32),
+            pltpu.SemaphoreType.DMA((2 * reach + 2,)),
         ],
-        2,
-        (odd_arg, tile_cols, gram, other, far_high, far_low, near_high, near_low),
-        2,
+        [pltpu.HBM] + [pltpu.VMEM] * 6,
+        (tile_cols, gram, other, far_high, far_low, near_high, near_low),
+        [pl.ANY] * 2,
     )
     return basis, factor
 

time: 51.2 us -> 50 us (0.977)
  Pallas kernels: 16.6 us -> 15.3 us
    pallas_call x5, Pallas kernels: 16.6 us -> 15.3 us  [call(): pl.pallas_call(kernel, out_shape=outs, in_specs=[pl.BlockSpec(memory_spac...]
where the time goes in v5:
time: 50 us; the launch traced here: 49.7 us
  starting transfers between devices  21.9 us (44%)
  Pallas kernels  15.3 us (31%)
  waiting for transfers between devices  11.8 us (24%)
  between operations  0.73 us (1%)
    pallas_call x5, Pallas kernels, call(): pl.pallas_call(kernel, out_shape=outs, in_specs=[pl.BlockSpec(memory_spac...  15.3 us
    ppermute x6, starting transfers between devices, per_device(): lax.ppermute(gram, AXES, [(i, i ^ (odd_mask if i % 2 else even_mask)) for...  13.5 us
    ppermute x6, waiting for transfers between devices, per_device(): lax.ppermute(gram, AXES, [(i, i ^ (odd_mask if i % 2 else even_mask)) for...  8.17 us
    ppermute x4, starting transfers between devices, swap(): lax.ppermute(value, AXES, [(i, i ^ mask) for i in range(device_count)])  7.71 us
    ppermute x4, waiting for transfers between devices, swap(): lax.ppermute(value, AXES, [(i, i ^ mask) for i in range(device_count)])  3.62 us
  transfers between devices with their start and end apart: 11, of which 8 were waited for; matrix products, arithmetic and copies ran while one was open for 0% of the time, Pallas kernels for 10%

profile of v5, /device:TPU:0, one launch (start us, length us, event | category | flops | bytes accessed | tf_op | source)
XLA Modules:
  0.0 49.7 jit_solution(12377140113444508032)
XLA Ops:
  0.6 0.0 copy-start
  0.6 0.0 copy-start.1
  0.7 1.2 %shard_map.59.refs_0_.outer_ref = bf16[1024,256]{1,0:T(8,128)(2,1)S(1)} custom-call(s32[8,9]{1,0:T(8,128)} %cols_hbm_ref.5, f32[16,128]{1,0:T(8,128)} %bitcast.1, bf16[2048,256]{1,0:T(8,128)(2,1)} %sketch_ref.3), custom_call_target="tpu_custom_call" | custom-call | flops 1 | bytes 1 | tf_op jit(solution)/shard_map/pallas_call | solution.py:301
  1.9 0.7 %collective-permute-start.2 = (bf16[1024,256]{1,0:T(8,128)(2,1)S(1)}, bf16[1024,256]{1,0:T(8,128)(2,1)S(1)}, u32[]{:S(2)}, u32[]{:S(2)}) collective-permute-start(bf16[1024,256]{1,0:T(8,128)(2,1)S(1)} %shard_map.59.refs_0_.outer_ref), channel_id=1, source_target_pairs={{1,2},{2,1},{3,4},{4,3},{5,6},{6,5},{7,8},{8,7},{9,10},{10,9},{11,... | collective-permute-start | bytes 1572872 | tf_op jit(solution)/shard_map/ppermute | solution.py:346
  2.6 1.2 %shard_map.60.inner_ref = bf16[1024,256]{1,0:T(8,128)(2,1)S(1)} custom-call(s32[8,9]{1,0:T(8,128)} %cols_hbm_ref.5, f32[16,128]{1,0:T(8,128)} %bitcast.2, bf16[2048,256]{1,0:T(8,128)(2,1)} %sketch_ref.3, bf16[1024,256]{1,0:T(8,128)(2,1)S(1)} %shard_map.59.refs_0_.outer_ref), custom_call_target="tpu_custom_call" | custom-call | flops 1 | bytes 1 | tf_op jit(solution)/shard_map/pallas_call | solution.py:301
  3.9 4.4 %collective-permute-start = (bf16[512,256]{1,0:T(8,128)(2,1)S(1)}, bf16[512,256]{1,0:T(8,128)(2,1)S(1)}, u32[]{:S(2)}, u32[]{:S(2)}) collective-permute-start(bf16[512,256]{1,0:T(8,128)(2,1)S(1)} %get-tuple-element.23), channel_id=1, source_target_pairs={{0,1},{1,0},{2,3},{3,2},{4,5},{5,4},{6,7},{7,6},{8,9},{9,8},{10,11... | collective-permute-start | bytes 786440 | tf_op jit(solution)/shard_map/ppermute | solution.py:320
  8.3 0.1 collective-permute-start.1
  8.4 1.1 %collective-permute-done.refs_0_ = bf16[512,256]{1,0:T(8,128)(2,1)S(1)} collective-permute-done((bf16[512,256]{1,0:T(8,128)(2,1)S(1)}, bf16[512,256]{1,0:T(8,128)(2,1)S(1)}, u32[]{:S(2)}, u32[]{:S(2)}) %collective-permute-start) | collective-permute-done | bytes 262176 | tf_op jit(solution)/shard_map/ppermute | solution.py:320
  9.4 0.4 collective-permute-done.1.refs_1_
  9.8 0.0 copy-done
  9.8 0.0 copy-done.1
  9.8 3.9 %shard_map.61 = (f32[1024,256]{1,0:T(8,128)S(1)}, f32[1024,128]{1,0:T(8,128)S(1)}, bf16[256,1024]{1,0:T(8,128)(2,1)S(1)}, bf16[1024,256]{1,0:T(8,128)(2,1)S(1)},...) custom-call(s32[8,9]{1,0:T(8,128)S(1)} %copy-done.1, bf16[9,256,256]{2,1,0:T(8,128)(2,1)} %cov_ref.1, ...), custom_call_target="tpu_custom_call" | custom-call | flops 1 | bytes 1 | tf_op jit(solution)/shard_map/pallas_call | solution.py:301
  13.8 0.0 collective-permute-done.2.halo_ref
  13.8 1.0 %shard_map.62 = (bf16[1024,256]{1,0:T(8,128)(2,1)S(1)}, bf16[1024,256]{1,0:T(8,128)(2,1)S(1)}, f32[72,256]{1,0:T(8,128)S(1)}, f32[72,256]{1,0:T(8,128)S(1)}) custom-call(bf16[256,1024]{1,0:T(8,128)(2,1)S(1)} %get-tuple-element.12.lag_ref, f32[1024,128]{1,0:T(8,128)S(1)} %get-tuple-element.13.scale_ref, f32[1024,256]{1,0:T(8,128)S(1)} %get-tuple-element.14.acc_ref, ...), custom_call_target="tpu_custom_call" | custom-call | flops 1 | bytes 1 | tf_op jit(solution)/shard_map/pallas_call | solution.py:301
  14.8 3.1 %collective-permute-start.3 = (f32[72,256]{1,0:T(8,128)S(1)}, f32[72,256]{1,0:T(8,128)S(1)}, u32[]{:S(2)}, u32[]{:S(2)}) collective-permute-start(f32[72,256]{1,0:T(8,128)S(1)} %get-tuple-element.17), channel_id=1, source_target_pairs={{0,1},{1,0},{2,3},{3,2},{4,5},{5,4},{6,7},{7,6},{8,9},{9,8},{10,11... | collective-permute-start | bytes 221192 | tf_op jit(solution)/shard_map/ppermute | solution.py:320
  18.0 0.9 %collective-permute-done.3 = f32[72,256]{1,0:T(8,128)S(1)} collective-permute-done((f32[72,256]{1,0:T(8,128)S(1)}, f32[72,256]{1,0:T(8,128)S(1)}, u32[]{:S(2)}, u32[]{:S(2)}) %collective-permute-start.3) | collective-permute-done | bytes 73760 | tf_op jit(solution)/shard_map/ppermute | solution.py:320
  18.9 6.6 %collective-permute-start.4 = (f32[72,256]{1,0:T(8,128)S(1)}, f32[72,256]{1,0:T(8,128)S(1)}, u32[]{:S(2)}, u32[]{:S(2)}) collective-permute-start(f32[72,256]{1,0:T(8,128)S(1)} %add.21), channel_id=1, source_target_pairs={{0,8},{1,3},{2,10},{3,1},{4,12},{5,7},{6,14},{7,5},{8,0},{9,11},{1... | collective-permute-start | bytes 221192 | tf_op jit(solution)/shard_map/ppermute | solution.py:383
  25.5 1.5 %collective-permute-start.5 = (f32[72,256]{1,0:T(8,128)S(1)}, f32[72,256]{1,0:T(8,128)S(1)}, u32[]{:S(2)}, u32[]{:S(2)}) collective-permute-start(f32[72,256]{1,0:T(8,128)S(1)} %add.21), channel_id=1, source_target_pairs={{0,16},{1,5},{2,18},{3,7},{4,20},{5,1},{6,22},{7,3},{8,24},{9,13},... | collective-permute-start | bytes 221192 | tf_op jit(solution)/shard_map/ppermute | solution.py:383
  27.0 0.9 %collective-permute-start.6 = (f32[72,256]{1,0:T(8,128)S(1)}, f32[72,256]{1,0:T(8,128)S(1)}, u32[]{:S(2)}, u32[]{:S(2)}) collective-permute-start(f32[72,256]{1,0:T(8,128)S(1)} %add.21), channel_id=1, source_target_pairs={{0,24},{1,7},{2,26},{3,5},{4,28},{5,3},{6,30},{7,1},{8,16},{9,15},... | collective-permute-start | bytes 221192 | tf_op jit(solution)/shard_map/ppermute | solution.py:383
  27.9 0.0 collective-permute-done.4
  27.9 2.0 %collective-permute-done.5 = f32[72,256]{1,0:T(8,128)S(1)} collective-permute-done((f32[72,256]{1,0:T(8,128)S(1)}, f32[72,256]{1,0:T(8,128)S(1)}, u32[]{:S(2)}, u32[]{:S(2)}) %collective-permute-start.5) | collective-permute-done | bytes 73760 | tf_op jit(solution)/shard_map/ppermute | solution.py:383
  29.8 2.4 %collective-permute-done.6 = f32[72,256]{1,0:T(8,128)S(1)} collective-permute-done((f32[72,256]{1,0:T(8,128)S(1)}, f32[72,256]{1,0:T(8,128)S(1)}, u32[]{:S(2)}, u32[]{:S(2)}) %collective-permute-start.6) | collective-permute-done | bytes 73760 | tf_op jit(solution)/shard_map/ppermute | solution.py:383
  32.3 0.1 collective-permute-start.7
  32.4 2.0 %collective-permute-start.8 = (f32[72,256]{1,0:T(8,128)S(1)}, f32[72,256]{1,0:T(8,128)S(1)}, u32[]{:S(2)}, u32[]{:S(2)}) collective-permute-start(f32[72,256]{1,0:T(8,128)S(1)} %add_add_fusion.1), channel_id=1, source_target_pairs={{0,4},{1,17},{2,6},{3,19},{4,0},{5,21},{6,2},{7,23},{8,12},{9,25},... | collective-permute-start | bytes 221192 | tf_op jit(solution)/shard_map/ppermute | solution.py:383
  34.4 2.4 %collective-permute-start.9 = (f32[72,256]{1,0:T(8,128)S(1)}, f32[72,256]{1,0:T(8,128)S(1)}, u32[]{:S(2)}, u32[]{:S(2)}) collective-permute-start(f32[72,256]{1,0:T(8,128)S(1)} %add_add_fusion.1), channel_id=1, source_target_pairs={{0,6},{1,25},{2,4},{3,27},{4,2},{5,29},{6,0},{7,31},{8,14},{9,17},... | collective-permute-start | bytes 221192 | tf_op jit(solution)/shard_map/ppermute | solution.py:383
  36.7 0.0 collective-permute-done.7
  36.7 0.9 %collective-permute-done.8 = f32[72,256]{1,0:T(8,128)S(1)} collective-permute-done((f32[72,256]{1,0:T(8,128)S(1)}, f32[72,256]{1,0:T(8,128)S(1)}, u32[]{:S(2)}, u32[]{:S(2)}) %collective-permute-start.8) | collective-permute-done | bytes 73760 | tf_op jit(solution)/shard_map/ppermute | solution.py:383
  37.7 2.9 %collective-permute-done.9 = f32[72,256]{1,0:T(8,128)S(1)} collective-permute-done((f32[72,256]{1,0:T(8,128)S(1)}, f32[72,256]{1,0:T(8,128)S(1)}, u32[]{:S(2)}, u32[]{:S(2)}) %collective-permute-start.9) | collective-permute-done | bytes 73760 | tf_op jit(solution)/shard_map/ppermute | solution.py:383
  40.6 0.1 collective-permute-start.10
  40.6 1.3 %collective-permute-done.10.other_ref = f32[72,256]{1,0:T(8,128)S(1)} collective-permute-done((f32[72,256]{1,0:T(8,128)S(1)}, f32[72,256]{1,0:T(8,128)S(1)}, u32[]{:S(2)}, u32[]{:S(2)}) %collective-permute-start.10) | collective-permute-done | bytes 73760 | tf_op jit(solution)/shard_map/ppermute | solution.py:320
  41.9 7.9 %shard_map.63 = (f32[2048,256]{1,0:T(8,128)}, f32[256,256]{1,0:T(8,128)}) custom-call(s32[8,9]{1,0:T(8,128)} %cols_hbm_ref.5, f32[72,256]{1,0:T(8,128)S(1)} %add_add_fusion.mine_ref, f32[72,256]{1,0:T(8,128)S(1)} %collective-permute-done.10.other_ref, bf16[1024,256]{1,0:T(8,128)(2,1)S(1)} %get-tuple-element.18.far_high_ref, ...), custom_call_target="tpu_custom_call" | custom-call | flops 1 | bytes 1 | tf_op jit(solution)/shard_map/pallas_call | solution.py:301
  (4 shorter events, 0.1 us)
Async XLA Ops:
  0.6 9.2 %copy-start = (f32[2048]{0:T(1024)S(1)}, f32[2048]{0:T(1024)}, u32[]{:S(2)}) copy-start(f32[2048]{0:T(1024)} %param.5) | copy-start | bytes 24580
  0.6 9.2 %copy-start.1 = (s32[8,9]{1,0:T(8,128)S(1)}, s32[8,9]{1,0:T(8,128)}, u32[]{:S(2)}) copy-start(s32[8,9]{1,0:T(8,128)} %cols_hbm_ref.5) | copy-start | bytes 868
  1.9 11.9 %collective-permute-start.2 = (bf16[1024,256]{1,0:T(8,128)(2,1)S(1)}, bf16[1024,256]{1,0:T(8,128)(2,1)S(1)}, u32[]{:S(2)}, u32[]{:S(2)}) collective-permute-start(bf16[1024,256]{1,0:T(8,128)(2,1)S(1)} %shard_map.59.refs_0_.outer_ref), channel_id=1, source_target_pairs={{1,2},{2,1},{3,4},{4,3},{5,6},{6,5},{7,8},{8,7},{9,10},{10,9},{11,... | collective-permute-start | bytes 1572872 | tf_op jit(solution)/shard_map/ppermute | solution.py:346
  3.9 5.6 %collective-permute-start = (bf16[512,256]{1,0:T(8,128)(2,1)S(1)}, bf16[512,256]{1,0:T(8,128)(2,1)S(1)}, u32[]{:S(2)}, u32[]{:S(2)}) collective-permute-start(bf16[512,256]{1,0:T(8,128)(2,1)S(1)} %get-tuple-element.23), channel_id=1, source_target_pairs={{0,1},{1,0},{2,3},{3,2},{4,5},{5,4},{6,7},{7,6},{8,9},{9,8},{10,11... | collective-permute-start | bytes 786440 | tf_op jit(solution)/shard_map/ppermute | solution.py:320
  8.3 1.5 %collective-permute-start.1 = (bf16[512,256]{1,0:T(8,128)(2,1)S(1)}, bf16[512,256]{1,0:T(8,128)(2,1)S(1)}, u32[]{:S(2)}, u32[]{:S(2)}) collective-permute-start(bf16[512,256]{1,0:T(8,128)(2,1)S(1)} %get-tuple-element.22), channel_id=1, source_target_pairs={{0,1},{1,0},{2,3},{3,2},{4,5},{5,4},{6,7},{7,6},{8,9},{9,8},{10,11... | collective-permute-start | bytes 786440 | tf_op jit(solution)/shard_map/ppermute | solution.py:320
  14.8 4.1 %collective-permute-start.3 = (f32[72,256]{1,0:T(8,128)S(1)}, f32[72,256]{1,0:T(8,128)S(1)}, u32[]{:S(2)}, u32[]{:S(2)}) collective-permute-start(f32[72,256]{1,0:T(8,128)S(1)} %get-tuple-element.17), channel_id=1, source_target_pairs={{0,1},{1,0},{2,3},{3,2},{4,5},{5,4},{6,7},{7,6},{8,9},{9,8},{10,11... | collective-permute-start | bytes 221192 | tf_op jit(solution)/shard_map/ppermute | solution.py:320
  18.9 9.0 %collective-permute-start.4 = (f32[72,256]{1,0:T(8,128)S(1)}, f32[72,256]{1,0:T(8,128)S(1)}, u32[]{:S(2)}, u32[]{:S(2)}) collective-permute-start(f32[72,256]{1,0:T(8,128)S(1)} %add.21), channel_id=1, source_target_pairs={{0,8},{1,3},{2,10},{3,1},{4,12},{5,7},{6,14},{7,5},{8,0},{9,11},{1... | collective-permute-start | bytes 221192 | tf_op jit(solution)/shard_map/ppermute | solution.py:383
  25.5 4.4 %collective-permute-start.5 = (f32[72,256]{1,0:T(8,128)S(1)}, f32[72,256]{1,0:T(8,128)S(1)}, u32[]{:S(2)}, u32[]{:S(2)}) collective-permute-start(f32[72,256]{1,0:T(8,128)S(1)} %add.21), channel_id=1, source_target_pairs={{0,16},{1,5},{2,18},{3,7},{4,20},{5,1},{6,22},{7,3},{8,24},{9,13},... | collective-permute-start | bytes 221192 | tf_op jit(solution)/shard_map/ppermute | solution.py:383
  27.0 5.3 %collective-permute-start.6 = (f32[72,256]{1,0:T(8,128)S(1)}, f32[72,256]{1,0:T(8,128)S(1)}, u32[]{:S(2)}, u32[]{:S(2)}) collective-permute-start(f32[72,256]{1,0:T(8,128)S(1)} %add.21), channel_id=1, source_target_pairs={{0,24},{1,7},{2,26},{3,5},{4,28},{5,3},{6,30},{7,1},{8,16},{9,15},... | collective-permute-start | bytes 221192 | tf_op jit(solution)/shard_map/ppermute | solution.py:383
  32.3 4.5 %collective-permute-start.7 = (f32[72,256]{1,0:T(8,128)S(1)}, f32[72,256]{1,0:T(8,128)S(1)}, u32[]{:S(2)}, u32[]{:S(2)}) collective-permute-start(f32[72,256]{1,0:T(8,128)S(1)} %add_add_fusion.1), channel_id=1, source_target_pairs={{0,2},{1,9},{2,0},{3,11},{4,6},{5,13},{6,4},{7,15},{8,10},{9,1},{1... | collective-permute-start | bytes 221192 | tf_op jit(solution)/shard_map/ppermute | solution.py:383
  32.4 5.3 %collective-permute-start.8 = (f32[72,256]{1,0:T(8,128)S(1)}, f32[72,256]{1,0:T(8,128)S(1)}, u32[]{:S(2)}, u32[]{:S(2)}) collective-permute-start(f32[72,256]{1,0:T(8,128)S(1)} %add_add_fusion.1), channel_id=1, source_target_pairs={{0,4},{1,17},{2,6},{3,19},{4,0},{5,21},{6,2},{7,23},{8,12},{9,25},... | collective-permute-start | bytes 221192 | tf_op jit(solution)/shard_map/ppermute | solution.py:383
  34.4 6.2 %collective-permute-start.9 = (f32[72,256]{1,0:T(8,128)S(1)}, f32[72,256]{1,0:T(8,128)S(1)}, u32[]{:S(2)}, u32[]{:S(2)}) collective-permute-start(f32[72,256]{1,0:T(8,128)S(1)} %add_add_fusion.1), channel_id=1, source_target_pairs={{0,6},{1,25},{2,4},{3,27},{4,2},{5,29},{6,0},{7,31},{8,14},{9,17},... | collective-permute-start | bytes 221192 | tf_op jit(solution)/shard_map/ppermute | solution.py:383
  40.6 1.3 %collective-permute-start.10 = (f32[72,256]{1,0:T(8,128)S(1)}, f32[72,256]{1,0:T(8,128)S(1)}, u32[]{:S(2)}, u32[]{:S(2)}) collective-permute-start(f32[72,256]{1,0:T(8,128)S(1)} %add_add_fusion.mine_ref), channel_id=1, source_target_pairs={{0,1},{1,0},{2,3},{3,2},{4,5},{5,4},{6,7},{7,6},{8,9},{9,8},{10,11... | collective-permute-start | bytes 221192 | tf_op jit(solution)/shard_map/ppermute | solution.py:320

commit v6 on v5

--- a/solution.py
+++ b/solution.py
@@ -62,23 +62,27 @@
     out_ref, cols_ref, std_ref, rows_ref, sems = refs[-5:]
     odd = odd_device()
     first = jnp.where(odd == (0 if inner else 1), reach, 0)
-    place = pl.multiple_of(first * tile, tile)
-    copies = [
-        pltpu.make_async_copy(sketch_ref.at[pl.ds(place, reach * tile), :], rows_ref, sems.at[0]),
-        pltpu.make_async_copy(cols_hbm_ref, cols_ref, sems.at[1]),
-        pltpu.make_async_copy(std_hbm_ref, std_ref, sems.at[2]),
-    ]
-    for copy in copies:
+    cols_copy = pltpu.make_async_copy(cols_hbm_ref, cols_ref, sems.at[reach])
+    std_copy = pltpu.make_async_copy(std_hbm_ref, std_ref, sems.at[reach + 1])
+    copies = []
+    for i in range(reach):
+        place = pl.multiple_of((first + i) * tile, tile)
+        target = rows_ref.at[pl.ds(i * tile, tile), :]
+        copies.append(pltpu.make_async_copy(sketch_ref.at[pl.ds(place, tile), :], target, sems.at[i]))
+    for copy in (std_copy, cols_copy, *copies):
         copy.start()
-    copies[1].wait()
-    copies[2].wait()
-    tiles = [own_tile(cols_ref, odd, line + (reach if inner else 0), reach) for line in range(reach)]
-    columns = [std_column(std_ref, index, tile, out_ref.shape[1]) for index in tiles]
-    copies[0].wait()
-    for line in range(reach):
-        place = pl.multiple_of((tiles[line] - first) * tile, tile)
-        rows = rows_ref[pl.ds(place, tile), :].astype(F32)
-        out_ref[line * tile : (line + 1) * tile, :] = (rows * columns[line]).astype(BF16)
+    std_copy.wait()
+    columns = [std_column(std_ref, first + i, tile, out_ref.shape[1]) for i in range(reach)]
+    cols_copy.wait()
+    for i in range(reach):
+        line = jnp.int32(0)
+        for e in range(reach):
+            line = line + jnp.where(cols_ref[first + i, e] >= cols_ref[first, reach], 1, 0)
+        line = jnp.where(odd == 1, reach - 1 - line, line)
+        copies[i].wait()
+        place = pl.multiple_of(line * tile, tile)
+        rows = rows_ref[i * tile : (i + 1) * tile, :].astype(F32)
+        out_ref[pl.ds(place, tile), :] = (rows * columns[i]).astype(BF16)
 
 
 def near_kernel(
@@ -187,76 +191,90 @@
     return jnp.broadcast_to(value, (SUBLANES, LANES))
 
 
-def eliminate(work_ref, factor_ref, inverse_ref, panel=32, held=16):
+def eliminate(work_ref, factor_ref, inverse_ref, panel=32, ahead=12, step=4):
     size = work_ref.shape[0]
     groups = panel // SUBLANES
     sublane = lax.broadcasted_iota(jnp.int32, (SUBLANES, LANES), 0)
-    lane = lax.broadcasted_iota(jnp.int32, (panel, size), 1)
-    row = lax.broadcasted_iota(jnp.int32, (panel, size), 0)
-    short_lane = lax.broadcasted_iota(jnp.int32, (panel, LANES), 1)
-    short_row = lax.broadcasted_iota(jnp.int32, (panel, LANES), 0)
+    lane = lax.broadcasted_iota(jnp.int32, (SUBLANES, LANES), 1)
+    wide_lane = lax.broadcasted_iota(jnp.int32, (panel, size), 1)
     chunks = range(0, size, LANES)
     for start in range(0, size, panel):
         stop = start + panel
         chunk = start // LANES * LANES
+        at_chunk = chunk // LANES
         offset = start - chunk
         block = work_ref[start:stop, :]
-        identity = jnp.where(short_lane - offset == short_row, 1.0, 0.0).astype(F32)
         natural = [
-            [block[i : i + SUBLANES, c : c + LANES] for c in chunks] + [identity[i : i + SUBLANES]]
-            for i in range(0, panel, SUBLANES)
+            [block[i : i + SUBLANES, c : c + LANES] for c in chunks] for i in range(0, panel, SUBLANES)
         ]
-        for begin in range(0, panel, held):
-            end = begin + held
-            columns = {
-                k: {
-                    g: spread(natural[g][chunk // LANES][:, offset + k : offset + k + 1])
+        lower = [jnp.zeros((SUBLANES, LANES), F32) for _ in range(groups)]
+        scale_row = jnp.zeros((SUBLANES, LANES), F32)
+        scale_column = [jnp.zeros((SUBLANES, LANES), F32) for _ in range(groups)]
+        columns = {}
+
+        def keep(count):
+            begin, end = len(columns), len(columns) + count
+            for k in range(begin, end):
+                columns[k] = {
+                    g: spread(natural[g][at_chunk][:, offset + k : offset + k + 1])
                     for g in range(k // SUBLANES, groups)
                 }
-                for k in range(begin, end)
-            }
-            pivot = None
-            for k in range(begin, end):
-                at, inside = divmod(k, SUBLANES)
-                if pivot is None:
-                    pivot = spread(columns[k][at][inside : inside + 1, :])
-                inverse = 1.0 / pivot
-                scale = lax.rsqrt(pivot)
-                ratio = {g: columns[k][g] * inverse for g in range(at, groups)}
-                if k + 1 < end:
-                    group, place = divmod(k + 1, SUBLANES)
-                    element = spread(columns[k][group][place : place + 1, :])
-                    pivot = spread(columns[k + 1][group][place : place + 1, :]) - element * element * inverse
-                for m in range(k + 1, end):
-                    group, place = divmod(m, SUBLANES)
-                    factor = spread(ratio[group][place : place + 1, :])
-                    for g in range(group, groups):
-                        columns[m][g] = columns[m][g] - columns[k][g] * factor
-                below = dict(ratio)
-                below[at] = jnp.where(sublane > inside, ratio[at], 0.0)
-                for c in range(len(natural[0])):
-                    raw = spread(natural[at][c][inside : inside + 1, :])
-                    for g in range(at, groups):
-                        natural[g][c] = natural[g][c] - below[g] * raw
-                    natural[at][c] = jnp.where(sublane == inside, raw * scale, natural[at][c])
-        done = jnp.concatenate([jnp.concatenate(v[:-1], axis=1) for v in natural], axis=0)
-        inverse = jnp.concatenate([v[-1] for v in natural], axis=0)
-        empty = jnp.zeros((panel, LANES), F32)
-        inverse = jnp.concatenate([inverse if c == chunk else empty for c in chunks], axis=1)
-        factor_ref[start:stop, :] = jnp.where(lane >= row + start, done, 0.0)
-        inverse_ref[start:stop, :] = jnp.where(lane < start, done, inverse)
+            kept = (lane >= offset + begin) & (lane < offset + end)
+            for g in range(groups):
+                identity = jnp.where(lane - offset == sublane + g * SUBLANES, 1.0, 0.0).astype(F32)
+                natural[g][at_chunk] = jnp.where(kept, identity, natural[g][at_chunk])
+
+        keep(ahead)
+        pivot = spread(columns[0][0][:1, :])
+        for k in range(panel):
+            at, inside = divmod(k, SUBLANES)
+            inverse = 1.0 / pivot
+            scale = lax.rsqrt(pivot)
+            ratio = {g: columns[k][g] * inverse for g in range(at, groups)}
+            if k + 1 < panel:
+                group, place = divmod(k + 1, SUBLANES)
+                element = spread(columns[k][group][place : place + 1, :])
+                pivot = spread(columns[k + 1][group][place : place + 1, :]) - element * element * inverse
+            for m in range(k + 1, len(columns)):
+                group, place = divmod(m, SUBLANES)
+                factor = spread(ratio[group][place : place + 1, :])
+                for g in range(group, groups):
+                    columns[m][g] = columns[m][g] - columns[k][g] * factor
+            below = dict(ratio)
+            below[at] = jnp.where(sublane > inside, ratio[at], 0.0)
+            for c in range(len(natural[0])):
+                raw = spread(natural[at][c][inside : inside + 1, :])
+                for g in range(at, groups):
+                    natural[g][c] = natural[g][c] - below[g] * raw
+            for g in range(at, groups):
+                lower[g] = jnp.where(lane == offset + k, columns[k][g], lower[g])
+            scale_row = jnp.where(lane == offset + k, scale, scale_row)
+            scale_column[at] = jnp.where(sublane == inside, scale, scale_column[at])
+            if (k + 1) % step == 0 and len(columns) < panel:
+                keep(step)
+        done = jnp.concatenate(
+            [jnp.concatenate([v * scale_column[g] for v in natural[g]], axis=1) for g in range(groups)], axis=0
+        )
         if stop < size:
-            own = (lane >= start) & (lane < stop)
             a, b, c = split3(done)
-            x, y, z = split3(jnp.where(own, inverse, done))
+            left = jnp.concatenate([a, a, b, a, c, b], axis=0)
+            right = jnp.concatenate([a, b, a, c, a, b], axis=0)
             first = stop // LANES * LANES
-            left = jnp.concatenate([a, a, b, a, c, b], axis=0)
-            right = jnp.concatenate([x, y, x, z, x, y], axis=0)
             update = rows_dot(left[:, first:], right)
             rest = work_ref[stop:, :]
             rest_lane = lax.broadcasted_iota(jnp.int32, rest.shape, 1)
             rest = jnp.where((rest_lane >= start) & (rest_lane < stop), 0.0, rest)
             work_ref[stop:, :] = rest - update[stop - first :, :]
+        corner = jnp.concatenate([v * scale_row for v in lower], axis=0)
+        row = lax.broadcasted_iota(jnp.int32, corner.shape, 0)
+        short_lane = lax.broadcasted_iota(jnp.int32, corner.shape, 1)
+        corner = jnp.where(short_lane <= row + offset, corner, 0.0)
+        parts = [jnp.zeros((offset, LANES), F32), corner, jnp.zeros((LANES - offset - panel, LANES), F32)]
+        turned = jnp.concatenate([v for v in parts if v.shape[0]], axis=0).T[offset : offset + panel]
+        empty = jnp.zeros((panel, LANES), F32)
+        turned = jnp.concatenate([turned if c == chunk else empty for c in chunks], axis=1)
+        factor_ref[start:stop, :] = jnp.where(wide_lane >= stop, done, turned)
+        inverse_ref[start:stop, :] = jnp.where(wide_lane < stop, done, 0.0)
 
 
 def basis_kernel(
@@ -335,7 +353,7 @@
                 pltpu.SMEM(tile_cols.shape, jnp.int32),
                 pltpu.VMEM(std_rows.shape, F32),
                 pltpu.VMEM((halo, width), BF16),
-                pltpu.SemaphoreType.DMA((3,)),
+                pltpu.SemaphoreType.DMA((reach + 2,)),
             ],
             [pltpu.HBM] * 3 + [pl.ANY] * len(after),
             (tile_cols, std_rows, sketch, *after),

time: 50 us -> 49.5 us (0.990)
  Pallas kernels: 15.3 us -> 14.8 us
    pallas_call x5, Pallas kernels: 15.3 us -> 14.8 us  [call(): pl.pallas_call(kernel, out_shape=outs, in_specs=[pl.BlockSpec(memory_spac...]
where the time goes in v6:
time: 49.5 us; the launch traced here: 49.3 us
  starting transfers between devices  21.9 us (44%)
  Pallas kernels  14.8 us (30%)
  waiting for transfers between devices  11.8 us (24%)
  between operations  0.73 us (1%)
    pallas_call x5, Pallas kernels, call(): pl.pallas_call(kernel, out_shape=outs, in_specs=[pl.BlockSpec(memory_spac...  14.8 us
    ppermute x6, starting transfers between devices, per_device(): lax.ppermute(gram, AXES, [(i, i ^ (odd_mask if i % 2 else even_mask)) for...  13.4 us
    ppermute x6, waiting for transfers between devices, per_device(): lax.ppermute(gram, AXES, [(i, i ^ (odd_mask if i % 2 else even_mask)) for...  8.17 us
    ppermute x4, starting transfers between devices, swap(): lax.ppermute(value, AXES, [(i, i ^ mask) for i in range(device_count)])  7.76 us
    ppermute x4, waiting for transfers between devices, swap(): lax.ppermute(value, AXES, [(i, i ^ mask) for i in range(device_count)])  3.62 us
  transfers between devices with their start and end apart: 11, of which 8 were waited for; matrix products, arithmetic and copies ran while one was open for 0% of the time, Pallas kernels for 10%

profile of v6, /device:TPU:0, one launch (start us, length us, event | category | flops | bytes accessed | tf_op | source)
XLA Modules:
  0.0 49.3 jit_solution(6186885562603137363)
XLA Ops:
  0.6 0.0 copy-start
  0.6 0.0 copy-start.1
  0.7 1.2 %shard_map.59.refs_0_.outer_ref = bf16[1024,256]{1,0:T(8,128)(2,1)S(1)} custom-call(s32[8,9]{1,0:T(8,128)} %cols_hbm_ref.5, f32[16,128]{1,0:T(8,128)} %bitcast.1, bf16[2048,256]{1,0:T(8,128)(2,1)} %sketch_ref.3), custom_call_target="tpu_custom_call" | custom-call | flops 1 | bytes 1 | tf_op jit(solution)/shard_map/pallas_call | solution.py:319
  1.9 0.7 %collective-permute-start.2 = (bf16[1024,256]{1,0:T(8,128)(2,1)S(1)}, bf16[1024,256]{1,0:T(8,128)(2,1)S(1)}, u32[]{:S(2)}, u32[]{:S(2)}) collective-permute-start(bf16[1024,256]{1,0:T(8,128)(2,1)S(1)} %shard_map.59.refs_0_.outer_ref), channel_id=1, source_target_pairs={{1,2},{2,1},{3,4},{4,3},{5,6},{6,5},{7,8},{8,7},{9,10},{10,9},{11,... | collective-permute-start | bytes 1572872 | tf_op jit(solution)/shard_map/ppermute | solution.py:364
  2.6 1.2 %shard_map.60.inner_ref = bf16[1024,256]{1,0:T(8,128)(2,1)S(1)} custom-call(s32[8,9]{1,0:T(8,128)} %cols_hbm_ref.5, f32[16,128]{1,0:T(8,128)} %bitcast.2, bf16[2048,256]{1,0:T(8,128)(2,1)} %sketch_ref.3, bf16[1024,256]{1,0:T(8,128)(2,1)S(1)} %shard_map.59.refs_0_.outer_ref), custom_call_target="tpu_custom_call" | custom-call | flops 1 | bytes 1 | tf_op jit(solution)/shard_map/pallas_call | solution.py:319
  3.8 4.4 %collective-permute-start = (bf16[512,256]{1,0:T(8,128)(2,1)S(1)}, bf16[512,256]{1,0:T(8,128)(2,1)S(1)}, u32[]{:S(2)}, u32[]{:S(2)}) collective-permute-start(bf16[512,256]{1,0:T(8,128)(2,1)S(1)} %get-tuple-element.23), channel_id=1, source_target_pairs={{0,1},{1,0},{2,3},{3,2},{4,5},{5,4},{6,7},{7,6},{8,9},{9,8},{10,11... | collective-permute-start | bytes 786440 | tf_op jit(solution)/shard_map/ppermute | solution.py:338
  8.2 0.1 collective-permute-start.1
  8.3 1.1 %collective-permute-done.refs_0_ = bf16[512,256]{1,0:T(8,128)(2,1)S(1)} collective-permute-done((bf16[512,256]{1,0:T(8,128)(2,1)S(1)}, bf16[512,256]{1,0:T(8,128)(2,1)S(1)}, u32[]{:S(2)}, u32[]{:S(2)}) %collective-permute-start) | collective-permute-done | bytes 262176 | tf_op jit(solution)/shard_map/ppermute | solution.py:338
  9.4 0.4 collective-permute-done.1.refs_1_
  9.8 0.0 copy-done
  9.8 0.0 copy-done.1
  9.8 3.9 %shard_map.61 = (f32[1024,256]{1,0:T(8,128)S(1)}, f32[1024,128]{1,0:T(8,128)S(1)}, bf16[256,1024]{1,0:T(8,128)(2,1)S(1)}, bf16[1024,256]{1,0:T(8,128)(2,1)S(1)},...) custom-call(s32[8,9]{1,0:T(8,128)S(1)} %copy-done.1, bf16[9,256,256]{2,1,0:T(8,128)(2,1)} %cov_ref.1, ...), custom_call_target="tpu_custom_call" | custom-call | flops 1 | bytes 1 | tf_op jit(solution)/shard_map/pallas_call | solution.py:319
  13.7 0.0 collective-permute-done.2.halo_ref
  13.7 1.0 %shard_map.62 = (bf16[1024,256]{1,0:T(8,128)(2,1)S(1)}, bf16[1024,256]{1,0:T(8,128)(2,1)S(1)}, f32[72,256]{1,0:T(8,128)S(1)}, f32[72,256]{1,0:T(8,128)S(1)}) custom-call(bf16[256,1024]{1,0:T(8,128)(2,1)S(1)} %get-tuple-element.12.lag_ref, f32[1024,128]{1,0:T(8,128)S(1)} %get-tuple-element.13.scale_ref, f32[1024,256]{1,0:T(8,128)S(1)} %get-tuple-element.14.acc_ref, ...), custom_call_target="tpu_custom_call" | custom-call | flops 1 | bytes 1 | tf_op jit(solution)/shard_map/pallas_call | solution.py:319
  14.7 3.2 %collective-permute-start.3 = (f32[72,256]{1,0:T(8,128)S(1)}, f32[72,256]{1,0:T(8,128)S(1)}, u32[]{:S(2)}, u32[]{:S(2)}) collective-permute-start(f32[72,256]{1,0:T(8,128)S(1)} %get-tuple-element.17), channel_id=1, source_target_pairs={{0,1},{1,0},{2,3},{3,2},{4,5},{5,4},{6,7},{7,6},{8,9},{9,8},{10,11... | collective-permute-start | bytes 221192 | tf_op jit(solution)/shard_map/ppermute | solution.py:338
  17.9 0.9 %collective-permute-done.3 = f32[72,256]{1,0:T(8,128)S(1)} collective-permute-done((f32[72,256]{1,0:T(8,128)S(1)}, f32[72,256]{1,0:T(8,128)S(1)}, u32[]{:S(2)}, u32[]{:S(2)}) %collective-permute-start.3) | collective-permute-done | bytes 73760 | tf_op jit(solution)/shard_map/ppermute | solution.py:338
  18.8 6.6 %collective-permute-start.4 = (f32[72,256]{1,0:T(8,128)S(1)}, f32[72,256]{1,0:T(8,128)S(1)}, u32[]{:S(2)}, u32[]{:S(2)}) collective-permute-start(f32[72,256]{1,0:T(8,128)S(1)} %add.21), channel_id=1, source_target_pairs={{0,8},{1,3},{2,10},{3,1},{4,12},{5,7},{6,14},{7,5},{8,0},{9,11},{1... | collective-permute-start | bytes 221192 | tf_op jit(solution)/shard_map/ppermute | solution.py:401
  25.5 1.5 %collective-permute-start.5 = (f32[72,256]{1,0:T(8,128)S(1)}, f32[72,256]{1,0:T(8,128)S(1)}, u32[]{:S(2)}, u32[]{:S(2)}) collective-permute-start(f32[72,256]{1,0:T(8,128)S(1)} %add.21), channel_id=1, source_target_pairs={{0,16},{1,5},{2,18},{3,7},{4,20},{5,1},{6,22},{7,3},{8,24},{9,13},... | collective-permute-start | bytes 221192 | tf_op jit(solution)/shard_map/ppermute | solution.py:401
  27.0 0.9 %collective-permute-start.6 = (f32[72,256]{1,0:T(8,128)S(1)}, f32[72,256]{1,0:T(8,128)S(1)}, u32[]{:S(2)}, u32[]{:S(2)}) collective-permute-start(f32[72,256]{1,0:T(8,128)S(1)} %add.21), channel_id=1, source_target_pairs={{0,24},{1,7},{2,26},{3,5},{4,28},{5,3},{6,30},{7,1},{8,16},{9,15},... | collective-permute-start | bytes 221192 | tf_op jit(solution)/shard_map/ppermute | solution.py:401
  27.9 0.0 collective-permute-done.4
  27.9 2.0 %collective-permute-done.5 = f32[72,256]{1,0:T(8,128)S(1)} collective-permute-done((f32[72,256]{1,0:T(8,128)S(1)}, f32[72,256]{1,0:T(8,128)S(1)}, u32[]{:S(2)}, u32[]{:S(2)}) %collective-permute-start.5) | collective-permute-done | bytes 73760 | tf_op jit(solution)/shard_map/ppermute | solution.py:401
  29.8 2.4 %collective-permute-done.6 = f32[72,256]{1,0:T(8,128)S(1)} collective-permute-done((f32[72,256]{1,0:T(8,128)S(1)}, f32[72,256]{1,0:T(8,128)S(1)}, u32[]{:S(2)}, u32[]{:S(2)}) %collective-permute-start.6) | collective-permute-done | bytes 73760 | tf_op jit(solution)/shard_map/ppermute | solution.py:401
  32.3 0.1 collective-permute-start.7
  32.3 2.0 %collective-permute-start.8 = (f32[72,256]{1,0:T(8,128)S(1)}, f32[72,256]{1,0:T(8,128)S(1)}, u32[]{:S(2)}, u32[]{:S(2)}) collective-permute-start(f32[72,256]{1,0:T(8,128)S(1)} %add_add_fusion.1), channel_id=1, source_target_pairs={{0,4},{1,17},{2,6},{3,19},{4,0},{5,21},{6,2},{7,23},{8,12},{9,25},... | collective-permute-start | bytes 221192 | tf_op jit(solution)/shard_map/ppermute | solution.py:401
  34.4 2.4 %collective-permute-start.9 = (f32[72,256]{1,0:T(8,128)S(1)}, f32[72,256]{1,0:T(8,128)S(1)}, u32[]{:S(2)}, u32[]{:S(2)}) collective-permute-start(f32[72,256]{1,0:T(8,128)S(1)} %add_add_fusion.1), channel_id=1, source_target_pairs={{0,6},{1,25},{2,4},{3,27},{4,2},{5,29},{6,0},{7,31},{8,14},{9,17},... | collective-permute-start | bytes 221192 | tf_op jit(solution)/shard_map/ppermute | solution.py:401
  36.7 0.0 collective-permute-done.7
  36.7 0.9 %collective-permute-done.8 = f32[72,256]{1,0:T(8,128)S(1)} collective-permute-done((f32[72,256]{1,0:T(8,128)S(1)}, f32[72,256]{1,0:T(8,128)S(1)}, u32[]{:S(2)}, u32[]{:S(2)}) %collective-permute-start.8) | collective-permute-done | bytes 73760 | tf_op jit(solution)/shard_map/ppermute | solution.py:401
  37.7 2.9 %collective-permute-done.9 = f32[72,256]{1,0:T(8,128)S(1)} collective-permute-done((f32[72,256]{1,0:T(8,128)S(1)}, f32[72,256]{1,0:T(8,128)S(1)}, u32[]{:S(2)}, u32[]{:S(2)}) %collective-permute-start.9) | collective-permute-done | bytes 73760 | tf_op jit(solution)/shard_map/ppermute | solution.py:401
  40.5 0.1 collective-permute-start.10
  40.6 1.3 %collective-permute-done.10.other_ref = f32[72,256]{1,0:T(8,128)S(1)} collective-permute-done((f32[72,256]{1,0:T(8,128)S(1)}, f32[72,256]{1,0:T(8,128)S(1)}, u32[]{:S(2)}, u32[]{:S(2)}) %collective-permute-start.10) | collective-permute-done | bytes 73760 | tf_op jit(solution)/shard_map/ppermute | solution.py:338
  41.9 7.4 %shard_map.63 = (f32[2048,256]{1,0:T(8,128)}, f32[256,256]{1,0:T(8,128)}) custom-call(s32[8,9]{1,0:T(8,128)} %cols_hbm_ref.5, f32[72,256]{1,0:T(8,128)S(1)} %add_add_fusion.mine_ref, f32[72,256]{1,0:T(8,128)S(1)} %collective-permute-done.10.other_ref, bf16[1024,256]{1,0:T(8,128)(2,1)S(1)} %get-tuple-element.18.far_high_ref, ...), custom_call_target="tpu_custom_call" | custom-call | flops 1 | bytes 1 | tf_op jit(solution)/shard_map/pallas_call | solution.py:319
  (4 shorter events, 0.1 us)
Async XLA Ops:
  0.6 9.1 %copy-start = (f32[2048]{0:T(1024)S(1)}, f32[2048]{0:T(1024)}, u32[]{:S(2)}) copy-start(f32[2048]{0:T(1024)} %param.5) | copy-start | bytes 24580
  0.6 9.1 %copy-start.1 = (s32[8,9]{1,0:T(8,128)S(1)}, s32[8,9]{1,0:T(8,128)}, u32[]{:S(2)}) copy-start(s32[8,9]{1,0:T(8,128)} %cols_hbm_ref.5) | copy-start | bytes 868
  1.9 11.9 %collective-permute-start.2 = (bf16[1024,256]{1,0:T(8,128)(2,1)S(1)}, bf16[1024,256]{1,0:T(8,128)(2,1)S(1)}, u32[]{:S(2)}, u32[]{:S(2)}) collective-permute-start(bf16[1024,256]{1,0:T(8,128)(2,1)S(1)} %shard_map.59.refs_0_.outer_ref), channel_id=1, source_target_pairs={{1,2},{2,1},{3,4},{4,3},{5,6},{6,5},{7,8},{8,7},{9,10},{10,9},{11,... | collective-permute-start | bytes 1572872 | tf_op jit(solution)/shard_map/ppermute | solution.py:364
  3.8 5.6 %collective-permute-start = (bf16[512,256]{1,0:T(8,128)(2,1)S(1)}, bf16[512,256]{1,0:T(8,128)(2,1)S(1)}, u32[]{:S(2)}, u32[]{:S(2)}) collective-permute-start(bf16[512,256]{1,0:T(8,128)(2,1)S(1)} %get-tuple-element.23), channel_id=1, source_target_pairs={{0,1},{1,0},{2,3},{3,2},{4,5},{5,4},{6,7},{7,6},{8,9},{9,8},{10,11... | collective-permute-start | bytes 786440 | tf_op jit(solution)/shard_map/ppermute | solution.py:338
  8.2 1.5 %collective-permute-start.1 = (bf16[512,256]{1,0:T(8,128)(2,1)S(1)}, bf16[512,256]{1,0:T(8,128)(2,1)S(1)}, u32[]{:S(2)}, u32[]{:S(2)}) collective-permute-start(bf16[512,256]{1,0:T(8,128)(2,1)S(1)} %get-tuple-element.22), channel_id=1, source_target_pairs={{0,1},{1,0},{2,3},{3,2},{4,5},{5,4},{6,7},{7,6},{8,9},{9,8},{10,11... | collective-permute-start | bytes 786440 | tf_op jit(solution)/shard_map/ppermute | solution.py:338
  14.7 4.1 %collective-permute-start.3 = (f32[72,256]{1,0:T(8,128)S(1)}, f32[72,256]{1,0:T(8,128)S(1)}, u32[]{:S(2)}, u32[]{:S(2)}) collective-permute-start(f32[72,256]{1,0:T(8,128)S(1)} %get-tuple-element.17), channel_id=1, source_target_pairs={{0,1},{1,0},{2,3},{3,2},{4,5},{5,4},{6,7},{7,6},{8,9},{9,8},{10,11... | collective-permute-start | bytes 221192 | tf_op jit(solution)/shard_map/ppermute | solution.py:338
  18.8 9.0 %collective-permute-start.4 = (f32[72,256]{1,0:T(8,128)S(1)}, f32[72,256]{1,0:T(8,128)S(1)}, u32[]{:S(2)}, u32[]{:S(2)}) collective-permute-start(f32[72,256]{1,0:T(8,128)S(1)} %add.21), channel_id=1, source_target_pairs={{0,8},{1,3},{2,10},{3,1},{4,12},{5,7},{6,14},{7,5},{8,0},{9,11},{1... | collective-permute-start | bytes 221192 | tf_op jit(solution)/shard_map/ppermute | solution.py:401
  25.5 4.4 %collective-permute-start.5 = (f32[72,256]{1,0:T(8,128)S(1)}, f32[72,256]{1,0:T(8,128)S(1)}, u32[]{:S(2)}, u32[]{:S(2)}) collective-permute-start(f32[72,256]{1,0:T(8,128)S(1)} %add.21), channel_id=1, source_target_pairs={{0,16},{1,5},{2,18},{3,7},{4,20},{5,1},{6,22},{7,3},{8,24},{9,13},... | collective-permute-start | bytes 221192 | tf_op jit(solution)/shard_map/ppermute | solution.py:401
  27.0 5.3 %collective-permute-start.6 = (f32[72,256]{1,0:T(8,128)S(1)}, f32[72,256]{1,0:T(8,128)S(1)}, u32[]{:S(2)}, u32[]{:S(2)}) collective-permute-start(f32[72,256]{1,0:T(8,128)S(1)} %add.21), channel_id=1, source_target_pairs={{0,24},{1,7},{2,26},{3,5},{4,28},{5,3},{6,30},{7,1},{8,16},{9,15},... | collective-permute-start | bytes 221192 | tf_op jit(solution)/shard_map/ppermute | solution.py:401
  32.3 4.5 %collective-permute-start.7 = (f32[72,256]{1,0:T(8,128)S(1)}, f32[72,256]{1,0:T(8,128)S(1)}, u32[]{:S(2)}, u32[]{:S(2)}) collective-permute-start(f32[72,256]{1,0:T(8,128)S(1)} %add_add_fusion.1), channel_id=1, source_target_pairs={{0,2},{1,9},{2,0},{3,11},{4,6},{5,13},{6,4},{7,15},{8,10},{9,1},{1... | collective-permute-start | bytes 221192 | tf_op jit(solution)/shard_map/ppermute | solution.py:401
  32.3 5.3 %collective-permute-start.8 = (f32[72,256]{1,0:T(8,128)S(1)}, f32[72,256]{1,0:T(8,128)S(1)}, u32[]{:S(2)}, u32[]{:S(2)}) collective-permute-start(f32[72,256]{1,0:T(8,128)S(1)} %add_add_fusion.1), channel_id=1, source_target_pairs={{0,4},{1,17},{2,6},{3,19},{4,0},{5,21},{6,2},{7,23},{8,12},{9,25},... | collective-permute-start | bytes 221192 | tf_op jit(solution)/shard_map/ppermute | solution.py:401
  34.4 6.2 %collective-permute-start.9 = (f32[72,256]{1,0:T(8,128)S(1)}, f32[72,256]{1,0:T(8,128)S(1)}, u32[]{:S(2)}, u32[]{:S(2)}) collective-permute-start(f32[72,256]{1,0:T(8,128)S(1)} %add_add_fusion.1), channel_id=1, source_target_pairs={{0,6},{1,25},{2,4},{3,27},{4,2},{5,29},{6,0},{7,31},{8,14},{9,17},... | collective-permute-start | bytes 221192 | tf_op jit(solution)/shard_map/ppermute | solution.py:401
  40.5 1.3 %collective-permute-start.10 = (f32[72,256]{1,0:T(8,128)S(1)}, f32[72,256]{1,0:T(8,128)S(1)}, u32[]{:S(2)}, u32[]{:S(2)}) collective-permute-start(f32[72,256]{1,0:T(8,128)S(1)} %add_add_fusion.mine_ref), channel_id=1, source_target_pairs={{0,1},{1,0},{2,3},{3,2},{4,5},{5,4},{6,7},{7,6},{8,9},{9,8},{10,11... | collective-permute-start | bytes 221192 | tf_op jit(solution)/shard_map/ppermute | solution.py:338

commit v7 on v6

--- a/solution.py
+++ b/solution.py
@@ -396,16 +396,19 @@
         gram = gram + swap(gram, bits.pop())
     rounds = [(bits[i], bits[i + 1]) for i in range(0, len(bits), 2)]
     middle = len(rounds) // 2
+
+    def partners(pair):
+        masks = (pair[0], pair[1], pair[0] | pair[1])
+        return masks if pair is rounds[-1] else masks[::-1]
+
     for even, odd_one in zip(rounds[middle:] + rounds[:middle], rounds):
-        near, across, both = (
+        first, second, third = (
             lax.ppermute(
                 gram, AXES, [(i, i ^ (odd_mask if i % 2 else even_mask)) for i in range(device_count)]
             )
-            for even_mask, odd_mask in zip(
-                (even[0], even[1], even[0] | even[1]), (odd_one[0], odd_one[1], odd_one[0] | odd_one[1])
-            )
-        )
-        gram = (gram + near) + (across + both)
+            for even_mask, odd_mask in zip(partners(even), partners(odd_one))
+        )
+        gram = (gram + second) + (first + third)
     other = swap(gram, 1)
     basis, factor = call(
         functools.partial(basis_kernel, reach=reach, tile=tile),

time: 49.5 us -> 48.2 us (0.974)
  starting transfers between devices: 21.9 us -> 21.1 us
  waiting for transfers between devices: 11.8 us -> 11.3 us
    ppermute x6, starting transfers between devices: 13.4 us -> 12.6 us  [per_device(): lax.ppermute(gram, AXES, [(i, i ^ (odd_mask if i % 2 else even_mask)) for...]
    ppermute x6, waiting for transfers between devices: 8.17 us -> 7.64 us  [per_device(): lax.ppermute(gram, AXES, [(i, i ^ (odd_mask if i % 2 else even_mask)) for...]
  transfers between devices with their start and end apart: 11 -> 11, of which waited for: 8 -> 10; matrix products, arithmetic and copies ran while one was open for 0% -> 0% of each run, Pallas kernels for 10% -> 11%
where the time goes in v7:
time: 48.2 us; the launch traced here: 47.9 us
  starting transfers between devices  21.1 us (44%)
  Pallas kernels  14.8 us (31%)
  waiting for transfers between devices  11.3 us (23%)
  between operations  0.72 us (1%)
    pallas_call x5, Pallas kernels, call(): pl.pallas_call(kernel, out_shape=outs, in_specs=[pl.BlockSpec(memory_spac...  14.8 us
    ppermute x6, starting transfers between devices, per_device(): lax.ppermute(gram, AXES, [(i, i ^ (odd_mask if i % 2 else even_mask)) for...  12.6 us
    ppermute x4, starting transfers between devices, swap(): lax.ppermute(value, AXES, [(i, i ^ mask) for i in range(device_count)])  7.76 us
    ppermute x6, waiting for transfers between devices, per_device(): lax.ppermute(gram, AXES, [(i, i ^ (odd_mask if i % 2 else even_mask)) for...  7.64 us
    ppermute x4, waiting for transfers between devices, swap(): lax.ppermute(value, AXES, [(i, i ^ mask) for i in range(device_count)])  3.62 us
  transfers between devices with their start and end apart: 11, of which 10 were waited for; matrix products, arithmetic and copies ran while one was open for 0% of the time, Pallas kernels for 11%

profile of v7, /device:TPU:0, one launch (start us, length us, event | category | flops | bytes accessed | tf_op | source)
XLA Modules:
  0.0 47.9 jit_solution(7393885563014629168)
XLA Ops:
  0.6 0.0 copy-start
  0.6 0.0 copy-start.1
  0.7 1.2 %shard_map.59.refs_0_.outer_ref = bf16[1024,256]{1,0:T(8,128)(2,1)S(1)} custom-call(s32[8,9]{1,0:T(8,128)} %cols_hbm_ref.5, f32[16,128]{1,0:T(8,128)} %bitcast.1, bf16[2048,256]{1,0:T(8,128)(2,1)} %sketch_ref.3), custom_call_target="tpu_custom_call" | custom-call | flops 1 | bytes 1 | tf_op jit(solution)/shard_map/pallas_call | solution.py:319
  1.9 0.7 %collective-permute-start.2 = (bf16[1024,256]{1,0:T(8,128)(2,1)S(1)}, bf16[1024,256]{1,0:T(8,128)(2,1)S(1)}, u32[]{:S(2)}, u32[]{:S(2)}) collective-permute-start(bf16[1024,256]{1,0:T(8,128)(2,1)S(1)} %shard_map.59.refs_0_.outer_ref), channel_id=1, source_target_pairs={{1,2},{2,1},{3,4},{4,3},{5,6},{6,5},{7,8},{8,7},{9,10},{10,9},{11,... | collective-permute-start | bytes 1572872 | tf_op jit(solution)/shard_map/ppermute | solution.py:364
  2.6 1.2 %shard_map.60.inner_ref = bf16[1024,256]{1,0:T(8,128)(2,1)S(1)} custom-call(s32[8,9]{1,0:T(8,128)} %cols_hbm_ref.5, f32[16,128]{1,0:T(8,128)} %bitcast.2, bf16[2048,256]{1,0:T(8,128)(2,1)} %sketch_ref.3, bf16[1024,256]{1,0:T(8,128)(2,1)S(1)} %shard_map.59.refs_0_.outer_ref), custom_call_target="tpu_custom_call" | custom-call | flops 1 | bytes 1 | tf_op jit(solution)/shard_map/pallas_call | solution.py:319
  3.8 4.4 %collective-permute-start = (bf16[512,256]{1,0:T(8,128)(2,1)S(1)}, bf16[512,256]{1,0:T(8,128)(2,1)S(1)}, u32[]{:S(2)}, u32[]{:S(2)}) collective-permute-start(bf16[512,256]{1,0:T(8,128)(2,1)S(1)} %get-tuple-element.23), channel_id=1, source_target_pairs={{0,1},{1,0},{2,3},{3,2},{4,5},{5,4},{6,7},{7,6},{8,9},{9,8},{10,11... | collective-permute-start | bytes 786440 | tf_op jit(solution)/shard_map/ppermute | solution.py:338
  8.2 0.1 collective-permute-start.1
  8.3 1.1 %collective-permute-done.refs_0_ = bf16[512,256]{1,0:T(8,128)(2,1)S(1)} collective-permute-done((bf16[512,256]{1,0:T(8,128)(2,1)S(1)}, bf16[512,256]{1,0:T(8,128)(2,1)S(1)}, u32[]{:S(2)}, u32[]{:S(2)}) %collective-permute-start) | collective-permute-done | bytes 262176 | tf_op jit(solution)/shard_map/ppermute | solution.py:338
  9.4 0.4 collective-permute-done.1.refs_1_
  9.8 0.0 copy-done
  9.8 0.0 copy-done.1
  9.8 3.9 %shard_map.61 = (f32[1024,256]{1,0:T(8,128)S(1)}, f32[1024,128]{1,0:T(8,128)S(1)}, bf16[256,1024]{1,0:T(8,128)(2,1)S(1)}, bf16[1024,256]{1,0:T(8,128)(2,1)S(1)},...) custom-call(s32[8,9]{1,0:T(8,128)S(1)} %copy-done.1, bf16[9,256,256]{2,1,0:T(8,128)(2,1)} %cov_ref.1, ...), custom_call_target="tpu_custom_call" | custom-call | flops 1 | bytes 1 | tf_op jit(solution)/shard_map/pallas_call | solution.py:319
  13.7 0.0 collective-permute-done.2.halo_ref
  13.7 1.0 %shard_map.62 = (bf16[1024,256]{1,0:T(8,128)(2,1)S(1)}, bf16[1024,256]{1,0:T(8,128)(2,1)S(1)}, f32[72,256]{1,0:T(8,128)S(1)}, f32[72,256]{1,0:T(8,128)S(1)}) custom-call(bf16[256,1024]{1,0:T(8,128)(2,1)S(1)} %get-tuple-element.12.lag_ref, f32[1024,128]{1,0:T(8,128)S(1)} %get-tuple-element.13.scale_ref, f32[1024,256]{1,0:T(8,128)S(1)} %get-tuple-element.14.acc_ref, ...), custom_call_target="tpu_custom_call" | custom-call | flops 1 | bytes 1 | tf_op jit(solution)/shard_map/pallas_call | solution.py:319
  14.7 3.2 %collective-permute-start.3 = (f32[72,256]{1,0:T(8,128)S(1)}, f32[72,256]{1,0:T(8,128)S(1)}, u32[]{:S(2)}, u32[]{:S(2)}) collective-permute-start(f32[72,256]{1,0:T(8,128)S(1)} %get-tuple-element.17), channel_id=1, source_target_pairs={{0,1},{1,0},{2,3},{3,2},{4,5},{5,4},{6,7},{7,6},{8,9},{9,8},{10,11... | collective-permute-start | bytes 221192 | tf_op jit(solution)/shard_map/ppermute | solution.py:338
  17.9 0.9 %collective-permute-done.3 = f32[72,256]{1,0:T(8,128)S(1)} collective-permute-done((f32[72,256]{1,0:T(8,128)S(1)}, f32[72,256]{1,0:T(8,128)S(1)}, u32[]{:S(2)}, u32[]{:S(2)}) %collective-permute-start.3) | collective-permute-done | bytes 73760 | tf_op jit(solution)/shard_map/ppermute | solution.py:338
  18.8 7.5 %collective-permute-start.4 = (f32[72,256]{1,0:T(8,128)S(1)}, f32[72,256]{1,0:T(8,128)S(1)}, u32[]{:S(2)}, u32[]{:S(2)}) collective-permute-start(f32[72,256]{1,0:T(8,128)S(1)} %add.21), channel_id=1, source_target_pairs={{0,16},{1,5},{2,18},{3,7},{4,20},{5,1},{6,22},{7,3},{8,24},{9,13},... | collective-permute-start | bytes 221192 | tf_op jit(solution)/shard_map/ppermute | solution.py:406
  26.4 0.6 %collective-permute-start.5 = (f32[72,256]{1,0:T(8,128)S(1)}, f32[72,256]{1,0:T(8,128)S(1)}, u32[]{:S(2)}, u32[]{:S(2)}) collective-permute-start(f32[72,256]{1,0:T(8,128)S(1)} %add.21), channel_id=1, source_target_pairs={{0,8},{1,7},{2,10},{3,5},{4,12},{5,3},{6,14},{7,1},{8,0},{9,15},{1... | collective-permute-start | bytes 221192 | tf_op jit(solution)/shard_map/ppermute | solution.py:406
  27.0 0.9 %collective-permute-start.6 = (f32[72,256]{1,0:T(8,128)S(1)}, f32[72,256]{1,0:T(8,128)S(1)}, u32[]{:S(2)}, u32[]{:S(2)}) collective-permute-start(f32[72,256]{1,0:T(8,128)S(1)} %add.21), channel_id=1, source_target_pairs={{0,24},{1,3},{2,26},{3,1},{4,28},{5,7},{6,30},{7,5},{8,16},{9,11},... | collective-permute-start | bytes 221192 | tf_op jit(solution)/shard_map/ppermute | solution.py:406
  27.9 0.8 %collective-permute-done.4 = f32[72,256]{1,0:T(8,128)S(1)} collective-permute-done((f32[72,256]{1,0:T(8,128)S(1)}, f32[72,256]{1,0:T(8,128)S(1)}, u32[]{:S(2)}, u32[]{:S(2)}) %collective-permute-start.4) | collective-permute-done | bytes 73760 | tf_op jit(solution)/shard_map/ppermute | solution.py:406
  28.7 2.0 %collective-permute-done.5 = f32[72,256]{1,0:T(8,128)S(1)} collective-permute-done((f32[72,256]{1,0:T(8,128)S(1)}, f32[72,256]{1,0:T(8,128)S(1)}, u32[]{:S(2)}, u32[]{:S(2)}) %collective-permute-start.5) | collective-permute-done | bytes 73760 | tf_op jit(solution)/shard_map/ppermute | solution.py:406
  30.7 1.5 %collective-permute-done.6 = f32[72,256]{1,0:T(8,128)S(1)} collective-permute-done((f32[72,256]{1,0:T(8,128)S(1)}, f32[72,256]{1,0:T(8,128)S(1)}, u32[]{:S(2)}, u32[]{:S(2)}) %collective-permute-start.6) | collective-permute-done | bytes 73760 | tf_op jit(solution)/shard_map/ppermute | solution.py:406
  32.3 0.5 %collective-permute-start.7 = (f32[72,256]{1,0:T(8,128)S(1)}, f32[72,256]{1,0:T(8,128)S(1)}, u32[]{:S(2)}, u32[]{:S(2)}) collective-permute-start(f32[72,256]{1,0:T(8,128)S(1)} %add_add_fusion.1), channel_id=1, source_target_pairs={{0,4},{1,17},{2,6},{3,19},{4,0},{5,21},{6,2},{7,23},{8,12},{9,25},... | collective-permute-start | bytes 221192 | tf_op jit(solution)/shard_map/ppermute | solution.py:406
  32.8 1.1 %collective-permute-start.8 = (f32[72,256]{1,0:T(8,128)S(1)}, f32[72,256]{1,0:T(8,128)S(1)}, u32[]{:S(2)}, u32[]{:S(2)}) collective-permute-start(f32[72,256]{1,0:T(8,128)S(1)} %add_add_fusion.1), channel_id=1, source_target_pairs={{0,6},{1,9},{2,4},{3,11},{4,2},{5,13},{6,0},{7,15},{8,14},{9,1},{1... | collective-permute-start | bytes 221192 | tf_op jit(solution)/shard_map/ppermute | solution.py:406
  33.9 1.9 %collective-permute-start.9 = (f32[72,256]{1,0:T(8,128)S(1)}, f32[72,256]{1,0:T(8,128)S(1)}, u32[]{:S(2)}, u32[]{:S(2)}) collective-permute-start(f32[72,256]{1,0:T(8,128)S(1)} %add_add_fusion.1), channel_id=1, source_target_pairs={{0,2},{1,25},{2,0},{3,27},{4,6},{5,29},{6,4},{7,31},{8,10},{9,17},... | collective-permute-start | bytes 221192 | tf_op jit(solution)/shard_map/ppermute | solution.py:406
  35.8 1.8 %collective-permute-done.7 = f32[72,256]{1,0:T(8,128)S(1)} collective-permute-done((f32[72,256]{1,0:T(8,128)S(1)}, f32[72,256]{1,0:T(8,128)S(1)}, u32[]{:S(2)}, u32[]{:S(2)}) %collective-permute-start.7) | collective-permute-done | bytes 73760 | tf_op jit(solution)/shard_map/ppermute | solution.py:406
  37.6 1.5 %collective-permute-done.8 = f32[72,256]{1,0:T(8,128)S(1)} collective-permute-done((f32[72,256]{1,0:T(8,128)S(1)}, f32[72,256]{1,0:T(8,128)S(1)}, u32[]{:S(2)}, u32[]{:S(2)}) %collective-permute-start.8) | collective-permute-done | bytes 73760 | tf_op jit(solution)/shard_map/ppermute | solution.py:406
  39.1 0.1 collective-permute-done.9
  39.2 0.1 collective-permute-start.10
  39.3 1.3 %collective-permute-done.10.other_ref = f32[72,256]{1,0:T(8,128)S(1)} collective-permute-done((f32[72,256]{1,0:T(8,128)S(1)}, f32[72,256]{1,0:T(8,128)S(1)}, u32[]{:S(2)}, u32[]{:S(2)}) %collective-permute-start.10) | collective-permute-done | bytes 73760 | tf_op jit(solution)/shard_map/ppermute | solution.py:338
  40.5 7.4 %shard_map.63 = (f32[2048,256]{1,0:T(8,128)}, f32[256,256]{1,0:T(8,128)}) custom-call(s32[8,9]{1,0:T(8,128)} %cols_hbm_ref.5, f32[72,256]{1,0:T(8,128)S(1)} %add_add_fusion.mine_ref, f32[72,256]{1,0:T(8,128)S(1)} %collective-permute-done.10.other_ref, bf16[1024,256]{1,0:T(8,128)(2,1)S(1)} %get-tuple-element.18.far_high_ref, ...), custom_call_target="tpu_custom_call" | custom-call | flops 1 | bytes 1 | tf_op jit(solution)/shard_map/pallas_call | solution.py:319
  (4 shorter events, 0.1 us)
Async XLA Ops:
  0.6 9.1 %copy-start = (f32[2048]{0:T(1024)S(1)}, f32[2048]{0:T(1024)}, u32[]{:S(2)}) copy-start(f32[2048]{0:T(1024)} %param.5) | copy-start | bytes 24580
  0.6 9.1 %copy-start.1 = (s32[8,9]{1,0:T(8,128)S(1)}, s32[8,9]{1,0:T(8,128)}, u32[]{:S(2)}) copy-start(s32[8,9]{1,0:T(8,128)} %cols_hbm_ref.5) | copy-start | bytes 868
  1.9 11.9 %collective-permute-start.2 = (bf16[1024,256]{1,0:T(8,128)(2,1)S(1)}, bf16[1024,256]{1,0:T(8,128)(2,1)S(1)}, u32[]{:S(2)}, u32[]{:S(2)}) collective-permute-start(bf16[1024,256]{1,0:T(8,128)(2,1)S(1)} %shard_map.59.refs_0_.outer_ref), channel_id=1, source_target_pairs={{1,2},{2,1},{3,4},{4,3},{5,6},{6,5},{7,8},{8,7},{9,10},{10,9},{11,... | collective-permute-start | bytes 1572872 | tf_op jit(solution)/shard_map/ppermute | solution.py:364
  3.8 5.6 %collective-permute-start = (bf16[512,256]{1,0:T(8,128)(2,1)S(1)}, bf16[512,256]{1,0:T(8,128)(2,1)S(1)}, u32[]{:S(2)}, u32[]{:S(2)}) collective-permute-start(bf16[512,256]{1,0:T(8,128)(2,1)S(1)} %get-tuple-element.23), channel_id=1, source_target_pairs={{0,1},{1,0},{2,3},{3,2},{4,5},{5,4},{6,7},{7,6},{8,9},{9,8},{10,11... | collective-permute-start | bytes 786440 | tf_op jit(solution)/shard_map/ppermute | solution.py:338
  8.2 1.5 %collective-permute-start.1 = (bf16[512,256]{1,0:T(8,128)(2,1)S(1)}, bf16[512,256]{1,0:T(8,128)(2,1)S(1)}, u32[]{:S(2)}, u32[]{:S(2)}) collective-permute-start(bf16[512,256]{1,0:T(8,128)(2,1)S(1)} %get-tuple-element.22), channel_id=1, source_target_pairs={{0,1},{1,0},{2,3},{3,2},{4,5},{5,4},{6,7},{7,6},{8,9},{9,8},{10,11... | collective-permute-start | bytes 786440 | tf_op jit(solution)/shard_map/ppermute | solution.py:338
  14.7 4.1 %collective-permute-start.3 = (f32[72,256]{1,0:T(8,128)S(1)}, f32[72,256]{1,0:T(8,128)S(1)}, u32[]{:S(2)}, u32[]{:S(2)}) collective-permute-start(f32[72,256]{1,0:T(8,128)S(1)} %get-tuple-element.17), channel_id=1, source_target_pairs={{0,1},{1,0},{2,3},{3,2},{4,5},{5,4},{6,7},{7,6},{8,9},{9,8},{10,11... | collective-permute-start | bytes 221192 | tf_op jit(solution)/shard_map/ppermute | solution.py:338
  18.8 9.9 %collective-permute-start.4 = (f32[72,256]{1,0:T(8,128)S(1)}, f32[72,256]{1,0:T(8,128)S(1)}, u32[]{:S(2)}, u32[]{:S(2)}) collective-permute-start(f32[72,256]{1,0:T(8,128)S(1)} %add.21), channel_id=1, source_target_pairs={{0,16},{1,5},{2,18},{3,7},{4,20},{5,1},{6,22},{7,3},{8,24},{9,13},... | collective-permute-start | bytes 221192 | tf_op jit(solution)/shard_map/ppermute | solution.py:406
  26.4 4.4 %collective-permute-start.5 = (f32[72,256]{1,0:T(8,128)S(1)}, f32[72,256]{1,0:T(8,128)S(1)}, u32[]{:S(2)}, u32[]{:S(2)}) collective-permute-start(f32[72,256]{1,0:T(8,128)S(1)} %add.21), channel_id=1, source_target_pairs={{0,8},{1,7},{2,10},{3,5},{4,12},{5,3},{6,14},{7,1},{8,0},{9,15},{1... | collective-permute-start | bytes 221192 | tf_op jit(solution)/shard_map/ppermute | solution.py:406
  27.0 5.3 %collective-permute-start.6 = (f32[72,256]{1,0:T(8,128)S(1)}, f32[72,256]{1,0:T(8,128)S(1)}, u32[]{:S(2)}, u32[]{:S(2)}) collective-permute-start(f32[72,256]{1,0:T(8,128)S(1)} %add.21), channel_id=1, source_target_pairs={{0,24},{1,3},{2,26},{3,1},{4,28},{5,7},{6,30},{7,5},{8,16},{9,11},... | collective-permute-start | bytes 221192 | tf_op jit(solution)/shard_map/ppermute | solution.py:406
  32.3 5.3 %collective-permute-start.7 = (f32[72,256]{1,0:T(8,128)S(1)}, f32[72,256]{1,0:T(8,128)S(1)}, u32[]{:S(2)}, u32[]{:S(2)}) collective-permute-start(f32[72,256]{1,0:T(8,128)S(1)} %add_add_fusion.1), channel_id=1, source_target_pairs={{0,4},{1,17},{2,6},{3,19},{4,0},{5,21},{6,2},{7,23},{8,12},{9,25},... | collective-permute-start | bytes 221192 | tf_op jit(solution)/shard_map/ppermute | solution.py:406
  32.8 6.3 %collective-permute-start.8 = (f32[72,256]{1,0:T(8,128)S(1)}, f32[72,256]{1,0:T(8,128)S(1)}, u32[]{:S(2)}, u32[]{:S(2)}) collective-permute-start(f32[72,256]{1,0:T(8,128)S(1)} %add_add_fusion.1), channel_id=1, source_target_pairs={{0,6},{1,9},{2,4},{3,11},{4,2},{5,13},{6,0},{7,15},{8,14},{9,1},{1... | collective-permute-start | bytes 221192 | tf_op jit(solution)/shard_map/ppermute | solution.py:406
  33.9 5.3 %collective-permute-start.9 = (f32[72,256]{1,0:T(8,128)S(1)}, f32[72,256]{1,0:T(8,128)S(1)}, u32[]{:S(2)}, u32[]{:S(2)}) collective-permute-start(f32[72,256]{1,0:T(8,128)S(1)} %add_add_fusion.1), channel_id=1, source_target_pairs={{0,2},{1,25},{2,0},{3,27},{4,6},{5,29},{6,4},{7,31},{8,10},{9,17},... | collective-permute-start | bytes 221192 | tf_op jit(solution)/shard_map/ppermute | solution.py:406
  39.2 1.3 %collective-permute-start.10 = (f32[72,256]{1,0:T(8,128)S(1)}, f32[72,256]{1,0:T(8,128)S(1)}, u32[]{:S(2)}, u32[]{:S(2)}) collective-permute-start(f32[72,256]{1,0:T(8,128)S(1)} %add_add_fusion.mine_ref), channel_id=1, source_target_pairs={{0,1},{1,0},{2,3},{3,2},{4,5},{5,4},{6,7},{7,6},{8,9},{9,8},{10,11... | collective-permute-start | bytes 221192 | tf_op jit(solution)/shard_map/ppermute | solution.py:338

commit v8 on v7

--- a/solution.py
+++ b/solution.py
@@ -181,7 +181,7 @@
     diagonal = jnp.broadcast_to(upper[half // 2 : half // 2 + 1, :half], (half, half))
     work_ref[:half, :half] = jnp.where(column >= row, mixed, turned)
     work_ref[:half, half:] = corner
-    work_ref[half:, :half] = corner.T
+    work_ref[half:, :half] = jnp.zeros((half, half), F32)
     work_ref[half:, half:] = jnp.where(
         row == column, diagonal, jnp.where(column > row, turned, mixed)
     )
@@ -274,7 +274,8 @@
         empty = jnp.zeros((panel, LANES), F32)
         turned = jnp.concatenate([turned if c == chunk else empty for c in chunks], axis=1)
         factor_ref[start:stop, :] = jnp.where(wide_lane >= stop, done, turned)
-        inverse_ref[start:stop, :] = jnp.where(wide_lane < stop, done, 0.0)
+        high, low = split2(jnp.where(wide_lane < stop, done, 0.0))
+        inverse_ref[start:stop, :] = jnp.concatenate([high, high, low], axis=1)
 
 
 def basis_kernel(
@@ -283,17 +284,14 @@
     *, reach, tile,
 ):
     odd = odd_device()
-    cols_copy = pltpu.make_async_copy(cols_hbm_ref, cols_ref, sems.at[2 * reach + 1])
+    cols_copy = pltpu.make_async_copy(cols_hbm_ref, cols_ref, sems.at[2 * reach])
     cols_copy.start()
     mine, other = mine_ref[...], other_ref[...]
     unpack(jnp.where(odd == 1, other, mine), jnp.where(odd == 1, mine, other), work_ref)
     eliminate(work_ref, held_ref, inverse_ref)
-    factor_copy = pltpu.make_async_copy(held_ref, factor_ref, sems.at[2 * reach])
-    factor_copy.start()
+    copies = [pltpu.make_async_copy(held_ref, factor_ref, sems.at[2 * reach + 1])]
     cols_copy.wait()
-    high, low = split2(inverse_ref[...])
-    right = jnp.concatenate([high, high, low], axis=1)
-    copies = []
+    right = inverse_ref[...]
     for line in range(2 * reach):
         high_ref, low_ref = (far_high_ref, far_low_ref) if line < reach else (near_high_ref, near_low_ref)
         rows = slice(line % reach * tile, (line % reach + 1) * tile)
@@ -306,9 +304,10 @@
             pltpu.make_async_copy(tiles_ref.at[line], basis_ref.at[pl.ds(place, tile), :], sems.at[line])
         )
         copies[-1].start()
+        if line == 0:
+            copies[0].start()
     for copy in copies:
         copy.wait()
-    factor_copy.wait()
 
 
 def call(kernel, outs, scratch, spaces, operands, out_spaces=None):
@@ -415,7 +414,7 @@
         [shape(row_count, width, F32), shape(width, width, F32)],
         [
             pltpu.VMEM((width, width), F32),
-            pltpu.VMEM((width, width), F32),
+            pltpu.VMEM((width, 3 * width), BF16),
             pltpu.VMEM((2 * reach, tile, width), F32),
             pltpu.VMEM((width, width), F32),
             pltpu.SMEM(tile_cols.shape, jnp.int32),

time: 48.2 us -> 48.1 us (level)
  no operation moved by 1% of the time
where the time goes in v8:
time: 48.1 us; the launch traced here: 47.9 us
  starting transfers between devices  21.1 us (44%)
  Pallas kernels  14.7 us (31%)
  waiting for transfers between devices  11.3 us (23%)
  between operations  0.72 us (1%)
    pallas_call x5, Pallas kernels, call(): pl.pallas_call(kernel, out_shape=outs, in_specs=[pl.BlockSpec(memory_spac...  14.7 us
    ppermute x6, starting transfers between devices, per_device(): lax.ppermute(gram, AXES, [(i, i ^ (odd_mask if i % 2 else even_mask)) for...  12.6 us
    ppermute x4, starting transfers between devices, swap(): lax.ppermute(value, AXES, [(i, i ^ mask) for i in range(device_count)])  7.76 us
    ppermute x6, waiting for transfers between devices, per_device(): lax.ppermute(gram, AXES, [(i, i ^ (odd_mask if i % 2 else even_mask)) for...  7.64 us
    ppermute x4, waiting for transfers between devices, swap(): lax.ppermute(value, AXES, [(i, i ^ mask) for i in range(device_count)])  3.62 us
  transfers between devices with their start and end apart: 11, of which 10 were waited for; matrix products, arithmetic and copies ran while one was open for 0% of the time, Pallas kernels for 11%

profile of v8, /device:TPU:0, one launch (start us, length us, event | category | flops | bytes accessed | tf_op | source)
XLA Modules:
  0.0 47.9 jit_solution(16241849166443030593)
XLA Ops:
  0.6 0.0 copy-start
  0.6 0.0 copy-start.1
  0.7 1.2 %shard_map.59.refs_0_.outer_ref = bf16[1024,256]{1,0:T(8,128)(2,1)S(1)} custom-call(s32[8,9]{1,0:T(8,128)} %cols_hbm_ref.5, f32[16,128]{1,0:T(8,128)} %bitcast.1, bf16[2048,256]{1,0:T(8,128)(2,1)} %sketch_ref.3), custom_call_target="tpu_custom_call" | custom-call | flops 1 | bytes 1 | tf_op jit(solution)/shard_map/pallas_call | solution.py:318
  1.9 0.7 %collective-permute-start.2 = (bf16[1024,256]{1,0:T(8,128)(2,1)S(1)}, bf16[1024,256]{1,0:T(8,128)(2,1)S(1)}, u32[]{:S(2)}, u32[]{:S(2)}) collective-permute-start(bf16[1024,256]{1,0:T(8,128)(2,1)S(1)} %shard_map.59.refs_0_.outer_ref), channel_id=1, source_target_pairs={{1,2},{2,1},{3,4},{4,3},{5,6},{6,5},{7,8},{8,7},{9,10},{10,9},{11,... | collective-permute-start | bytes 1572872 | tf_op jit(solution)/shard_map/ppermute | solution.py:363
  2.6 1.2 %shard_map.60.inner_ref = bf16[1024,256]{1,0:T(8,128)(2,1)S(1)} custom-call(s32[8,9]{1,0:T(8,128)} %cols_hbm_ref.5, f32[16,128]{1,0:T(8,128)} %bitcast.2, bf16[2048,256]{1,0:T(8,128)(2,1)} %sketch_ref.3, bf16[1024,256]{1,0:T(8,128)(2,1)S(1)} %shard_map.59.refs_0_.outer_ref), custom_call_target="tpu_custom_call" | custom-call | flops 1 | bytes 1 | tf_op jit(solution)/shard_map/pallas_call | solution.py:318
  3.8 4.4 %collective-permute-start = (bf16[512,256]{1,0:T(8,128)(2,1)S(1)}, bf16[512,256]{1,0:T(8,128)(2,1)S(1)}, u32[]{:S(2)}, u32[]{:S(2)}) collective-permute-start(bf16[512,256]{1,0:T(8,128)(2,1)S(1)} %get-tuple-element.23), channel_id=1, source_target_pairs={{0,1},{1,0},{2,3},{3,2},{4,5},{5,4},{6,7},{7,6},{8,9},{9,8},{10,11... | collective-permute-start | bytes 786440 | tf_op jit(solution)/shard_map/ppermute | solution.py:337
  8.2 0.1 collective-permute-start.1
  8.3 1.1 %collective-permute-done.refs_0_ = bf16[512,256]{1,0:T(8,128)(2,1)S(1)} collective-permute-done((bf16[512,256]{1,0:T(8,128)(2,1)S(1)}, bf16[512,256]{1,0:T(8,128)(2,1)S(1)}, u32[]{:S(2)}, u32[]{:S(2)}) %collective-permute-start) | collective-permute-done | bytes 262176 | tf_op jit(solution)/shard_map/ppermute | solution.py:337
  9.4 0.4 collective-permute-done.1.refs_1_
  9.8 0.0 copy-done
  9.8 0.0 copy-done.1
  9.8 3.9 %shard_map.61 = (f32[1024,256]{1,0:T(8,128)S(1)}, f32[1024,128]{1,0:T(8,128)S(1)}, bf16[256,1024]{1,0:T(8,128)(2,1)S(1)}, bf16[1024,256]{1,0:T(8,128)(2,1)S(1)},...) custom-call(s32[8,9]{1,0:T(8,128)S(1)} %copy-done.1, bf16[9,256,256]{2,1,0:T(8,128)(2,1)} %cov_ref.1, ...), custom_call_target="tpu_custom_call" | custom-call | flops 1 | bytes 1 | tf_op jit(solution)/shard_map/pallas_call | solution.py:318
  13.7 0.0 collective-permute-done.2.halo_ref
  13.7 1.0 %shard_map.62 = (bf16[1024,256]{1,0:T(8,128)(2,1)S(1)}, bf16[1024,256]{1,0:T(8,128)(2,1)S(1)}, f32[72,256]{1,0:T(8,128)S(1)}, f32[72,256]{1,0:T(8,128)S(1)}) custom-call(bf16[256,1024]{1,0:T(8,128)(2,1)S(1)} %get-tuple-element.12.lag_ref, f32[1024,128]{1,0:T(8,128)S(1)} %get-tuple-element.13.scale_ref, f32[1024,256]{1,0:T(8,128)S(1)} %get-tuple-element.14.acc_ref, ...), custom_call_target="tpu_custom_call" | custom-call | flops 1 | bytes 1 | tf_op jit(solution)/shard_map/pallas_call | solution.py:318
  14.7 3.2 %collective-permute-start.3 = (f32[72,256]{1,0:T(8,128)S(1)}, f32[72,256]{1,0:T(8,128)S(1)}, u32[]{:S(2)}, u32[]{:S(2)}) collective-permute-start(f32[72,256]{1,0:T(8,128)S(1)} %get-tuple-element.17), channel_id=1, source_target_pairs={{0,1},{1,0},{2,3},{3,2},{4,5},{5,4},{6,7},{7,6},{8,9},{9,8},{10,11... | collective-permute-start | bytes 221192 | tf_op jit(solution)/shard_map/ppermute | solution.py:337
  17.9 0.9 %collective-permute-done.3 = f32[72,256]{1,0:T(8,128)S(1)} collective-permute-done((f32[72,256]{1,0:T(8,128)S(1)}, f32[72,256]{1,0:T(8,128)S(1)}, u32[]{:S(2)}, u32[]{:S(2)}) %collective-permute-start.3) | collective-permute-done | bytes 73760 | tf_op jit(solution)/shard_map/ppermute | solution.py:337
  18.8 7.5 %collective-permute-start.4 = (f32[72,256]{1,0:T(8,128)S(1)}, f32[72,256]{1,0:T(8,128)S(1)}, u32[]{:S(2)}, u32[]{:S(2)}) collective-permute-start(f32[72,256]{1,0:T(8,128)S(1)} %add.21), channel_id=1, source_target_pairs={{0,16},{1,5},{2,18},{3,7},{4,20},{5,1},{6,22},{7,3},{8,24},{9,13},... | collective-permute-start | bytes 221192 | tf_op jit(solution)/shard_map/ppermute | solution.py:405
  26.4 0.6 %collective-permute-start.5 = (f32[72,256]{1,0:T(8,128)S(1)}, f32[72,256]{1,0:T(8,128)S(1)}, u32[]{:S(2)}, u32[]{:S(2)}) collective-permute-start(f32[72,256]{1,0:T(8,128)S(1)} %add.21), channel_id=1, source_target_pairs={{0,8},{1,7},{2,10},{3,5},{4,12},{5,3},{6,14},{7,1},{8,0},{9,15},{1... | collective-permute-start | bytes 221192 | tf_op jit(solution)/shard_map/ppermute | solution.py:405
  27.0 0.9 %collective-permute-start.6 = (f32[72,256]{1,0:T(8,128)S(1)}, f32[72,256]{1,0:T(8,128)S(1)}, u32[]{:S(2)}, u32[]{:S(2)}) collective-permute-start(f32[72,256]{1,0:T(8,128)S(1)} %add.21), channel_id=1, source_target_pairs={{0,24},{1,3},{2,26},{3,1},{4,28},{5,7},{6,30},{7,5},{8,16},{9,11},... | collective-permute-start | bytes 221192 | tf_op jit(solution)/shard_map/ppermute | solution.py:405
  27.9 0.8 %collective-permute-done.4 = f32[72,256]{1,0:T(8,128)S(1)} collective-permute-done((f32[72,256]{1,0:T(8,128)S(1)}, f32[72,256]{1,0:T(8,128)S(1)}, u32[]{:S(2)}, u32[]{:S(2)}) %collective-permute-start.4) | collective-permute-done | bytes 73760 | tf_op jit(solution)/shard_map/ppermute | solution.py:405
  28.7 2.0 %collective-permute-done.5 = f32[72,256]{1,0:T(8,128)S(1)} collective-permute-done((f32[72,256]{1,0:T(8,128)S(1)}, f32[72,256]{1,0:T(8,128)S(1)}, u32[]{:S(2)}, u32[]{:S(2)}) %collective-permute-start.5) | collective-permute-done | bytes 73760 | tf_op jit(solution)/shard_map/ppermute | solution.py:405
  30.7 1.5 %collective-permute-done.6 = f32[72,256]{1,0:T(8,128)S(1)} collective-permute-done((f32[72,256]{1,0:T(8,128)S(1)}, f32[72,256]{1,0:T(8,128)S(1)}, u32[]{:S(2)}, u32[]{:S(2)}) %collective-permute-start.6) | collective-permute-done | bytes 73760 | tf_op jit(solution)/shard_map/ppermute | solution.py:405
  32.3 0.5 %collective-permute-start.7 = (f32[72,256]{1,0:T(8,128)S(1)}, f32[72,256]{1,0:T(8,128)S(1)}, u32[]{:S(2)}, u32[]{:S(2)}) collective-permute-start(f32[72,256]{1,0:T(8,128)S(1)} %add_add_fusion.1), channel_id=1, source_target_pairs={{0,4},{1,17},{2,6},{3,19},{4,0},{5,21},{6,2},{7,23},{8,12},{9,25},... | collective-permute-start | bytes 221192 | tf_op jit(solution)/shard_map/ppermute | solution.py:405
  32.8 1.1 %collective-permute-start.8 = (f32[72,256]{1,0:T(8,128)S(1)}, f32[72,256]{1,0:T(8,128)S(1)}, u32[]{:S(2)}, u32[]{:S(2)}) collective-permute-start(f32[72,256]{1,0:T(8,128)S(1)} %add_add_fusion.1), channel_id=1, source_target_pairs={{0,6},{1,9},{2,4},{3,11},{4,2},{5,13},{6,0},{7,15},{8,14},{9,1},{1... | collective-permute-start | bytes 221192 | tf_op jit(solution)/shard_map/ppermute | solution.py:405
  33.9 1.9 %collective-permute-start.9 = (f32[72,256]{1,0:T(8,128)S(1)}, f32[72,256]{1,0:T(8,128)S(1)}, u32[]{:S(2)}, u32[]{:S(2)}) collective-permute-start(f32[72,256]{1,0:T(8,128)S(1)} %add_add_fusion.1), channel_id=1, source_target_pairs={{0,2},{1,25},{2,0},{3,27},{4,6},{5,29},{6,4},{7,31},{8,10},{9,17},... | collective-permute-start | bytes 221192 | tf_op jit(solution)/shard_map/ppermute | solution.py:405
  35.8 1.8 %collective-permute-done.7 = f32[72,256]{1,0:T(8,128)S(1)} collective-permute-done((f32[72,256]{1,0:T(8,128)S(1)}, f32[72,256]{1,0:T(8,128)S(1)}, u32[]{:S(2)}, u32[]{:S(2)}) %collective-permute-start.7) | collective-permute-done | bytes 73760 | tf_op jit(solution)/shard_map/ppermute | solution.py:405
  37.6 1.5 %collective-permute-done.8 = f32[72,256]{1,0:T(8,128)S(1)} collective-permute-done((f32[72,256]{1,0:T(8,128)S(1)}, f32[72,256]{1,0:T(8,128)S(1)}, u32[]{:S(2)}, u32[]{:S(2)}) %collective-permute-start.8) | collective-permute-done | bytes 73760 | tf_op jit(solution)/shard_map/ppermute | solution.py:405
  39.1 0.1 collective-permute-done.9
  39.2 0.1 collective-permute-start.10
  39.3 1.3 %collective-permute-done.10.other_ref = f32[72,256]{1,0:T(8,128)S(1)} collective-permute-done((f32[72,256]{1,0:T(8,128)S(1)}, f32[72,256]{1,0:T(8,128)S(1)}, u32[]{:S(2)}, u32[]{:S(2)}) %collective-permute-start.10) | collective-permute-done | bytes 73760 | tf_op jit(solution)/shard_map/ppermute | solution.py:337
  40.5 7.4 %shard_map.63 = (f32[2048,256]{1,0:T(8,128)}, f32[256,256]{1,0:T(8,128)}) custom-call(s32[8,9]{1,0:T(8,128)} %cols_hbm_ref.5, f32[72,256]{1,0:T(8,128)S(1)} %add_add_fusion.mine_ref, f32[72,256]{1,0:T(8,128)S(1)} %collective-permute-done.10.other_ref, bf16[1024,256]{1,0:T(8,128)(2,1)S(1)} %get-tuple-element.18.far_high_ref, ...), custom_call_target="tpu_custom_call" | custom-call | flops 1 | bytes 1 | tf_op jit(solution)/shard_map/pallas_call | solution.py:318
  (4 shorter events, 0.1 us)
Async XLA Ops:
  0.6 9.1 %copy-start = (f32[2048]{0:T(1024)S(1)}, f32[2048]{0:T(1024)}, u32[]{:S(2)}) copy-start(f32[2048]{0:T(1024)} %param.5) | copy-start | bytes 24580
  0.6 9.1 %copy-start.1 = (s32[8,9]{1,0:T(8,128)S(1)}, s32[8,9]{1,0:T(8,128)}, u32[]{:S(2)}) copy-start(s32[8,9]{1,0:T(8,128)} %cols_hbm_ref.5) | copy-start | bytes 868
  1.9 11.9 %collective-permute-start.2 = (bf16[1024,256]{1,0:T(8,128)(2,1)S(1)}, bf16[1024,256]{1,0:T(8,128)(2,1)S(1)}, u32[]{:S(2)}, u32[]{:S(2)}) collective-permute-start(bf16[1024,256]{1,0:T(8,128)(2,1)S(1)} %shard_map.59.refs_0_.outer_ref), channel_id=1, source_target_pairs={{1,2},{2,1},{3,4},{4,3},{5,6},{6,5},{7,8},{8,7},{9,10},{10,9},{11,... | collective-permute-start | bytes 1572872 | tf_op jit(solution)/shard_map/ppermute | solution.py:363
  3.8 5.6 %collective-permute-start = (bf16[512,256]{1,0:T(8,128)(2,1)S(1)}, bf16[512,256]{1,0:T(8,128)(2,1)S(1)}, u32[]{:S(2)}, u32[]{:S(2)}) collective-permute-start(bf16[512,256]{1,0:T(8,128)(2,1)S(1)} %get-tuple-element.23), channel_id=1, source_target_pairs={{0,1},{1,0},{2,3},{3,2},{4,5},{5,4},{6,7},{7,6},{8,9},{9,8},{10,11... | collective-permute-start | bytes 786440 | tf_op jit(solution)/shard_map/ppermute | solution.py:337
  8.2 1.5 %collective-permute-start.1 = (bf16[512,256]{1,0:T(8,128)(2,1)S(1)}, bf16[512,256]{1,0:T(8,128)(2,1)S(1)}, u32[]{:S(2)}, u32[]{:S(2)}) collective-permute-start(bf16[512,256]{1,0:T(8,128)(2,1)S(1)} %get-tuple-element.22), channel_id=1, source_target_pairs={{0,1},{1,0},{2,3},{3,2},{4,5},{5,4},{6,7},{7,6},{8,9},{9,8},{10,11... | collective-permute-start | bytes 786440 | tf_op jit(solution)/shard_map/ppermute | solution.py:337
  14.7 4.1 %collective-permute-start.3 = (f32[72,256]{1,0:T(8,128)S(1)}, f32[72,256]{1,0:T(8,128)S(1)}, u32[]{:S(2)}, u32[]{:S(2)}) collective-permute-start(f32[72,256]{1,0:T(8,128)S(1)} %get-tuple-element.17), channel_id=1, source_target_pairs={{0,1},{1,0},{2,3},{3,2},{4,5},{5,4},{6,7},{7,6},{8,9},{9,8},{10,11... | collective-permute-start | bytes 221192 | tf_op jit(solution)/shard_map/ppermute | solution.py:337
  18.8 9.9 %collective-permute-start.4 = (f32[72,256]{1,0:T(8,128)S(1)}, f32[72,256]{1,0:T(8,128)S(1)}, u32[]{:S(2)}, u32[]{:S(2)}) collective-permute-start(f32[72,256]{1,0:T(8,128)S(1)} %add.21), channel_id=1, source_target_pairs={{0,16},{1,5},{2,18},{3,7},{4,20},{5,1},{6,22},{7,3},{8,24},{9,13},... | collective-permute-start | bytes 221192 | tf_op jit(solution)/shard_map/ppermute | solution.py:405
  26.4 4.4 %collective-permute-start.5 = (f32[72,256]{1,0:T(8,128)S(1)}, f32[72,256]{1,0:T(8,128)S(1)}, u32[]{:S(2)}, u32[]{:S(2)}) collective-permute-start(f32[72,256]{1,0:T(8,128)S(1)} %add.21), channel_id=1, source_target_pairs={{0,8},{1,7},{2,10},{3,5},{4,12},{5,3},{6,14},{7,1},{8,0},{9,15},{1... | collective-permute-start | bytes 221192 | tf_op jit(solution)/shard_map/ppermute | solution.py:405
  27.0 5.3 %collective-permute-start.6 = (f32[72,256]{1,0:T(8,128)S(1)}, f32[72,256]{1,0:T(8,128)S(1)}, u32[]{:S(2)}, u32[]{:S(2)}) collective-permute-start(f32[72,256]{1,0:T(8,128)S(1)} %add.21), channel_id=1, source_target_pairs={{0,24},{1,3},{2,26},{3,1},{4,28},{5,7},{6,30},{7,5},{8,16},{9,11},... | collective-permute-start | bytes 221192 | tf_op jit(solution)/shard_map/ppermute | solution.py:405
  32.3 5.3 %collective-permute-start.7 = (f32[72,256]{1,0:T(8,128)S(1)}, f32[72,256]{1,0:T(8,128)S(1)}, u32[]{:S(2)}, u32[]{:S(2)}) collective-permute-start(f32[72,256]{1,0:T(8,128)S(1)} %add_add_fusion.1), channel_id=1, source_target_pairs={{0,4},{1,17},{2,6},{3,19},{4,0},{5,21},{6,2},{7,23},{8,12},{9,25},... | collective-permute-start | bytes 221192 | tf_op jit(solution)/shard_map/ppermute | solution.py:405
  32.8 6.3 %collective-permute-start.8 = (f32[72,256]{1,0:T(8,128)S(1)}, f32[72,256]{1,0:T(8,128)S(1)}, u32[]{:S(2)}, u32[]{:S(2)}) collective-permute-start(f32[72,256]{1,0:T(8,128)S(1)} %add_add_fusion.1), channel_id=1, source_target_pairs={{0,6},{1,9},{2,4},{3,11},{4,2},{5,13},{6,0},{7,15},{8,14},{9,1},{1... | collective-permute-start | bytes 221192 | tf_op jit(solution)/shard_map/ppermute | solution.py:405
  33.9 5.3 %collective-permute-start.9 = (f32[72,256]{1,0:T(8,128)S(1)}, f32[72,256]{1,0:T(8,128)S(1)}, u32[]{:S(2)}, u32[]{:S(2)}) collective-permute-start(f32[72,256]{1,0:T(8,128)S(1)} %add_add_fusion.1), channel_id=1, source_target_pairs={{0,2},{1,25},{2,0},{3,27},{4,6},{5,29},{6,4},{7,31},{8,10},{9,17},... | collective-permute-start | bytes 221192 | tf_op jit(solution)/shard_map/ppermute | solution.py:405
  39.2 1.3 %collective-permute-start.10 = (f32[72,256]{1,0:T(8,128)S(1)}, f32[72,256]{1,0:T(8,128)S(1)}, u32[]{:S(2)}, u32[]{:S(2)}) collective-permute-start(f32[72,256]{1,0:T(8,128)S(1)} %add_add_fusion.mine_ref), channel_id=1, source_target_pairs={{0,1},{1,0},{2,3},{3,2},{4,5},{5,4},{6,7},{7,6},{8,9},{9,8},{10,11... | collective-permute-start | bytes 221192 | tf_op jit(solution)/shard_map/ppermute | solution.py:337
